TPU v7x, 512 devices: a whole 4x4x16 slice. The times are simulated.
512 devices in a mesh: dp: 2 (over y_lo), ctx: 16 (over z), head: 16 (over y_hi, x, core).
Axes of the slice: x: 4, y: 4 (y_hi: 2, y_lo: 2; y = y_hi * 2 + y_lo), z: 16, core: 2. Of those that a mesh axis runs over, the one named last changes fastest.
Arguments:
- latent: bfloat16 [2, 2048, 576], P('dp', 'ctx'), may hold values from -8 to 8
- q_nope: bfloat16 [2, 2048, 8192], P('dp', 'ctx', 'head'), may hold values from -6 to 6
- q_rope: bfloat16 [2, 2048, 4096], P('dp', 'ctx', 'head'), may hold values from -8 to 8
- grad_out: bfloat16 [2, 2048, 8192], P('dp', 'ctx', 'head'), may hold values from -6 to 6
- w_uk: bfloat16 [512, 8192], P(None, 'head'), may hold values from -0.25 to 0.25
- w_uv: bfloat16 [512, 8192], P(None, 'head'), may hold values from -0.25 to 0.25
- stretch_order: int32 [32], replicated, may hold values from 0 to 31, as said below
Outputs:
- d_latent: float32 [2, 2048, 576], P('dp', ('ctx', 'head'))
- d_q_nope: bfloat16 [2, 2048, 8192], P('dp', 'ctx', 'head')
- d_q_rope: bfloat16 [2, 2048, 4096], P('dp', 'ctx', 'head')
- d_w_uk: float32 [512, 8192], P(None, 'head')
- d_w_uv: float32 [512, 8192], P(None, 'head')
Inputs may be any that keep to these rules, and one draw needn't show every extreme that they name: `stretch_order`: entries 2d and 2d+1 name the causal blocks of the two row blocks of the d-th block of 128 rows; all entries together are a permutation, and each such pair sums to 31.
All inputs are finite; a program needn't handle non-finite values.
Results may differ from a plain program's by a relative error of at most 0.02.
Values may be sent and summed in bfloat16 or wider, within the bound.
No kernel may reach another device: no remote copies, remote signals or barrier semaphores. Data moves between devices by JAX's collectives and lax.ppermute only.
A program may use at most 64 MiB of HBM per device.

v0:
```python
import math

import jax
import jax.numpy as jnp
from jax import lax
from jax.sharding import PartitionSpec as P

D_LAT = 512
D_ROPE = 64
D_NOPE = 128
D_V = 128
TOK_DEV = 128
STRETCH = 64


NEG_FILL = -1e30


def table_lookup(table, slot_index):
    entries = table.shape[0]
    match = slot_index[:, None] == jnp.arange(entries, dtype=jnp.int32)[None, :]
    return jnp.sum(jnp.where(match, table[None, :], 0), axis=1)


def row_positions(stretch_order, first_row, row_count):
    row_index = first_row + jnp.arange(row_count, dtype=jnp.int32)
    slot_index = 2 * (row_index // TOK_DEV) + row_index % TOK_DEV // STRETCH
    return table_lookup(stretch_order, slot_index) * STRETCH + row_index % STRETCH


def keep_same(current):
    return current


def local(latent, q_nope, q_rope, grad_out, w_uk, w_uv, stretch_order):
    head_count = w_uk.shape[1] // D_NOPE
    n_head = lax.axis_size("head")
    n_ctx = lax.axis_size("ctx")
    ctx_index = lax.axis_index("ctx")
    score_scale = 1.0 / math.sqrt(D_NOPE + D_ROPE)
    key_width = D_LAT + D_ROPE
    w_key = w_uk.reshape(D_LAT, head_count, D_NOPE)
    w_value = w_uv.reshape(D_LAT, head_count, D_V)
    query_heads = q_nope[0].reshape(TOK_DEV, head_count, D_NOPE)
    rope_heads = q_rope[0].reshape(TOK_DEV, head_count, D_ROPE)
    grad_heads = grad_out[0].reshape(TOK_DEV, head_count, D_V)
    query_latent = jnp.einsum(
        "thd,fhd->htf", query_heads, w_key, preferred_element_type=jnp.float32
    ).astype(jnp.bfloat16)
    query_cat = jnp.concatenate([query_latent, rope_heads.transpose(1, 0, 2)], axis=2)
    grad_latent = jnp.einsum(
        "thd,fhd->htf", grad_heads, w_value, preferred_element_type=jnp.float32
    ).astype(jnp.bfloat16)

    def halves(values):
        return (
            values.reshape(head_count, 2, STRETCH, values.shape[-1])
            .transpose(1, 0, 2, 3)
            .reshape(2, head_count * STRETCH, values.shape[-1])
        )

    def unhalve(values):
        return (
            values.reshape(2, head_count, STRETCH, values.shape[-1])
            .transpose(1, 0, 2, 3)
            .reshape(head_count, TOK_DEV, values.shape[-1])
        )

    query_rows = halves(query_cat)
    grad_rows = halves(grad_latent)
    local_pos = row_positions(stretch_order, ctx_index * TOK_DEV, TOK_DEV)
    row_pos = jnp.tile(local_pos.reshape(2, 1, STRETCH), (1, head_count, 1)).reshape(
        2, head_count * STRETCH
    )
    row_top = jnp.max(row_pos, axis=1)
    row_count = head_count * STRETCH

    def scores_of(block_index, key_rows, key_pos):
        raw_score = (
            jnp.einsum(
                "rf,kf->rk", query_rows[block_index], key_rows, preferred_element_type=jnp.float32
            )
            * score_scale
        )
        allowed = key_pos[None, :] <= row_pos[block_index][:, None]
        prob_grad = jnp.einsum(
            "rf,kf->rk",
            grad_rows[block_index],
            key_rows[:, :D_LAT],
            preferred_element_type=jnp.float32,
        )
        return (jnp.where(allowed, raw_score, -jnp.inf), prob_grad)

    stats_init = (
        jnp.full((2, row_count), NEG_FILL, jnp.float32),
        jnp.zeros((2, row_count), jnp.float32),
        jnp.zeros((2, row_count), jnp.float32),
    )
    running = stats_init
    key_rows = lax.all_gather(latent, "ctx", axis=1, tiled=True)[0]
    key_pos = row_positions(stretch_order, jnp.int32(0), key_rows.shape[0])
    for block_index in range(2):

        def stats_update(current, block_index=block_index):
            row_max, row_total, weighted = current
            raw_score, prob_grad = scores_of(block_index, key_rows, key_pos)
            old_max = row_max[block_index]
            new_max = jnp.maximum(old_max, jnp.max(raw_score, axis=1))
            shrink = jnp.exp(old_max - new_max)
            expo = jnp.exp(raw_score - new_max[:, None])
            new_total = row_total[block_index] * shrink + jnp.sum(expo, axis=1)
            new_weighted = weighted[block_index] * shrink + jnp.sum(expo * prob_grad, axis=1)
            return (
                row_max.at[block_index].set(new_max),
                row_total.at[block_index].set(new_total),
                weighted.at[block_index].set(new_weighted),
            )

        needed = jnp.min(key_pos) <= row_top[block_index]
        running = lax.cond(needed, stats_update, keep_same, running)
    row_max, row_total, weighted = running
    log_total = row_max + jnp.log(row_total)
    row_delta = weighted / row_total
    grad_init = (
        jnp.zeros((2, row_count, key_width), jnp.float32),
        jnp.zeros((2, row_count, D_LAT), jnp.float32),
        jnp.zeros((TOK_DEV * n_ctx, key_width), jnp.float32),
    )
    running = grad_init
    grad_key_rows = lax.all_gather(latent, "ctx", axis=1, tiled=True)[0]
    key_count = grad_key_rows.shape[0]
    grad_key_pos = row_positions(stretch_order, jnp.int32(0), key_count)
    for block_index in range(2):

        def grad_update(current, block_index=block_index):
            query_sum, output_sum, latent_sum = current
            raw_score, prob_grad = scores_of(block_index, grad_key_rows, grad_key_pos)
            probability = jnp.exp(raw_score - log_total[block_index][:, None])
            score_grad = (
                score_scale * probability * (prob_grad - row_delta[block_index][:, None])
            ).astype(jnp.bfloat16)
            prob_low = probability.astype(jnp.bfloat16)
            query_sum = query_sum.at[block_index].add(
                jnp.dot(score_grad, grad_key_rows, preferred_element_type=jnp.float32)
            )
            output_sum = output_sum.at[block_index].add(
                jnp.dot(prob_low, grad_key_rows[:, :D_LAT], preferred_element_type=jnp.float32)
            )
            key_term = jnp.einsum(
                "rk,rf->kf", score_grad, query_rows[block_index], preferred_element_type=jnp.float32
            )
            value_term = jnp.einsum(
                "rk,rf->kf", prob_low, grad_rows[block_index], preferred_element_type=jnp.float32
            )
            key_term = key_term.at[:, :D_LAT].add(value_term)
            previous = latent_sum
            latent_sum = previous + key_term
            return (query_sum, output_sum, latent_sum)

        needed = jnp.min(grad_key_pos) <= row_top[block_index]
        running = lax.cond(needed, grad_update, keep_same, running)
    query_sum, output_sum, latent_sum = running
    query_low = unhalve(query_sum.astype(jnp.bfloat16))
    latent_query = query_low[:, :, :D_LAT]
    rope_grad = query_low[:, :, D_LAT:].transpose(1, 0, 2).reshape(1, TOK_DEV, head_count * D_ROPE)
    nope_grad = jnp.einsum("htf,fhd->thd", latent_query, w_key, preferred_element_type=jnp.float32)
    nope_grad = nope_grad.astype(jnp.bfloat16).reshape(1, TOK_DEV, head_count * D_NOPE)
    output_low = unhalve(output_sum.astype(jnp.bfloat16))
    key_weight = jnp.einsum(
        "htf,thd->fhd", latent_query, query_heads, preferred_element_type=jnp.float32
    ).reshape(D_LAT, head_count * D_NOPE)
    value_weight = jnp.einsum(
        "htf,thd->fhd", output_low, grad_heads, preferred_element_type=jnp.float32
    ).reshape(D_LAT, head_count * D_V)
    key_weight, value_weight = lax.psum((key_weight, value_weight), ("dp", "ctx"))
    rows_out = TOK_DEV // n_head
    owner_rows = lax.psum_scatter(
        latent_sum.astype(jnp.bfloat16), "ctx", scatter_dimension=0, tiled=True
    ).astype(jnp.float32)
    owned_rows = lax.psum_scatter(owner_rows, "head", scatter_dimension=0, tiled=True)
    return (
        owned_rows.reshape(1, rows_out, key_width),
        nope_grad,
        rope_grad,
        key_weight,
        value_weight,
    )


def solution(mesh):
    placed = (
        P("dp", "ctx", None),
        P("dp", "ctx", "head"),
        P("dp", "ctx", "head"),
        P("dp", "ctx", "head"),
        P(None, "head"),
        P(None, "head"),
        P(),
    )
    return jax.shard_map(
        local,
        mesh=mesh,
        in_specs=placed,
        out_specs=(
            P("dp", ("ctx", "head"), None),
            P("dp", "ctx", "head"),
            P("dp", "ctx", "head"),
            P(None, "head"),
            P(None, "head"),
        ),
        check_vma=False,
    )
```

profile of v0, /device:TPU:2, one launch (start us, length us, event | category | flops | bytes accessed | tf_op | source)
XLA Modules:
  0.0 638.1 jit_solution(8334506287447708330)
XLA Ops:
  7.2 1.8 copy.117
  16.9 1.3 copy.136
  19.7 70.5 %all-gather.2.cloned.1.call-done = bf16[1,2048,576]{2,1,0:T(8,128)(2,1)} async-done(((bf16[1,128,576]{2,1,0:T(8,128)(2,1)}), bf16[1,2048,576]{2,1,0:T(8,128)(2,1)}) %all-gather.2.cloned.1.call-update) | async-done | bytes 2359312 | tf_op jit(solution)/shard_map/all_gather | solution.py:130
  90.1 4.4 conditional.4
  90.1 3.0 fusion.104
  94.5 4.5 conditional.5
  94.6 3.0 fusion.105
  99.1 17.1 %conditional.6 = (f32[2,256,576]{1,2,0:T(8,128)}, f32[2,256,512]{2,1,0:T(8,128)}, f32[2048,576]{0,1:T(8,128)}) conditional(s32[]{:T(128)} %convert_element_type.45, () %tuple.106, (s32[2048]{0:T(1024)S(1)}, s32[2,256]{1,0:T(2,128)S(1)}, bf16[2,256,576]{2,1,0:T(8,128)(2,1)S(1)}, bf16[2048,576]{1,0:T(8,128)(2,1)}, f32[2,256]{1,0:T(2,128)S(1)}, ...), branch_computations={%region_14.15_spmd, %region_15.17_spmd} | conditional | flops 3429892096 | bytes 48645692 | solution.py:161
  99.1 3.0 fusion.15
  102.9 1.1 convolution_bitcast_fusion
  104.1 1.1 scatter-add.1
  105.9 1.1 scatter-add.6
  107.0 3.0 fusion.26
  110.6 5.5 fusion.12
  116.1 18.1 %conditional.7 = ((f32[2,256,576]{1,2,0:T(8,128)}, f32[2,256,512]{2,1,0:T(8,128)}, f32[2048,576]{0,1:T(8,128)})) conditional(s32[]{:T(128)} %convert_element_type.44, (f32[2,256,576]{1,2,0:T(8,128)}, f32[2,256,512]{2,1,0:T(8,128)}, f32[2048,576]{0,1:T(8,128)}) %conditional.6, (f32[2,256,576]{1,2,0:T(8,128)}, s32[2048]{0:T(1024)S(1)}, ...), branch_computations={%region_17.18_spmd, %region_18.20_spmd} | conditional | flops 3431350272 | bytes 60572732 | solution.py:161
  116.2 3.0 fusion.38
  120.0 3.1 fusion.54
  123.0 2.5 fusion.50
  127.0 1.8 fusion.35
  128.9 5.4 add.195
  134.2 2.7 convert_element_type.48
  136.9 2.6 copy.133
  139.6 1.6 copy.122
  141.2 69.6 %reduce-scatter.4.cloned.1.call-done = bf16[128,576]{1,0:T(8,128)(2,1)} async-done(((bf16[2048,576]{1,0:T(8,128)(2,1)}), bf16[128,576]{1,0:T(8,128)(2,1)}) %reduce-scatter.4.cloned.1.call-update) | async-done | bytes 147472
  213.2 1.3 copy.127
  214.5 1.3 convert_element_type.53
  216.1 1.3 copy.130
  217.5 1.3 dynamic-slice.94
  221.4 138.0 %all-reduce.10.cloned.1.call-done = f32[128,576]{1,0:T(8,128)} async-done(((f32[128,576]{1,0:T(8,128)}), f32[128,576]{1,0:T(8,128)}) %all-reduce.10.cloned.1.call-update) | async-done | bytes 294928
  359.4 1.3 dynamic-slice_bitcast_fusion
  360.7 267.6 %all-reduce.12.cloned.1.call-done = (f32[512,512]{1,0:T(8,128)}, f32[512,512]{1,0:T(8,128)}) async-done(((f32[512,512]{1,0:T(8,128)}, f32[512,512]{1,0:T(8,128)}), (f32[512,512]{1,0:T(8,128)}, f32[512,512]{1,0:T(8,128)})) %all-reduce.12.cloned.1.call-update) | async-done | bytes 2097168 | tf_op jit(solution)/shard_map/psum | solution.py:175
  628.3 2.4 copy.177
  (90 shorter events, 19.5 us)
Async XLA Ops:
  7.2 12.1 %copy-start = (bf16[512,512]{1,0:T(8,128)(2,1)S(1)}, bf16[512,512]{1,0:T(8,128)(2,1)}, u32[]{:S(2)}) copy-start(bf16[512,512]{1,0:T(8,128)(2,1)} %param.44) | copy-start | bytes 1572868
  7.2 83.0 %all-gather.2.cloned.1.call-start = ((), (), s32[]{:S(2)}) async-start(), calls=%async_computation.1 | async-start | bytes 2785280 | tf_op jit(solution)/shard_map/all_gather | solution.py:130
  9.0 201.9 %reduce-scatter.4.cloned.1.call-start = ((), (), s32[]{:S(2)}) async-start(), calls=%async_computation.2 | async-start | bytes 2785280
  16.9 1.7 copy-start.5
  18.2 0.9 copy-start.8
  90.1 3.1 copy-start.1
  94.6 3.5 copy-start.2
  99.1 3.0 copy-start.3
  116.2 3.0 copy-start.4
  139.5 219.8 %all-reduce.10.cloned.1.call-start = ((), (), s32[]{:S(2)}) async-start(), calls=%async_computation.3 | async-start | bytes 655360
  139.6 73.3 %copy-start.6 = (bf16[1,128,512]{1,2,0:T(8,128)(2,1)S(1)}, bf16[1,128,512]{1,2,0:T(8,128)(2,1)}, u32[]{:S(2)}) copy-start(bf16[1,128,512]{1,2,0:T(8,128)(2,1)} %copy-done.5) | copy-start | bytes 393220
  212.9 415.4 %all-reduce.12.cloned.1.call-start = ((), (), s32[]{:S(2)}) async-start(), calls=%async_computation.4 | async-start | bytes 4194304 | tf_op jit(solution)/shard_map/psum | solution.py:175
  628.3 2.4 copy-start.7
Sparse Core Ops, SparseCore 0:
  10.7 79.4 all-gather.1
  139.6 71.2 reduce-scatter.3
  213.8 145.4 all-reduce.9
  363.0 265.2 all-reduce.11
where the time goes:
time: 639 us; the launch traced here: 638 us
  waiting for transfers between devices  546 us (85%)
  matrix products  35.4 us (6%)
  local copies, waits for them, and re-layouts  25.4 us (4%)
  between operations  17.2 us (3%)
  other arithmetic  13.9 us (2%)
    psum x1, waiting for transfers between devices, local(): lax.psum((key_weight, value_weight), ('dp', 'ctx'))  268 us
    unnamed x6, waiting for transfers between devices  208 us
    all_gather x1, waiting for transfers between devices, local(): grad_key_rows = lax.all_gather(latent, 'ctx', axis=1, tiled=True)[0]  70.5 us
    unnamed x19, local copies, waits for them, and re-layouts  12.9 us
  transfers between devices with their start and end apart: 4, of which 4 were waited for; matrix products, arithmetic and copies ran while one was open for 3% of the time, Pallas kernels for 0%

commit v1 on v0

v1 whole, which is shorter than its diff:
```python
import math

import jax
import jax.numpy as jnp
from jax import lax
from jax.experimental import pallas as pl
from jax.experimental.pallas import tpu as pltpu
from jax.sharding import Mesh
from jax.sharding import PartitionSpec as P

D_LAT = 512
D_ROPE = 64
D_NOPE = 128
D_V = 128
KEY_WIDTH = D_LAT + D_ROPE
HEADS_DEV = 4
TOK_DEV = 128
STRETCH = 64
N_SLOT = 32
N_CTX = 16
ROWS = HEADS_DEV * STRETCH
CHUNK = 256
PER_CHUNK = CHUNK // STRETCH
STEPS = N_SLOT // PER_CHUNK + 1
SLICE = 8
NEG = -1e30
SCALE = 1.0 / math.sqrt(D_NOPE + D_ROPE)
LOG2E = 1.0 / math.log(2.0)
F32 = jnp.float32
BF16 = jnp.bfloat16
Z_AXES = ("zh", "z0")
PLANE = ("yh", "x")


def dot_nt(a, b):
    return lax.dot_general(a, b, (((1,), (1,)), ((), ())), preferred_element_type=F32)


def dot_tn(a, b):
    return lax.dot_general(a, b, (((0,), (0,)), ((), ())), preferred_element_type=F32)


def dot_nn(a, b):
    return lax.dot_general(a, b, (((1,), (0,)), ((), ())), preferred_element_type=F32)


def attention_kernel(
    order_ref,
    place_ref,
    own_ref,
    other_ref,
    qn_ref,
    qr_ref,
    go_ref,
    wk_ref,
    wv_ref,
    g_own_ref,
    g_other_ref,
    nope_ref,
    rope_ref,
    dw_ref,
    keys,
    query,
    grad,
    score,
    prob_grad,
    side,
    out_sum,
    query_sum,
    gap,
):
    ctx = place_ref[0]
    core = place_ref[1]
    first = order_ref[2 * ctx]
    second = order_ref[2 * ctx + 1]

    for slot in range(N_SLOT):
        block, upper = slot // 2, slot % 2
        rows = jnp.concatenate(
            [own_ref[upper, :, block].astype(F32), other_ref[upper, :, block].astype(F32)], axis=0
        )
        keys[order_ref[slot]] = rows.reshape(STRETCH, KEY_WIDTH).astype(BF16)

    for head in range(HEADS_DEV):
        cols = slice(head * D_NOPE, (head + 1) * D_NOPE)
        q_lat = dot_nt(qn_ref[:, cols], wk_ref[:, cols]).astype(BF16)
        g_lat = dot_nt(go_ref[:, cols], wv_ref[:, cols]).astype(BF16)
        for half in range(2):
            toks = slice(half * STRETCH, (half + 1) * STRETCH)
            into = slice(head * STRETCH, (head + 1) * STRETCH)
            query[half, into, :D_LAT] = q_lat[toks]
            query[half, into, D_LAT:] = qr_ref[toks, head * D_ROPE : (head + 1) * D_ROPE]
            grad[half, into, :] = g_lat[toks]

    col = lax.broadcasted_iota(jnp.int32, (ROWS, CHUNK), 1)
    row = lax.broadcasted_iota(jnp.int32, (ROWS, CHUNK), 0)
    within = col % STRETCH
    side_of = (within // 32 + core) % 2
    key_pos = (col // STRETCH) * STRETCH + ((within % 32) // SLICE) * 16 + side_of * SLICE + within % SLICE
    gap[...] = key_pos - row % STRETCH

    count = first // PER_CHUNK + 1
    zero_col = jnp.zeros((ROWS, 1), F32)

    def place_of(step):
        half = jnp.where(step >= count, 1, 0)
        return half, step - half * count

    def chunk_of(ref, chunk):
        return ref[pl.ds(chunk * PER_CHUNK, PER_CHUNK)].reshape(CHUNK, KEY_WIDTH)

    tops = []
    for step in range(STEPS):
        half, chunk = place_of(step)
        key_rows = chunk_of(keys, chunk)
        limit = jnp.where(half == 1, second, first) * STRETCH - chunk * CHUNK
        raw = dot_nt(query[half], key_rows) * (SCALE * LOG2E)
        raw = jnp.where(gap[...] <= limit, raw, NEG)
        score[step] = raw
        prob_grad[step] = dot_nt(grad[half], key_rows[:, :D_LAT])
        tops.append(jnp.max(raw, axis=1, keepdims=True))

    def by_half(values, join, start):
        sums = [start, start]
        for step, value in enumerate(values):
            in_first = step < count
            sums[0] = join(sums[0], jnp.where(in_first, value, start))
            sums[1] = join(sums[1], jnp.where(in_first, start, value))
        return sums

    top = by_half(tops, jnp.maximum, zero_col + NEG)
    totals, weights = [], []
    for step in range(STEPS):
        expo = jnp.exp2(score[step] - jnp.where(step < count, top[0], top[1]))
        score[step] = expo
        totals.append(jnp.sum(expo, axis=1, keepdims=True))
        weights.append(jnp.sum(expo * prob_grad[step], axis=1, keepdims=True))
    total = by_half(totals, jnp.add, zero_col)
    weight = by_half(weights, jnp.add, zero_col)
    inverse = [1.0 / total[0], 1.0 / total[1]]
    delta = [weight[0] * inverse[0], weight[1] * inverse[1]]

    side[...] = jnp.zeros_like(side)
    out_sum[...] = jnp.zeros_like(out_sum)
    query_sum[...] = jnp.zeros_like(query_sum)
    for step in range(STEPS):
        half, chunk = place_of(step)
        in_first = step < count
        key_rows = chunk_of(keys, chunk)
        probability = score[step] * jnp.where(in_first, inverse[0], inverse[1])
        prob_low = probability.astype(BF16)
        drift = prob_grad[step] - jnp.where(in_first, delta[0], delta[1])
        score_grad = (SCALE * probability * drift).astype(BF16)
        out_sum[half] += dot_nn(prob_low, key_rows[:, :D_LAT])
        query_sum[half] += dot_nn(score_grad, key_rows)
        where = pl.ds(chunk * PER_CHUNK, PER_CHUNK)
        key_side = dot_tn(score_grad, query[half]).reshape(PER_CHUNK, STRETCH, KEY_WIDTH)
        value_side = dot_tn(prob_low, grad[half]).reshape(PER_CHUNK, STRETCH, D_LAT)
        side[where] += key_side
        side[where, :, :D_LAT] += value_side

    for head in range(HEADS_DEV):
        cols = slice(head * D_NOPE, (head + 1) * D_NOPE)
        into = slice(head * STRETCH, (head + 1) * STRETCH)
        query_low = jnp.concatenate([query_sum[0, into, :], query_sum[1, into, :]], axis=0).astype(BF16)
        out_low = jnp.concatenate([out_sum[0, into, :], out_sum[1, into, :]], axis=0).astype(BF16)
        lat_low = query_low[:, :D_LAT]
        rope_ref[:, head * D_ROPE : (head + 1) * D_ROPE] = query_low[:, D_LAT:]
        nope_ref[:, cols] = dot_nn(lat_low, wk_ref[:, cols]).astype(BF16)
        dw_ref[:D_LAT, cols] = dot_tn(lat_low, qn_ref[:, cols]).astype(BF16)
        dw_ref[D_LAT:, cols] = dot_tn(out_low, go_ref[:, cols]).astype(BF16)

    for slot in range(N_SLOT):
        block, upper = slot // 2, slot % 2
        rows = side[order_ref[slot]].reshape(2, 4, SLICE, KEY_WIDTH).astype(BF16)
        g_own_ref[upper, :, block] = rows[0]
        g_other_ref[upper, :, block] = rows[1]


def attention(order, place, own, other, qn, qr, go, wk, wv):
    vmem = pl.BlockSpec(memory_space=pltpu.VMEM)
    smem = pl.BlockSpec(memory_space=pltpu.SMEM)
    part = jax.ShapeDtypeStruct(own.shape, BF16)
    return pl.pallas_call(
        attention_kernel,
        out_shape=(
            part,
            part,
            jax.ShapeDtypeStruct((TOK_DEV, HEADS_DEV * D_NOPE), BF16),
            jax.ShapeDtypeStruct((TOK_DEV, HEADS_DEV * D_ROPE), BF16),
            jax.ShapeDtypeStruct((2 * D_LAT, HEADS_DEV * D_NOPE), BF16),
        ),
        in_specs=[smem, smem] + [vmem] * 7,
        out_specs=(vmem,) * 5,
        scratch_shapes=[
            pltpu.VMEM((N_SLOT, STRETCH, KEY_WIDTH), BF16),
            pltpu.VMEM((2, ROWS, KEY_WIDTH), BF16),
            pltpu.VMEM((2, ROWS, D_LAT), BF16),
            pltpu.VMEM((STEPS, ROWS, CHUNK), F32),
            pltpu.VMEM((STEPS, ROWS, CHUNK), F32),
            pltpu.VMEM((N_SLOT, STRETCH, KEY_WIDTH), F32),
            pltpu.VMEM((2, ROWS, D_LAT), F32),
            pltpu.VMEM((2, ROWS, KEY_WIDTH), F32),
            pltpu.VMEM((ROWS, CHUNK), jnp.int32),
        ],
        compiler_params=pltpu.CompilerParams(vmem_limit_bytes=48 * 1024 * 1024),
        name="latent_attention",
    )(order, place, own, other, qn, qr, go, wk, wv)


def swap(values, axes):
    return lax.all_to_all(values, axes, 0, 0, tiled=True)


def local(latent, q_nope, q_rope, grad_out, w_uk, w_uv, stretch_order):
    ctx = lax.axis_index(Z_AXES)
    core = lax.axis_index("c")
    head = lax.axis_index(PLANE + ("c",))
    other_core = [(0, 1), (1, 0)]
    place = jnp.stack([ctx, core]).astype(jnp.int32)

    mine = lax.dynamic_slice_in_dim(latent[0], head * SLICE, SLICE, 0)
    column = swap(jnp.broadcast_to(mine, (N_CTX, SLICE, KEY_WIDTH)), Z_AXES)
    own = swap(jnp.broadcast_to(column, (8, N_CTX, SLICE, KEY_WIDTH)), PLANE)
    own = own.reshape(2, 4, N_CTX, SLICE, KEY_WIDTH)
    other = lax.ppermute(own, "c", other_core)

    g_own, g_other, nope_grad, rope_grad, dw = attention(
        stretch_order, place, own, other, q_nope[0], q_rope[0], grad_out[0], w_uk, w_uv
    )

    came = lax.ppermute(g_other, "c", other_core)
    pair = (g_own.astype(F32) + came.astype(F32)).astype(BF16)
    planes = swap(pair.reshape(8, N_CTX, SLICE, KEY_WIDTH), PLANE)
    plane_sum = jnp.sum(planes.astype(F32), axis=0).astype(BF16)

    corners = swap(dw.reshape(4, 256, 512), ("dp", "z0"))
    quarter = jnp.sum(corners.astype(F32), axis=0).astype(BF16).reshape(N_CTX, 16, 512)

    packed = jnp.concatenate(
        [
            quarter,
            plane_sum[:, :, :D_LAT],
            plane_sum[:, :, D_LAT:].reshape(N_CTX, 1, SLICE * D_ROPE),
        ],
        axis=1,
    )
    columns = swap(packed, Z_AXES).astype(F32)
    owned = jnp.sum(columns[:, 16:], axis=0)
    d_latent = jnp.concatenate([owned[:8], owned[8].reshape(SLICE, D_ROPE)], axis=1)
    pieces = jnp.sum(columns[:, :16].reshape(8, 2, 16, 512), axis=0).astype(BF16)

    whole = swap(jnp.broadcast_to(pieces, (8, 2, 16, 512)).reshape(N_CTX, 16, 512), Z_AXES)
    whole = swap(jnp.broadcast_to(whole.reshape(256, 512), (4, 256, 512)), ("dp", "z0"))
    whole = whole.reshape(1024, 512).astype(F32)
    return (
        d_latent[None],
        nope_grad[None],
        rope_grad[None],
        whole[:D_LAT],
        whole[D_LAT:],
    )


def solution(mesh):
    fine = Mesh(mesh.devices.reshape(2, 8, 2, 2, 4, 2), ("dp", "zh", "z0", "yh", "x", "c"))
    heads = ("yh", "x", "c")
    placed = (
        P("dp", Z_AXES, None),
        P("dp", Z_AXES, heads),
        P("dp", Z_AXES, heads),
        P("dp", Z_AXES, heads),
        P(None, heads),
        P(None, heads),
        P(),
    )
    return jax.shard_map(
        local,
        mesh=fine,
        in_specs=placed,
        out_specs=(
            P("dp", Z_AXES + heads, None),
            P("dp", Z_AXES, heads),
            P("dp", Z_AXES, heads),
            P(None, heads),
            P(None, heads),
        ),
        check_vma=False,
    )
```

time: 639 us -> 197 us (0.31)
  the two profiles are of different devices: /device:TPU:2 before, /device:TPU:1 now
where the time goes in v1:
time: 197 us
  blocking collectives  126 us (64%)
  waiting for transfers between devices  31.1 us (16%)
  starting transfers between devices  21.7 us (11%)
  Pallas kernels  10.9 us (6%)
  local copies, waits for them, and re-layouts  4.22 us (2%)
    all_to_all x5, blocking collectives, swap(): return lax.all_to_all(values, axes, 0, 0, tiled=True)  126 us
    all_to_all x2, waiting for transfers between devices, swap(): return lax.all_to_all(values, axes, 0, 0, tiled=True)  25.8 us
    all_to_all x2, starting transfers between devices, swap(): return lax.all_to_all(values, axes, 0, 0, tiled=True)  12.2 us
    pallas_call x1, Pallas kernels, attention(): pl.pallas_call(attention_kernel, out_shape=(part, part, jax.ShapeDtypeStr...  10.9 us
    ppermute x1, starting transfers between devices, local(): other = lax.ppermute(own, 'c', other_core)  7.19 us
  transfers between devices with their start and end apart: 4, of which 4 were waited for; matrix products, arithmetic and copies ran while one was open for 1% of the time, Pallas kernels for 0%

profile of v1, /device:TPU:1, one launch (start us, length us, event | category | flops | bytes accessed | tf_op | source)
XLA Modules:
  0.0 196.5 jit_solution(4043472342104912942)
XLA Ops:
  0.6 0.0 copy-start
  0.7 0.9 copy-done
  1.5 0.1 constant_dynamic-slice_fusion
  1.7 0.1 copy.21
  1.8 27.8 %all_to_all.35 = bf16[16,8,576]{2,1,0:T(8,128)(2,1)S(1)} all-to-all(bf16[16,8,576]{2,1,0:T(8,128)(2,1)S(1)} %broadcast_in_dim.21), channel_id=1, replica_groups=mesh['dp'=2,'zh'=8,'z0'=2,'yh'=2,'x'=4,'c'=2] {'zh','z0'}, dimensions={0} | all-to-all | bytes 294912 | tf_op jit(solution)/shard_map/all_to_all | solution.py:212
  29.6 0.1 broadcast_in_dim.22
  29.7 0.0 copy-start.2
  29.7 22.3 %all_to_all.36 = bf16[8,16,8,576]{3,2,1,0:T(8,128)(2,1)S(1)} all-to-all(bf16[8,16,8,576]{3,2,1,0:T(8,128)(2,1)S(1)} %broadcast_in_dim.22), channel_id=1, replica_groups=mesh['dp'=2,'zh'=8,'z0'=2,'yh'=2,'x'=4,'c'=2] {'yh','x'}, dimensions={0} | all-to-all | bytes 2359296 | tf_op jit(solution)/shard_map/all_to_all | solution.py:212
  52.0 7.2 %collective-permute-start = (bf16[2,4,16,8,576]{4,3,2,1,0:T(8,128)(2,1)S(1)}, bf16[2,4,16,8,576]{4,3,2,1,0:T(8,128)(2,1)}, u32[]{:S(2)}, u32[]{:S(2)}) collective-permute-start(bf16[2,4,16,8,576]{4,3,2,1,0:T(8,128)(2,1)S(1)} %bitcast.22), channel_id=1, source_target_pairs={{0,1},{1,0},{2,3},{3,2},{4,5},{5,4},{6,7},{7,6},{8,9},{9,8},{10,11... | collective-permute-start | bytes 3538952 | tf_op jit(solution)/shard_map/ppermute | solution.py:226
  59.2 0.1 pad_add_fusion.place_ref
  59.3 2.7 %collective-permute-done.other_ref = bf16[2,4,16,8,576]{4,3,2,1,0:T(8,128)(2,1)} collective-permute-done((bf16[2,4,16,8,576]{4,3,2,1,0:T(8,128)(2,1)S(1)}, bf16[2,4,16,8,576]{4,3,2,1,0:T(8,128)(2,1)}, u32[]{:S(2)}, u32[]{:S(2)}) %collective-permute-start) | collective-permute-done | bytes 1179680 | tf_op jit(solution)/shard_map/ppermute | solution.py:226
  62.0 10.9 %latent_attention.1 = (bf16[2,4,16,8,576]{4,3,2,1,0:T(8,128)(2,1)S(1)}, bf16[2,4,16,8,576]{4,3,2,1,0:T(8,128)(2,1)S(1)}, bf16[128,512]{1,0:T(8,128)(2,1)}, bf16[128,256]{1,0:T(8,128)(2,1)}, bf16[1024,512]{1,0:T(8,128)(2,1)}) custom-call(s32[32]{0:T(128)S(1)} %copy-done.6, s32[2]{0:T(128)S(1)} %pad_add_fusion.place_ref, bf16[2,4,16,8,576]{4,3,2,1,0:T(8,128)(2,1)} %bitcast.23, ...), custom_call_target="tpu_custom_call" | custom-call | tf_op jit(solution)/shard_map/latent_attention/pallas_call | solution.py:184
  72.9 2.3 %collective-permute-start.1 = (bf16[2,4,16,8,576]{4,3,2,1,0:T(8,128)(2,1)S(1)}, bf16[2,4,16,8,576]{4,3,2,1,0:T(8,128)(2,1)S(1)}, u32[]{:S(2)}, u32[]{:S(2)}) collective-permute-start(bf16[2,4,16,8,576]{4,3,2,1,0:T(8,128)(2,1)S(1)} %get-tuple-element.12), channel_id=1, source_target_pairs={{0,1},{1,0},{2,3},{3,2},{4,5},{5,4},{6,7},{7,6},{8,9},{9,8},{10,11... | collective-permute-start | bytes 3538952 | tf_op jit(solution)/shard_map/ppermute | solution.py:232
  75.2 2.6 %collective-permute-done.1 = bf16[2,4,16,8,576]{4,3,2,1,0:T(8,128)(2,1)S(1)} collective-permute-done((bf16[2,4,16,8,576]{4,3,2,1,0:T(8,128)(2,1)S(1)}, bf16[2,4,16,8,576]{4,3,2,1,0:T(8,128)(2,1)S(1)}, u32[]{:S(2)}, u32[]{:S(2)}) %collective-permute-start.1) | collective-permute-done | bytes 1179680 | tf_op jit(solution)/shard_map/ppermute | solution.py:232
  77.8 0.4 add_convert_fusion
  78.2 22.6 %all_to_all.37 = bf16[8,16,8,576]{3,2,1,0:T(8,128)(2,1)S(1)} all-to-all(bf16[8,16,8,576]{3,2,1,0:T(8,128)(2,1)S(1)} %bitcast.24), channel_id=1, replica_groups=mesh['dp'=2,'zh'=8,'z0'=2,'yh'=2,'x'=4,'c'=2] {'yh','x'}, dimensions={0} | all-to-all | bytes 2359296 | tf_op jit(solution)/shard_map/all_to_all | solution.py:212
  100.8 4.3 %all-to-all-start.2 = ((bf16[4,256,512]{2,1,0:T(8,128)(2,1)}), bf16[4,256,512]{2,1,0:T(8,128)(2,1)S(1)}, u32[]{:S(2)}, u32[]{:S(2)}) async-start(bf16[4,256,512]{2,1,0:T(8,128)(2,1)} %bitcast.7), calls=%async_computation.2 | async-start | bytes 2097152 | tf_op jit(solution)/shard_map/all_to_all | solution.py:212
  105.1 0.2 reduce_sum.43
  105.3 0.1 reshape.47
  105.4 13.6 %all-to-all-done.2 = bf16[4,256,512]{2,1,0:T(8,128)(2,1)S(1)} async-done(((bf16[4,256,512]{2,1,0:T(8,128)(2,1)}), bf16[4,256,512]{2,1,0:T(8,128)(2,1)S(1)}, u32[]{:S(2)}, u32[]{:S(2)}) %all-to-all-start.2) | async-done | bytes 1048608 | tf_op jit(solution)/shard_map/all_to_all | solution.py:212
  119.0 0.2 reduce_sum.42
  119.2 0.1 pad_maximum_fusion
  119.3 28.4 %all_to_all.38 = bf16[16,25,512]{2,1,0:T(8,128)(2,1)S(1)} all-to-all(bf16[16,25,512]{2,1,0:T(8,128)(2,1)S(1)} %pad_maximum_fusion), channel_id=1, replica_groups=mesh['dp'=2,'zh'=8,'z0'=2,'yh'=2,'x'=4,'c'=2] {'zh','z0'}, dimensions={0} | all-to-all | bytes 819200 | tf_op jit(solution)/shard_map/all_to_all | solution.py:212
  147.7 0.1 slice.45
  147.8 25.1 %all_to_all.39 = bf16[16,16,512]{2,1,0:T(8,128)(2,1)S(1)} all-to-all(bf16[16,16,512]{2,1,0:T(8,128)(2,1)S(1)} %bitcast.28), channel_id=1, replica_groups=mesh['dp'=2,'zh'=8,'z0'=2,'yh'=2,'x'=4,'c'=2] {'zh','z0'}, dimensions={0} | all-to-all | bytes 524288 | tf_op jit(solution)/shard_map/all_to_all | solution.py:212
  172.9 1.1 broadcast_in_dim.27
  173.9 7.9 %all-to-all-start.6 = ((bf16[4,256,512]{2,1,0:T(8,128)(2,1)}), bf16[4,256,512]{2,1,0:T(8,128)(2,1)S(1)}, u32[]{:S(2)}, u32[]{:S(2)}) async-start(bf16[4,256,512]{2,1,0:T(8,128)(2,1)} %broadcast_in_dim.27), calls=%async_computation.6 | async-start | bytes 2097152 | tf_op jit(solution)/shard_map/all_to_all | solution.py:212
  181.8 0.1 convert_element_type.26
  182.0 0.1 reshape_squeeze.3
  182.1 0.6 maximum_bitcast_fusion
  182.7 12.2 %all-to-all-done.6 = bf16[4,256,512]{2,1,0:T(8,128)(2,1)S(1)} async-done(((bf16[4,256,512]{2,1,0:T(8,128)(2,1)}), bf16[4,256,512]{2,1,0:T(8,128)(2,1)S(1)}, u32[]{:S(2)}, u32[]{:S(2)}) %all-to-all-start.6) | async-done | bytes 1048608 | tf_op jit(solution)/shard_map/all_to_all | solution.py:212
  194.9 1.6 fusion
  (21 shorter events, 0.2 us)
Async XLA Ops:
  0.6 0.9 copy-start
  29.7 32.3 %copy-start.1 = (bf16[512,512]{1,0:T(8,128)(2,1)S(1)}, bf16[512,512]{1,0:T(8,128)(2,1)}, u32[]{:S(2)}) copy-start(bf16[512,512]{1,0:T(8,128)(2,1)} %wk_ref.1) | copy-start | bytes 1572868
  29.7 32.3 %copy-start.2 = (bf16[512,512]{1,0:T(8,128)(2,1)S(1)}, bf16[512,512]{1,0:T(8,128)(2,1)}, u32[]{:S(2)}) copy-start(bf16[512,512]{1,0:T(8,128)(2,1)} %wv_ref.1) | copy-start | bytes 1572868
  29.7 32.3 %copy-start.3 = (bf16[1,128,512]{2,1,0:T(8,128)(2,1)S(1)}, bf16[1,128,512]{2,1,0:T(8,128)(2,1)}, u32[]{:S(2)}) copy-start(bf16[1,128,512]{2,1,0:T(8,128)(2,1)} %param.8) | copy-start | bytes 393220
  29.7 32.3 %copy-start.4 = (bf16[1,128,512]{2,1,0:T(8,128)(2,1)S(1)}, bf16[1,128,512]{2,1,0:T(8,128)(2,1)}, u32[]{:S(2)}) copy-start(bf16[1,128,512]{2,1,0:T(8,128)(2,1)} %param.10) | copy-start | bytes 393220
  29.7 32.3 %copy-start.5 = (bf16[1,128,256]{2,1,0:T(8,128)(2,1)S(1)}, bf16[1,128,256]{2,1,0:T(8,128)(2,1)}, u32[]{:S(2)}) copy-start(bf16[1,128,256]{2,1,0:T(8,128)(2,1)} %param.9) | copy-start | bytes 196612
  29.7 32.3 %copy-start.6 = (s32[32]{0:T(128)S(1)}, s32[32]{0:T(128)}, u32[]{:S(2)}) copy-start(s32[32]{0:T(128)} %order_ref.1) | copy-start | bytes 388
  52.0 10.0 %copy-start.7 = (bf16[8,16,8,576]{3,2,1,0:T(8,128)(2,1)}, bf16[8,16,8,576]{3,2,1,0:T(8,128)(2,1)S(1)}, u32[]{:S(2)}) copy-start(bf16[8,16,8,576]{3,2,1,0:T(8,128)(2,1)S(1)} %all_to_all.36) | copy-start | bytes 3538948
  52.0 10.0 %collective-permute-start = (bf16[2,4,16,8,576]{4,3,2,1,0:T(8,128)(2,1)S(1)}, bf16[2,4,16,8,576]{4,3,2,1,0:T(8,128)(2,1)}, u32[]{:S(2)}, u32[]{:S(2)}) collective-permute-start(bf16[2,4,16,8,576]{4,3,2,1,0:T(8,128)(2,1)S(1)} %bitcast.22), channel_id=1, source_target_pairs={{0,1},{1,0},{2,3},{3,2},{4,5},{5,4},{6,7},{7,6},{8,9},{9,8},{10,11... | collective-permute-start | bytes 3538952 | tf_op jit(solution)/shard_map/ppermute | solution.py:226
  72.9 4.9 %collective-permute-start.1 = (bf16[2,4,16,8,576]{4,3,2,1,0:T(8,128)(2,1)S(1)}, bf16[2,4,16,8,576]{4,3,2,1,0:T(8,128)(2,1)S(1)}, u32[]{:S(2)}, u32[]{:S(2)}) collective-permute-start(bf16[2,4,16,8,576]{4,3,2,1,0:T(8,128)(2,1)S(1)} %get-tuple-element.12), channel_id=1, source_target_pairs={{0,1},{1,0},{2,3},{3,2},{4,5},{5,4},{6,7},{7,6},{8,9},{9,8},{10,11... | collective-permute-start | bytes 3538952 | tf_op jit(solution)/shard_map/ppermute | solution.py:232
  100.8 18.2 %all-to-all-start.2 = ((bf16[4,256,512]{2,1,0:T(8,128)(2,1)}), bf16[4,256,512]{2,1,0:T(8,128)(2,1)S(1)}, u32[]{:S(2)}, u32[]{:S(2)}) async-start(bf16[4,256,512]{2,1,0:T(8,128)(2,1)} %bitcast.7), calls=%async_computation.2 | async-start | bytes 2097152 | tf_op jit(solution)/shard_map/all_to_all | solution.py:212
  173.9 21.0 %all-to-all-start.6 = ((bf16[4,256,512]{2,1,0:T(8,128)(2,1)}), bf16[4,256,512]{2,1,0:T(8,128)(2,1)S(1)}, u32[]{:S(2)}, u32[]{:S(2)}) async-start(bf16[4,256,512]{2,1,0:T(8,128)(2,1)} %broadcast_in_dim.27), calls=%async_computation.6 | async-start | bytes 2097152 | tf_op jit(solution)/shard_map/all_to_all | solution.py:212

commit v2 on v1

v2 whole, which is shorter than its diff:
```python
import math

import jax
import jax.numpy as jnp
from jax import lax
from jax.experimental import pallas as pl
from jax.experimental.pallas import tpu as pltpu
from jax.sharding import Mesh
from jax.sharding import PartitionSpec as P

D_LAT = 512
D_ROPE = 64
D_NOPE = 128
D_V = 128
KEY_WIDTH = D_LAT + D_ROPE
HEADS_DEV = 4
TOK_DEV = 128
STRETCH = 64
N_SLOT = 32
N_CTX = 16
TEAM = 4
ROWS = TEAM * STRETCH
CHUNK = 256
PER_CHUNK = CHUNK // STRETCH
CHUNKS = N_SLOT // PER_CHUNK
LOW_CHUNKS = CHUNKS // 2
STEPS = CHUNKS + LOW_CHUNKS
SENT = D_NOPE + D_V + 128
SLICE = 8
NEG = -1e30
SCALE = 1.0 / math.sqrt(D_NOPE + D_ROPE)
LOG2E = 1.0 / math.log(2.0)
F32 = jnp.float32
BF16 = jnp.bfloat16
Z_AXES = ("zq", "z1", "z0")
PLANE = ("yh", "x")


def dot_nt(a, b):
    return lax.dot_general(a, b, (((1,), (1,)), ((), ())), preferred_element_type=F32)


def dot_tn(a, b):
    return lax.dot_general(a, b, (((0,), (0,)), ((), ())), preferred_element_type=F32)


def dot_nn(a, b):
    return lax.dot_general(a, b, (((1,), (0,)), ((), ())), preferred_element_type=F32)


def scaled(index, unit):
    return pl.ds(pl.multiple_of(index * unit, unit), unit)


def member(place_ref, ahead):
    return (place_ref[0] % TEAM) ^ ahead


def low_half(order_ref, place_ref, ahead):
    block = place_ref[0] ^ ahead
    return jnp.where(order_ref[2 * block] > order_ref[2 * block + 1], 1, 0)


def split_kernel(place_ref, qn_ref, qr_ref, go_ref, *out_refs):
    for ahead, out_ref in enumerate(out_refs):
        head = member(place_ref, ahead)
        out_ref[:, :D_NOPE] = qn_ref[:, scaled(head, D_NOPE)]
        out_ref[:, D_NOPE : D_NOPE + D_V] = go_ref[:, scaled(head, D_V)]
        two = qr_ref[:, scaled(head // 2, 2 * D_ROPE)]
        one = jnp.where(head % 2 == 1, two[:, D_ROPE:].astype(F32), two[:, :D_ROPE].astype(F32))
        out_ref[:, D_NOPE + D_V : D_NOPE + D_V + D_ROPE] = one.astype(BF16)
        out_ref[:, D_NOPE + D_V + D_ROPE :] = jnp.zeros((TOK_DEV, D_ROPE), BF16)


def prepare_kernel(order_ref, place_ref, *refs):
    rows_refs, (wk_ref, wv_ref, query, grad, qn, go) = refs[:TEAM], refs[TEAM:]
    head = scaled(member(place_ref, 0), D_NOPE)
    wk, wv = wk_ref[:, head], wv_ref[:, head]
    for ahead, rows_ref in enumerate(rows_refs):
        nope, out = rows_ref[:, :D_NOPE], rows_ref[:, D_NOPE : D_NOPE + D_V]
        rope = rows_ref[:, D_NOPE + D_V : D_NOPE + D_V + D_ROPE]
        q_lat = dot_nt(nope, wk).astype(BF16)
        g_lat = dot_nt(out, wv).astype(BF16)
        late = low_half(order_ref, place_ref, ahead)
        into = slice(ahead * STRETCH, (ahead + 1) * STRETCH)
        for half in range(2):
            toks = slice(half * STRETCH, (half + 1) * STRETCH)
            group = half ^ late
            query[group, into, :D_LAT] = q_lat[toks]
            query[group, into, D_LAT:] = rope[toks]
            grad[group, into, :] = g_lat[toks]
            qn[group, into, :] = nope[toks]
            go[group, into, :] = out[toks]


def score_kernel(
    order_ref,
    place_ref,
    own_ref,
    other_ref,
    query,
    grad,
    prob_ref,
    score_grad_ref,
    keys,
    score,
    prob_grad,
):
    @pl.loop(0, N_CTX, unroll=4)
    def _(block):
        for upper in range(2):
            rows = jnp.concatenate(
                [own_ref[upper, :, block].astype(F32), other_ref[upper, :, block].astype(F32)], axis=0
            )
            keys[order_ref[2 * block + upper]] = rows.reshape(STRETCH, KEY_WIDTH).astype(BF16)

    col = lax.broadcasted_iota(jnp.int32, (1, CHUNK), 1)
    within = col % STRETCH
    side_of = (within // 32 + place_ref[1]) % 2
    key_pos = (col // STRETCH) * STRETCH + ((within % 32) // SLICE) * 16 + side_of * SLICE + within % SLICE

    row = lax.broadcasted_iota(jnp.int32, (ROWS, 1), 0)
    row_pos = [row % STRETCH, row % STRETCH]
    for ahead in range(TEAM):
        block = place_ref[0] ^ ahead
        first, second = order_ref[2 * block], order_ref[2 * block + 1]
        mine = row // STRETCH == ahead
        row_pos[0] += jnp.where(mine, jnp.minimum(first, second) * STRETCH, 0)
        row_pos[1] += jnp.where(mine, jnp.maximum(first, second) * STRETCH, 0)

    for group in range(2):
        first_step, chunks = (0, LOW_CHUNKS) if group == 0 else (LOW_CHUNKS, CHUNKS)
        top = jnp.full((ROWS, 1), NEG, F32)
        for chunk in range(chunks):
            cols = slice((first_step + chunk) * CHUNK, (first_step + chunk + 1) * CHUNK)
            key_rows = keys[chunk * PER_CHUNK : (chunk + 1) * PER_CHUNK].reshape(CHUNK, KEY_WIDTH)
            raw = dot_nt(query[group], key_rows) * (SCALE * LOG2E)
            if group == 0 or chunk >= LOW_CHUNKS:
                raw = jnp.where(key_pos + chunk * CHUNK <= row_pos[group], raw, NEG)
            score[:, cols] = raw
            prob_grad[:, cols] = dot_nt(grad[group], key_rows[:, :D_LAT])
            top = jnp.maximum(top, jnp.max(raw, axis=1, keepdims=True))
        total = jnp.zeros((ROWS, 1), F32)
        weight = jnp.zeros((ROWS, 1), F32)
        for chunk in range(chunks):
            cols = slice((first_step + chunk) * CHUNK, (first_step + chunk + 1) * CHUNK)
            expo = jnp.exp2(score[:, cols] - top)
            score[:, cols] = expo
            total += jnp.sum(expo, axis=1, keepdims=True)
            weight += jnp.sum(expo * prob_grad[:, cols], axis=1, keepdims=True)
        inverse = 1.0 / total
        delta = weight * inverse
        for chunk in range(chunks):
            cols = slice((first_step + chunk) * CHUNK, (first_step + chunk + 1) * CHUNK)
            probability = score[:, cols] * inverse
            prob_ref[:, cols] = probability.astype(BF16)
            score_grad_ref[:, cols] = (SCALE * probability * (prob_grad[:, cols] - delta)).astype(BF16)


def query_kernel(
    order_ref,
    place_ref,
    keys,
    prob_ref,
    score_grad_ref,
    qn_ref,
    go_ref,
    wk_ref,
    dw_ref,
    *refs,
):
    rows_refs, (query_low, out_low, nope) = refs[:TEAM], refs[TEAM:]
    for group in range(2):
        cols = slice(0, LOW_CHUNKS * CHUNK) if group == 0 else slice(LOW_CHUNKS * CHUNK, STEPS * CHUNK)
        count = N_SLOT // 2 if group == 0 else N_SLOT
        key_rows = keys[:count].reshape(count * STRETCH, KEY_WIDTH)
        out_low[group] = dot_nn(prob_ref[:, cols], key_rows[:, :D_LAT]).astype(BF16)
        query_low[group] = dot_nn(score_grad_ref[:, cols], key_rows).astype(BF16)

    wk = wk_ref[:, scaled(member(place_ref, 0), D_NOPE)]
    lat_low = query_low[:, :, :D_LAT].reshape(2 * ROWS, D_LAT)
    dw_ref[0] = dot_tn(lat_low, qn_ref[...].reshape(2 * ROWS, D_NOPE)).astype(BF16)
    dw_ref[1] = dot_tn(out_low[...].reshape(2 * ROWS, D_LAT), go_ref[...].reshape(2 * ROWS, D_V)).astype(BF16)
    nope[...] = dot_nn(lat_low, wk).astype(BF16).reshape(2, ROWS, D_NOPE)
    for ahead, rows_ref in enumerate(rows_refs):
        late = low_half(order_ref, place_ref, ahead)
        rows = slice(ahead * STRETCH, (ahead + 1) * STRETCH)
        for half in range(2):
            toks = slice(half * STRETCH, (half + 1) * STRETCH)
            group = half ^ late
            rows_ref[toks, :D_NOPE] = nope[group, rows]
            rows_ref[toks, D_NOPE:] = query_low[group, rows, D_LAT:]


def heads_kernel(place_ref, *refs):
    rows_refs, (nope_ref, rope_ref, store) = refs[:TEAM], refs[TEAM:]
    for ahead, rows_ref in enumerate(rows_refs):
        store[member(place_ref, ahead)] = rows_ref[...]
    for head in range(TEAM):
        nope_ref[:, head * D_NOPE : (head + 1) * D_NOPE] = store[head, :, :D_NOPE]
        rope_ref[:, head * D_ROPE : (head + 1) * D_ROPE] = store[head, :, D_NOPE:]


def side_kernel(
    order_ref, place_ref, query, grad, prob_ref, score_grad_ref, g_own_ref, g_other_ref, side
):
    both_query = query[...].reshape(2 * ROWS, KEY_WIDTH)
    both_grad = grad[...].reshape(2 * ROWS, D_LAT)
    for chunk in range(CHUNKS):
        late = slice((LOW_CHUNKS + chunk) * CHUNK, (LOW_CHUNKS + chunk + 1) * CHUNK)
        early = slice(chunk * CHUNK, (chunk + 1) * CHUNK)
        where = slice(chunk * PER_CHUNK, (chunk + 1) * PER_CHUNK)
        if chunk < LOW_CHUNKS:
            score_grad = jnp.concatenate([score_grad_ref[:, early], score_grad_ref[:, late]], axis=0)
            prob = jnp.concatenate([prob_ref[:, early], prob_ref[:, late]], axis=0)
            key_side, value_side = dot_tn(score_grad, both_query), dot_tn(prob, both_grad)
        else:
            key_side = dot_tn(score_grad_ref[:, late], query[1])
            value_side = dot_tn(prob_ref[:, late], grad[1])
        lat = key_side[:, :D_LAT] + value_side
        side[where, :, :D_LAT] = lat.reshape(PER_CHUNK, STRETCH, D_LAT)
        side[where, :, D_LAT:] = key_side[:, D_LAT:].reshape(PER_CHUNK, STRETCH, D_ROPE)

    @pl.loop(0, N_CTX, unroll=4)
    def _(block):
        for upper in range(2):
            rows = side[order_ref[2 * block + upper]].reshape(2, 4, SLICE, KEY_WIDTH).astype(BF16)
            apart = (upper + place_ref[2]) % 2
            for line in range(4):
                ahead = (line + 4 - place_ref[3]) % 4
                g_own_ref[ahead, apart, block] = rows[0, line]
                g_other_ref[ahead, apart, block] = rows[1, line]


def pair_kernel(own_ref, came_ref, *out_refs):
    for ahead, out_ref in enumerate(out_refs):
        out_ref[...] = (own_ref[ahead].astype(F32) + came_ref[ahead].astype(F32)).astype(BF16)


def line_kernel(a_ref, b_ref, c_ref, d_ref, keep_ref, give_ref):
    for apart, out_ref in enumerate((keep_ref, give_ref)):
        total = a_ref[apart].astype(F32) + b_ref[apart].astype(F32)
        total += c_ref[apart].astype(F32) + d_ref[apart].astype(F32)
        out_ref[...] = total.astype(BF16)


def pack_kernel(columns_ref, keep_ref, came_ref, out_ref):
    pieces = []
    for head in range(TEAM):
        total = columns_ref[head].astype(F32)
        for source in range(head + TEAM, 2 * N_CTX, TEAM):
            total += columns_ref[source].astype(F32)
        pieces.append(total)
    for target in range(N_CTX):
        for pick in range(2):
            piece = pieces[2 * pick + target % 2]
            for octet in range(4):
                lanes = slice((4 * pick + octet) * 128, (4 * pick + octet + 1) * 128)
                out_ref[target, :, lanes] = piece[octet * SLICE : (octet + 1) * SLICE].astype(BF16)
    side = keep_ref[...].astype(F32) + came_ref[...].astype(F32)
    out_ref[:, :, 1024:] = side.astype(BF16)


def spread_kernel(whole_ref, key_ref, value_ref):
    for corner in range(4):
        out_ref, parity = (key_ref, value_ref)[corner // 2], corner % 2
        for source in range(N_CTX):
            for pick in range(2):
                head = 2 * pick + parity
                for octet in range(4):
                    lanes = slice((4 * pick + octet) * 128, (4 * pick + octet + 1) * 128)
                    rows = slice(source * 32 + octet * SLICE, source * 32 + (octet + 1) * SLICE)
                    out_ref[rows, head * 128 : (head + 1) * 128] = whole_ref[corner, source, :, lanes].astype(F32)


VMEM = pl.BlockSpec(memory_space=pltpu.VMEM)
SMEM = pl.BlockSpec(memory_space=pltpu.SMEM)


def call(kernel, name, n_smem, args, outs, scratch=(), flops=2**20, moved=2**20, dtype=BF16):
    shapes = tuple(jax.ShapeDtypeStruct(shape, dtype) for shape in outs)
    return pl.pallas_call(
        kernel,
        out_shape=shapes,
        in_specs=[SMEM] * n_smem + [VMEM] * (len(args) - n_smem),
        out_specs=(VMEM,) * len(outs),
        scratch_shapes=list(scratch),
        compiler_params=pltpu.CompilerParams(vmem_limit_bytes=24 * 1024 * 1024),
        cost_estimate=pl.CostEstimate(flops=flops, bytes_accessed=moved, transcendentals=0),
        name=name,
    )(*args)


QUERY_SHAPE = (2, ROWS, KEY_WIDTH)
GRAD_SHAPE = (2, ROWS, D_LAT)
HEAD_SHAPE = (2, ROWS, D_NOPE)
STEP_SHAPE = (ROWS, STEPS * CHUNK)


def split(place, qn, qr, go):
    return call(split_kernel, "split_heads", 1, (place, qn, qr, go), ((TOK_DEV, SENT),) * TEAM)


def prepare(order, place, rows, wk, wv):
    outs = (QUERY_SHAPE, GRAD_SHAPE, HEAD_SHAPE, HEAD_SHAPE)
    return call(prepare_kernel, "query_latents", 2, (order, place, *rows, wk, wv), outs, (), 2**28, 2**21)


def scores(order, place, own, other, query, grad):
    return call(
        score_kernel,
        "scores",
        2,
        (order, place, own, other, query, grad),
        (STEP_SHAPE, STEP_SHAPE, (N_SLOT, STRETCH, KEY_WIDTH)),
        [pltpu.VMEM(STEP_SHAPE, F32), pltpu.VMEM(STEP_SHAPE, F32)],
        2**31,
        2**23,
    )


def query_side(order, place, keys, prob, score_grad, qn, go, wk):
    rows = (TOK_DEV, D_NOPE + D_ROPE)
    return call(
        query_kernel,
        "query_side",
        2,
        (order, place, keys, prob, score_grad, qn, go, wk),
        ((2, D_LAT, D_NOPE),) + (rows,) * TEAM,
        [pltpu.VMEM(QUERY_SHAPE, BF16), pltpu.VMEM(GRAD_SHAPE, BF16), pltpu.VMEM(HEAD_SHAPE, BF16)],
        2**31,
        2**23,
    )


def put_heads(place, rows):
    return call(
        heads_kernel,
        "put_heads",
        1,
        (place, *rows),
        ((TOK_DEV, TEAM * D_NOPE), (TOK_DEV, TEAM * D_ROPE)),
        [pltpu.VMEM((TEAM, TOK_DEV, D_NOPE + D_ROPE), BF16)],
    )


def side_sums(order, place, query, grad, prob, score_grad):
    part = (4, 2, N_CTX, SLICE, KEY_WIDTH)
    return call(
        side_kernel,
        "key_side",
        2,
        (order, place, query, grad, prob, score_grad),
        (part, part),
        [pltpu.VMEM((N_SLOT, STRETCH, KEY_WIDTH), F32)],
        2**31,
        2**23,
    )


def swap(values, axes):
    return lax.all_to_all(values, axes, 0, 0, tiled=True)


def flip(values, axis):
    return lax.ppermute(values, axis, [(0, 1), (1, 0)])


def team_swap(parts):
    moved = [parts[0]]
    for ahead in range(1, TEAM):
        moved.append(lax.ppermute(parts[ahead], ("z1", "z0"), [(i, i ^ ahead) for i in range(TEAM)]))
    return moved


def local(latent, q_nope, q_rope, grad_out, w_uk, w_uv, stretch_order):
    head = lax.axis_index(PLANE + ("c",))
    places = (Z_AXES, "c", "yh", "x")
    place = jnp.stack([lax.axis_index(axis) for axis in places]).astype(jnp.int32)

    mine = lax.dynamic_slice_in_dim(latent[0], head * SLICE, SLICE, 0)
    column = swap(jnp.broadcast_to(mine, (N_CTX, SLICE, KEY_WIDTH)), Z_AXES)
    own = swap(jnp.broadcast_to(column, (8, N_CTX, SLICE, KEY_WIDTH)), PLANE)
    rows = team_swap(split(place, q_nope[0], q_rope[0], grad_out[0]))
    own, *rows = lax.optimization_barrier((own, *rows))
    query, grad, qn, go = prepare(stretch_order, place, rows, w_uk, w_uv)
    own = own.reshape(2, 4, N_CTX, SLICE, KEY_WIDTH)
    other = flip(own, "c")

    prob, score_grad, keys = scores(stretch_order, place, own, other, query, grad)
    g_own, g_other = side_sums(stretch_order, place, query, grad, prob, score_grad)
    came = flip(g_other, "c")
    prob, g_own = lax.optimization_barrier((prob, g_own))
    dw, *rows = query_side(stretch_order, place, keys, prob, score_grad, qn, go, w_uk)

    half = (2, N_CTX, SLICE, KEY_WIDTH)
    parts = call(pair_kernel, "pair_sum", 0, (g_own, came), (half,) * 4)
    dw, *parts = lax.optimization_barrier((dw, *parts))
    lines = [parts[0]]
    for ahead in (1, 3, 2):
        lines.append(lax.ppermute(parts[ahead], "x", [(i, (i + ahead) % 4) for i in range(4)]))

    columns = swap(dw.reshape(2 * N_CTX, 32, D_NOPE), ("dp", *Z_AXES))

    keep, give = call(line_kernel, "line_sum", 0, lines, (half[1:],) * 2)
    came = flip(give, "yh")
    (packed,) = call(pack_kernel, "pack", 0, (columns, keep, came), ((N_CTX, SLICE, 1024 + KEY_WIDTH),))
    packed = swap(packed, Z_AXES)
    nope_grad, rope_grad = put_heads(place, team_swap(rows))
    d_latent = jnp.sum(packed[:, :, 1024:].astype(F32), axis=0)
    whole = swap(jnp.broadcast_to(packed[:, :, :1024], (4, N_CTX, SLICE, 1024)), ("dp", "z0"))
    wide = (D_LAT, HEADS_DEV * D_NOPE)
    key_weight, value_weight = call(spread_kernel, "spread", 0, (whole,), (wide, wide), dtype=F32)
    return (d_latent[None], nope_grad[None], rope_grad[None], key_weight, value_weight)


def solution(mesh):
    fine = Mesh(mesh.devices.reshape(2, 4, 2, 2, 2, 4, 2), ("dp", *Z_AXES, "yh", "x", "c"))
    heads = ("yh", "x", "c")
    placed = (
        P("dp", Z_AXES, None),
        P("dp", Z_AXES, heads),
        P("dp", Z_AXES, heads),
        P("dp", Z_AXES, heads),
        P(None, heads),
        P(None, heads),
        P(),
    )
    return jax.shard_map(
        local,
        mesh=fine,
        in_specs=placed,
        out_specs=(
            P("dp", Z_AXES + heads, None),
            P("dp", Z_AXES, heads),
            P("dp", Z_AXES, heads),
            P(None, heads),
            P(None, heads),
        ),
        check_vma=False,
    )
```

time: 197 us -> 174 us (0.88)
  the two profiles are of different devices: /device:TPU:1 before, /device:TPU:2 now
where the time goes in v2:
time: 174 us
  blocking collectives  64.5 us (37%)
  starting transfers between devices  57 us (33%)
  waiting for transfers between devices  30.5 us (18%)
  Pallas kernels  16.5 us (9%)
  local copies, waits for them, and re-layouts  3.48 us (2%)
    all_to_all x2, blocking collectives, swap(): return lax.all_to_all(values, axes, 0, 0, tiled=True)  64.5 us
    ppermute x6, starting transfers between devices, team_swap(): lax.ppermute(parts[ahead], ('z1', 'z0'), [(i, i ^ ahead) for i in range(T...  21.2 us
    all_to_all x3, starting transfers between devices, swap(): return lax.all_to_all(values, axes, 0, 0, tiled=True)  19 us
    pallas_call x10, Pallas kernels, call(): pl.pallas_call(kernel, out_shape=shapes, in_specs=[SMEM] * n_smem + [VMEM...  16.5 us
    ppermute x3, waiting for transfers between devices, local(): lax.ppermute(parts[ahead], 'x', [(i, (i + ahead) % 4) for i in range(4)])  12.8 us
    ppermute x6, waiting for transfers between devices, team_swap(): lax.ppermute(parts[ahead], ('z1', 'z0'), [(i, i ^ ahead) for i in range(T...  10.9 us
    ppermute x3, starting transfers between devices, local(): lax.ppermute(parts[ahead], 'x', [(i, (i + ahead) % 4) for i in range(4)])  8.97 us
    ppermute x3, starting transfers between devices, flip(): return lax.ppermute(values, axis, [(0, 1), (1, 0)])  7.88 us
  transfers between devices with their start and end apart: 15, of which 9 were waited for; matrix products, arithmetic and copies ran while one was open for 0% of the time, Pallas kernels for 4%

profile of v2, /device:TPU:2, one launch (start us, length us, event | category | flops | bytes accessed | tf_op | source)
XLA Modules:
  0.0 173.5 jit_solution(6174419298494040813)
XLA Ops:
  1.8 30.6 %all_to_all.25 = bf16[16,8,576]{2,1,0:T(8,128)(2,1)S(1)} all-to-all(bf16[16,8,576]{2,1,0:T(8,128)(2,1)S(1)} %broadcast_in_dim.18), channel_id=1, replica_groups=mesh['dp'=2,'zq'=4,'z1'=2,'z0'=2,'yh'=2,'x'=4,'c'=2] {'zq','z1','z0'}, dimensions={0} | all-to-all | bytes 294912 | tf_op jit(solution)/shard_map/all_to_all | solution.py:362
  32.4 1.2 broadcast_in_dim.19
  33.7 7.6 %all-to-all-start.1 = ((bf16[8,16,8,576]{3,2,1,0:T(8,128)(2,1)}), bf16[8,16,8,576]{3,2,1,0:T(8,128)(2,1)S(1)}, u32[]{:S(2)}, u32[]{:S(2)}) async-start(bf16[8,16,8,576]{3,2,1,0:T(8,128)(2,1)} %broadcast_in_dim.19), calls=%async_computation.1 | async-start | bytes 2621440 | tf_op jit(solution)/shard_map/all_to_all | solution.py:362
  42.1 3.1 %collective-permute-start = (bf16[128,384]{1,0:T(8,128)(2,1)S(1)}, bf16[128,384]{1,0:T(8,128)(2,1)S(1)}, u32[]{:S(2)}, u32[]{:S(2)}) collective-permute-start(bf16[128,384]{1,0:T(8,128)(2,1)S(1)} %get-tuple-element.46), channel_id=1, source_target_pairs={{0,16},{16,0},{32,48},{48,32},{1,17},{17,1},{33,49},{49,33},{2,18}... | collective-permute-start | bytes 294920 | tf_op jit(solution)/shard_map/ppermute | solution.py:372
  45.2 3.7 %collective-permute-start.1 = (bf16[128,384]{1,0:T(8,128)(2,1)S(1)}, bf16[128,384]{1,0:T(8,128)(2,1)S(1)}, u32[]{:S(2)}, u32[]{:S(2)}) collective-permute-start(bf16[128,384]{1,0:T(8,128)(2,1)S(1)} %get-tuple-element.47), channel_id=1, source_target_pairs={{0,32},{16,48},{32,0},{48,16},{1,33},{17,49},{33,1},{49,17},{2,34}... | collective-permute-start | bytes 294920 | tf_op jit(solution)/shard_map/ppermute | solution.py:372
  48.9 3.4 %collective-permute-start.2 = (bf16[128,384]{1,0:T(8,128)(2,1)S(1)}, bf16[128,384]{1,0:T(8,128)(2,1)S(1)}, u32[]{:S(2)}, u32[]{:S(2)}) collective-permute-start(bf16[128,384]{1,0:T(8,128)(2,1)S(1)} %get-tuple-element.48), channel_id=1, source_target_pairs={{0,48},{16,32},{32,16},{48,0},{1,49},{17,33},{33,17},{49,1},{2,50}... | collective-permute-start | bytes 294920 | tf_op jit(solution)/shard_map/ppermute | solution.py:372
  52.3 2.7 %collective-permute-done.1.refs_2_ = bf16[128,384]{1,0:T(8,128)(2,1)S(1)} collective-permute-done((bf16[128,384]{1,0:T(8,128)(2,1)S(1)}, bf16[128,384]{1,0:T(8,128)(2,1)S(1)}, u32[]{:S(2)}, u32[]{:S(2)}) %collective-permute-start.1) | collective-permute-done | bytes 98336 | tf_op jit(solution)/shard_map/ppermute | solution.py:372
  55.0 2.2 %collective-permute-done.2.refs_3_ = bf16[128,384]{1,0:T(8,128)(2,1)S(1)} collective-permute-done((bf16[128,384]{1,0:T(8,128)(2,1)S(1)}, bf16[128,384]{1,0:T(8,128)(2,1)S(1)}, u32[]{:S(2)}, u32[]{:S(2)}) %collective-permute-start.2) | collective-permute-done | bytes 98336 | tf_op jit(solution)/shard_map/ppermute | solution.py:372
  57.2 1.9 %collective-permute-start.3 = (bf16[2,4,16,8,576]{4,3,2,1,0:T(8,128)(2,1)S(1)}, bf16[2,4,16,8,576]{4,3,2,1,0:T(8,128)(2,1)S(1)}, u32[]{:S(2)}, u32[]{:S(2)}) collective-permute-start(bf16[2,4,16,8,576]{4,3,2,1,0:T(8,128)(2,1)S(1)} %bitcast.13), channel_id=1, source_target_pairs={{0,1},{1,0},{2,3},{3,2},{4,5},{5,4},{6,7},{7,6},{8,9},{9,8},{10,11... | collective-permute-start | bytes 3538952 | tf_op jit(solution)/shard_map/ppermute | solution.py:366
  60.1 2.0 %collective-permute-done.3.other_ref = bf16[2,4,16,8,576]{4,3,2,1,0:T(8,128)(2,1)S(1)} collective-permute-done((bf16[2,4,16,8,576]{4,3,2,1,0:T(8,128)(2,1)S(1)}, bf16[2,4,16,8,576]{4,3,2,1,0:T(8,128)(2,1)S(1)}, u32[]{:S(2)}, u32[]{:S(2)}) %collective-permute-start.3) | collective-permute-done | bytes 1179680 | tf_op jit(solution)/shard_map/ppermute | solution.py:366
  62.1 4.1 %scores.1 = (bf16[256,3072]{1,0:T(8,128)(2,1)S(1)}, bf16[256,3072]{1,0:T(8,128)(2,1)S(1)}, bf16[32,64,576]{2,1,0:T(8,128)(2,1)S(1)}) custom-call(s32[32]{0:T(128)S(1)} %copy-done.6, s32[4]{0:T(128)S(1)} %pad_add_fusion.place_ref, bf16[2,4,16,8,576]{4,3,2,1,0:T(8,128)(2,1)S(1)} %bitcast.14, bf16[2,4,16,8,576]{4,3,2,1,0:T(8,128)(2,1)S(1)} %collective-permute-done.3.other_ref, ...), custom_call_target="tpu_custom_call" | custom-call | flops 2147483648 | bytes 8388608 | tf_op jit(solution)/shard_map/scores/pallas_call | solution.py:282
  66.2 3.4 %key_side.1 = (bf16[4,2,16,8,576]{4,3,2,1,0:T(8,128)(2,1)S(1)}, bf16[4,2,16,8,576]{4,3,2,1,0:T(8,128)(2,1)S(1)}) custom-call(s32[32]{0:T(128)S(1)} %copy-done.6, s32[4]{0:T(128)S(1)} %pad_add_fusion.place_ref, bf16[2,256,576]{2,1,0:T(8,128)(2,1)S(1)} %get-tuple-element.54.query, bf16[2,256,512]{2,1,0:T(8,128)(2,1)S(1)} %get-tuple-element.55.grad, ...), custom_call_target="tpu_custom_call" | custom-call | flops 2147483648 | bytes 8388608 | tf_op jit(solution)/shard_map/key_side/pallas_call | solution.py:282
  69.6 2.0 %collective-permute-start.4 = (bf16[4,2,16,8,576]{4,3,2,1,0:T(8,128)(2,1)S(1)}, bf16[4,2,16,8,576]{4,3,2,1,0:T(8,128)(2,1)S(1)}, u32[]{:S(2)}, u32[]{:S(2)}) collective-permute-start(bf16[4,2,16,8,576]{4,3,2,1,0:T(8,128)(2,1)S(1)} %get-tuple-element.65), channel_id=1, source_target_pairs={{0,1},{1,0},{2,3},{3,2},{4,5},{5,4},{6,7},{7,6},{8,9},{9,8},{10,11... | collective-permute-start | bytes 3538952 | tf_op jit(solution)/shard_map/ppermute | solution.py:366
  71.7 4.0 %query_side.1 = (bf16[2,512,128]{2,1,0:T(8,128)(2,1)}, bf16[128,192]{1,0:T(8,128)(2,1)S(1)}, bf16[128,192]{1,0:T(8,128)(2,1)S(1)}, bf16[128,192]{1,0:T(8,128)(2,1)S(1)}, bf16[128,192]{1,0:T(8,128)(2,1)S(1)}) custom-call(s32[32]{0:T(128)S(1)} %copy-done.6, s32[4]{0:T(128)S(1)} %pad_add_fusion.place_ref, bf16[32,64,576]{2,1,0:T(8,128)(2,1)S(1)} %get-tuple-element.56.keys, ...), custom_call_target="tpu_custom_call" | custom-call | flops 2147483648 | bytes 8388608 | tf_op jit(solution)/shard_map/query_side/pallas_call | solution.py:282
  76.0 7.6 %all-to-all-start.2 = ((bf16[32,32,128]{2,1,0:T(8,128)(2,1)}), bf16[32,32,128]{2,1,0:T(8,128)(2,1)S(1)}, u32[]{:S(2)}, u32[]{:S(2)}) async-start(bf16[32,32,128]{2,1,0:T(8,128)(2,1)} %bitcast.9), calls=%async_computation.2 | async-start | bytes 524288 | tf_op jit(solution)/shard_map/all_to_all | solution.py:362
  83.6 1.9 %collective-permute-start.5 = (bf16[2,16,8,576]{3,2,1,0:T(8,128)(2,1)S(1)}, bf16[2,16,8,576]{3,2,1,0:T(8,128)(2,1)S(1)}, u32[]{:S(2)}, u32[]{:S(2)}) collective-permute-start(bf16[2,16,8,576]{3,2,1,0:T(8,128)(2,1)S(1)} %get-tuple-element.72), channel_id=1, source_target_pairs={{0,2},{2,4},{4,6},{6,0},{1,3},{3,5},{5,7},{7,1},{8,10},{10,12},{12... | collective-permute-start | bytes 884744 | tf_op jit(solution)/shard_map/ppermute | solution.py:401
  85.5 3.9 %collective-permute-start.6 = (bf16[2,16,8,576]{3,2,1,0:T(8,128)(2,1)S(1)}, bf16[2,16,8,576]{3,2,1,0:T(8,128)(2,1)S(1)}, u32[]{:S(2)}, u32[]{:S(2)}) collective-permute-start(bf16[2,16,8,576]{3,2,1,0:T(8,128)(2,1)S(1)} %get-tuple-element.73), channel_id=1, source_target_pairs={{0,6},{2,0},{4,2},{6,4},{1,7},{3,1},{5,3},{7,5},{8,14},{10,8},{12,... | collective-permute-start | bytes 884744 | tf_op jit(solution)/shard_map/ppermute | solution.py:401
  89.5 3.1 %collective-permute-start.7 = (bf16[2,16,8,576]{3,2,1,0:T(8,128)(2,1)S(1)}, bf16[2,16,8,576]{3,2,1,0:T(8,128)(2,1)S(1)}, u32[]{:S(2)}, u32[]{:S(2)}) collective-permute-start(bf16[2,16,8,576]{3,2,1,0:T(8,128)(2,1)S(1)} %get-tuple-element.74), channel_id=1, source_target_pairs={{0,4},{2,6},{4,0},{6,2},{1,5},{3,7},{5,1},{7,3},{8,12},{10,14},{12... | collective-permute-start | bytes 884744 | tf_op jit(solution)/shard_map/ppermute | solution.py:401
  92.6 3.5 %collective-permute-done.5.b_ref = bf16[2,16,8,576]{3,2,1,0:T(8,128)(2,1)S(1)} collective-permute-done((bf16[2,16,8,576]{3,2,1,0:T(8,128)(2,1)S(1)}, bf16[2,16,8,576]{3,2,1,0:T(8,128)(2,1)S(1)}, u32[]{:S(2)}, u32[]{:S(2)}) %collective-permute-start.5) | collective-permute-done | bytes 294944 | tf_op jit(solution)/shard_map/ppermute | solution.py:401
  96.1 1.5 collective-permute-done.6.c_ref
  97.6 7.8 %collective-permute-done.7.d_ref = bf16[2,16,8,576]{3,2,1,0:T(8,128)(2,1)S(1)} collective-permute-done((bf16[2,16,8,576]{3,2,1,0:T(8,128)(2,1)S(1)}, bf16[2,16,8,576]{3,2,1,0:T(8,128)(2,1)S(1)}, u32[]{:S(2)}, u32[]{:S(2)}) %collective-permute-start.7) | collective-permute-done | bytes 294944 | tf_op jit(solution)/shard_map/ppermute | solution.py:401
  105.5 3.9 %collective-permute-start.8 = (bf16[16,8,576]{2,1,0:T(8,128)(2,1)S(1)}, bf16[16,8,576]{2,1,0:T(8,128)(2,1)S(1)}, u32[]{:S(2)}, u32[]{:S(2)}) collective-permute-start(bf16[16,8,576]{2,1,0:T(8,128)(2,1)S(1)} %get-tuple-element.76), channel_id=1, source_target_pairs={{0,8},{8,0},{1,9},{9,1},{2,10},{10,2},{3,11},{11,3},{4,12},{12,4},... | collective-permute-start | bytes 442376 | tf_op jit(solution)/shard_map/ppermute | solution.py:366
  109.5 4.8 %collective-permute-done.8.came_ref = bf16[16,8,576]{2,1,0:T(8,128)(2,1)S(1)} collective-permute-done((bf16[16,8,576]{2,1,0:T(8,128)(2,1)S(1)}, bf16[16,8,576]{2,1,0:T(8,128)(2,1)S(1)}, u32[]{:S(2)}, u32[]{:S(2)}) %collective-permute-start.8) | collective-permute-done | bytes 147488 | tf_op jit(solution)/shard_map/ppermute | solution.py:366
  114.4 33.8 %all_to_all.26 = bf16[16,8,1600]{2,1,0:T(8,128)(2,1)S(1)} all-to-all(bf16[16,8,1600]{2,1,0:T(8,128)(2,1)S(1)} %pack.1), channel_id=1, replica_groups=mesh['dp'=2,'zq'=4,'z1'=2,'z0'=2,'yh'=2,'x'=4,'c'=2] {'zq','z1','z0'}, dimensions={0} | all-to-all | bytes 819200 | tf_op jit(solution)/shard_map/all_to_all | solution.py:362
  149.3 3.7 %all-to-all-start.4 = ((bf16[4,16,8,1024]{3,2,1,0:T(8,128)(2,1)}), bf16[4,16,8,1024]{3,2,1,0:T(8,128)(2,1)S(1)}, u32[]{:S(2)}, u32[]{:S(2)}) async-start(bf16[4,16,8,1024]{3,2,1,0:T(8,128)(2,1)} %broadcast_in_dim.23), calls=%async_computation.4 | async-start | bytes 2097152 | tf_op jit(solution)/shard_map/all_to_all | solution.py:362
  153.0 3.9 %collective-permute-start.9 = (bf16[128,192]{1,0:T(8,128)(2,1)S(1)}, bf16[128,192]{1,0:T(8,128)(2,1)S(1)}, u32[]{:S(2)}, u32[]{:S(2)}) collective-permute-start(bf16[128,192]{1,0:T(8,128)(2,1)S(1)} %get-tuple-element.78), channel_id=1, source_target_pairs={{0,16},{16,0},{32,48},{48,32},{1,17},{17,1},{33,49},{49,33},{2,18}... | collective-permute-start | bytes 147464 | tf_op jit(solution)/shard_map/ppermute | solution.py:372
  157.0 5.2 %collective-permute-start.10 = (bf16[128,192]{1,0:T(8,128)(2,1)S(1)}, bf16[128,192]{1,0:T(8,128)(2,1)S(1)}, u32[]{:S(2)}, u32[]{:S(2)}) collective-permute-start(bf16[128,192]{1,0:T(8,128)(2,1)S(1)} %get-tuple-element.79), channel_id=1, source_target_pairs={{0,32},{16,48},{32,0},{48,16},{1,33},{17,49},{33,1},{49,17},{2,34}... | collective-permute-start | bytes 147464 | tf_op jit(solution)/shard_map/ppermute | solution.py:372
  162.2 1.9 %collective-permute-start.11 = (bf16[128,192]{1,0:T(8,128)(2,1)S(1)}, bf16[128,192]{1,0:T(8,128)(2,1)S(1)}, u32[]{:S(2)}, u32[]{:S(2)}) collective-permute-start(bf16[128,192]{1,0:T(8,128)(2,1)S(1)} %get-tuple-element.80), channel_id=1, source_target_pairs={{0,48},{16,32},{32,16},{48,0},{1,49},{17,33},{33,17},{49,1},{2,50}... | collective-permute-start | bytes 147464 | tf_op jit(solution)/shard_map/ppermute | solution.py:372
  164.1 2.3 %collective-permute-done.9.refs_1_ = bf16[128,192]{1,0:T(8,128)(2,1)S(1)} collective-permute-done((bf16[128,192]{1,0:T(8,128)(2,1)S(1)}, bf16[128,192]{1,0:T(8,128)(2,1)S(1)}, u32[]{:S(2)}, u32[]{:S(2)}) %collective-permute-start.9) | collective-permute-done | bytes 49184 | tf_op jit(solution)/shard_map/ppermute | solution.py:372
  166.4 3.7 %collective-permute-done.11.refs_3_ = bf16[128,192]{1,0:T(8,128)(2,1)S(1)} collective-permute-done((bf16[128,192]{1,0:T(8,128)(2,1)S(1)}, bf16[128,192]{1,0:T(8,128)(2,1)S(1)}, u32[]{:S(2)}, u32[]{:S(2)}) %collective-permute-start.11) | collective-permute-done | bytes 49184 | tf_op jit(solution)/shard_map/ppermute | solution.py:372
  170.1 1.3 put_heads.1
  172.1 1.4 spread.1
  (32 shorter events, 5.3 us)
Async XLA Ops:
  0.6 0.9 copy-start
  33.6 7.7 %copy-start.3 = (bf16[1,128,512]{2,1,0:T(8,128)(2,1)S(1)}, bf16[1,128,512]{2,1,0:T(8,128)(2,1)}, u32[]{:S(2)}) copy-start(bf16[1,128,512]{2,1,0:T(8,128)(2,1)} %param.8) | copy-start | bytes 393220
  33.6 7.7 %copy-start.4 = (bf16[1,128,512]{2,1,0:T(8,128)(2,1)S(1)}, bf16[1,128,512]{2,1,0:T(8,128)(2,1)}, u32[]{:S(2)}) copy-start(bf16[1,128,512]{2,1,0:T(8,128)(2,1)} %param.10) | copy-start | bytes 393220
  33.6 7.7 %copy-start.5 = (bf16[1,128,256]{2,1,0:T(8,128)(2,1)S(1)}, bf16[1,128,256]{2,1,0:T(8,128)(2,1)}, u32[]{:S(2)}) copy-start(bf16[1,128,256]{2,1,0:T(8,128)(2,1)} %param.9) | copy-start | bytes 196612
  33.6 25.5 %copy-start.1 = (bf16[512,512]{1,0:T(8,128)(2,1)S(1)}, bf16[512,512]{1,0:T(8,128)(2,1)}, u32[]{:S(2)}) copy-start(bf16[512,512]{1,0:T(8,128)(2,1)} %refs_5_.1) | copy-start | bytes 1572868
  33.6 25.5 %copy-start.2 = (bf16[512,512]{1,0:T(8,128)(2,1)S(1)}, bf16[512,512]{1,0:T(8,128)(2,1)}, u32[]{:S(2)}) copy-start(bf16[512,512]{1,0:T(8,128)(2,1)} %wk_ref.1) | copy-start | bytes 1572868
  33.7 25.5 %copy-start.6 = (s32[32]{0:T(128)S(1)}, s32[32]{0:T(128)}, u32[]{:S(2)}) copy-start(s32[32]{0:T(128)} %order_ref.7) | copy-start | bytes 388
  33.7 23.5 %all-to-all-start.1 = ((bf16[8,16,8,576]{3,2,1,0:T(8,128)(2,1)}), bf16[8,16,8,576]{3,2,1,0:T(8,128)(2,1)S(1)}, u32[]{:S(2)}, u32[]{:S(2)}) async-start(bf16[8,16,8,576]{3,2,1,0:T(8,128)(2,1)} %broadcast_in_dim.19), calls=%async_computation.1 | async-start | bytes 2621440 | tf_op jit(solution)/shard_map/all_to_all | solution.py:362
  42.1 10.1 %collective-permute-start = (bf16[128,384]{1,0:T(8,128)(2,1)S(1)}, bf16[128,384]{1,0:T(8,128)(2,1)S(1)}, u32[]{:S(2)}, u32[]{:S(2)}) collective-permute-start(bf16[128,384]{1,0:T(8,128)(2,1)S(1)} %get-tuple-element.46), channel_id=1, source_target_pairs={{0,16},{16,0},{32,48},{48,32},{1,17},{17,1},{33,49},{49,33},{2,18}... | collective-permute-start | bytes 294920 | tf_op jit(solution)/shard_map/ppermute | solution.py:372
  45.2 9.8 %collective-permute-start.1 = (bf16[128,384]{1,0:T(8,128)(2,1)S(1)}, bf16[128,384]{1,0:T(8,128)(2,1)S(1)}, u32[]{:S(2)}, u32[]{:S(2)}) collective-permute-start(bf16[128,384]{1,0:T(8,128)(2,1)S(1)} %get-tuple-element.47), channel_id=1, source_target_pairs={{0,32},{16,48},{32,0},{48,16},{1,33},{17,49},{33,1},{49,17},{2,34}... | collective-permute-start | bytes 294920 | tf_op jit(solution)/shard_map/ppermute | solution.py:372
  48.9 8.3 %collective-permute-start.2 = (bf16[128,384]{1,0:T(8,128)(2,1)S(1)}, bf16[128,384]{1,0:T(8,128)(2,1)S(1)}, u32[]{:S(2)}, u32[]{:S(2)}) collective-permute-start(bf16[128,384]{1,0:T(8,128)(2,1)S(1)} %get-tuple-element.48), channel_id=1, source_target_pairs={{0,48},{16,32},{32,16},{48,0},{1,49},{17,33},{33,17},{49,1},{2,50}... | collective-permute-start | bytes 294920 | tf_op jit(solution)/shard_map/ppermute | solution.py:372
  57.2 4.9 %collective-permute-start.3 = (bf16[2,4,16,8,576]{4,3,2,1,0:T(8,128)(2,1)S(1)}, bf16[2,4,16,8,576]{4,3,2,1,0:T(8,128)(2,1)S(1)}, u32[]{:S(2)}, u32[]{:S(2)}) collective-permute-start(bf16[2,4,16,8,576]{4,3,2,1,0:T(8,128)(2,1)S(1)} %bitcast.13), channel_id=1, source_target_pairs={{0,1},{1,0},{2,3},{3,2},{4,5},{5,4},{6,7},{7,6},{8,9},{9,8},{10,11... | collective-permute-start | bytes 3538952 | tf_op jit(solution)/shard_map/ppermute | solution.py:366
  69.6 6.0 %collective-permute-start.4 = (bf16[4,2,16,8,576]{4,3,2,1,0:T(8,128)(2,1)S(1)}, bf16[4,2,16,8,576]{4,3,2,1,0:T(8,128)(2,1)S(1)}, u32[]{:S(2)}, u32[]{:S(2)}) collective-permute-start(bf16[4,2,16,8,576]{4,3,2,1,0:T(8,128)(2,1)S(1)} %get-tuple-element.65), channel_id=1, source_target_pairs={{0,1},{1,0},{2,3},{3,2},{4,5},{5,4},{6,7},{7,6},{8,9},{9,8},{10,11... | collective-permute-start | bytes 3538952 | tf_op jit(solution)/shard_map/ppermute | solution.py:366
  76.0 38.3 %all-to-all-start.2 = ((bf16[32,32,128]{2,1,0:T(8,128)(2,1)}), bf16[32,32,128]{2,1,0:T(8,128)(2,1)S(1)}, u32[]{:S(2)}, u32[]{:S(2)}) async-start(bf16[32,32,128]{2,1,0:T(8,128)(2,1)} %bitcast.9), calls=%async_computation.2 | async-start | bytes 524288 | tf_op jit(solution)/shard_map/all_to_all | solution.py:362
  83.6 12.5 %collective-permute-start.5 = (bf16[2,16,8,576]{3,2,1,0:T(8,128)(2,1)S(1)}, bf16[2,16,8,576]{3,2,1,0:T(8,128)(2,1)S(1)}, u32[]{:S(2)}, u32[]{:S(2)}) collective-permute-start(bf16[2,16,8,576]{3,2,1,0:T(8,128)(2,1)S(1)} %get-tuple-element.72), channel_id=1, source_target_pairs={{0,2},{2,4},{4,6},{6,0},{1,3},{3,5},{5,7},{7,1},{8,10},{10,12},{12... | collective-permute-start | bytes 884744 | tf_op jit(solution)/shard_map/ppermute | solution.py:401
  85.5 12.0 %collective-permute-start.6 = (bf16[2,16,8,576]{3,2,1,0:T(8,128)(2,1)S(1)}, bf16[2,16,8,576]{3,2,1,0:T(8,128)(2,1)S(1)}, u32[]{:S(2)}, u32[]{:S(2)}) collective-permute-start(bf16[2,16,8,576]{3,2,1,0:T(8,128)(2,1)S(1)} %get-tuple-element.73), channel_id=1, source_target_pairs={{0,6},{2,0},{4,2},{6,4},{1,7},{3,1},{5,3},{7,5},{8,14},{10,8},{12,... | collective-permute-start | bytes 884744 | tf_op jit(solution)/shard_map/ppermute | solution.py:401
  89.5 15.9 %collective-permute-start.7 = (bf16[2,16,8,576]{3,2,1,0:T(8,128)(2,1)S(1)}, bf16[2,16,8,576]{3,2,1,0:T(8,128)(2,1)S(1)}, u32[]{:S(2)}, u32[]{:S(2)}) collective-permute-start(bf16[2,16,8,576]{3,2,1,0:T(8,128)(2,1)S(1)} %get-tuple-element.74), channel_id=1, source_target_pairs={{0,4},{2,6},{4,0},{6,2},{1,5},{3,7},{5,1},{7,3},{8,12},{10,14},{12... | collective-permute-start | bytes 884744 | tf_op jit(solution)/shard_map/ppermute | solution.py:401
  105.5 8.7 %collective-permute-start.8 = (bf16[16,8,576]{2,1,0:T(8,128)(2,1)S(1)}, bf16[16,8,576]{2,1,0:T(8,128)(2,1)S(1)}, u32[]{:S(2)}, u32[]{:S(2)}) collective-permute-start(bf16[16,8,576]{2,1,0:T(8,128)(2,1)S(1)} %get-tuple-element.76), channel_id=1, source_target_pairs={{0,8},{8,0},{1,9},{9,1},{2,10},{10,2},{3,11},{11,3},{4,12},{12,4},... | collective-permute-start | bytes 442376 | tf_op jit(solution)/shard_map/ppermute | solution.py:366
  149.3 22.8 %all-to-all-start.4 = ((bf16[4,16,8,1024]{3,2,1,0:T(8,128)(2,1)}), bf16[4,16,8,1024]{3,2,1,0:T(8,128)(2,1)S(1)}, u32[]{:S(2)}, u32[]{:S(2)}) async-start(bf16[4,16,8,1024]{3,2,1,0:T(8,128)(2,1)} %broadcast_in_dim.23), calls=%async_computation.4 | async-start | bytes 2097152 | tf_op jit(solution)/shard_map/all_to_all | solution.py:362
  153.0 13.3 %collective-permute-start.9 = (bf16[128,192]{1,0:T(8,128)(2,1)S(1)}, bf16[128,192]{1,0:T(8,128)(2,1)S(1)}, u32[]{:S(2)}, u32[]{:S(2)}) collective-permute-start(bf16[128,192]{1,0:T(8,128)(2,1)S(1)} %get-tuple-element.78), channel_id=1, source_target_pairs={{0,16},{16,0},{32,48},{48,32},{1,17},{17,1},{33,49},{49,33},{2,18}... | collective-permute-start | bytes 147464 | tf_op jit(solution)/shard_map/ppermute | solution.py:372
  157.0 9.4 %collective-permute-start.10 = (bf16[128,192]{1,0:T(8,128)(2,1)S(1)}, bf16[128,192]{1,0:T(8,128)(2,1)S(1)}, u32[]{:S(2)}, u32[]{:S(2)}) collective-permute-start(bf16[128,192]{1,0:T(8,128)(2,1)S(1)} %get-tuple-element.79), channel_id=1, source_target_pairs={{0,32},{16,48},{32,0},{48,16},{1,33},{17,49},{33,1},{49,17},{2,34}... | collective-permute-start | bytes 147464 | tf_op jit(solution)/shard_map/ppermute | solution.py:372
  162.2 8.0 %collective-permute-start.11 = (bf16[128,192]{1,0:T(8,128)(2,1)S(1)}, bf16[128,192]{1,0:T(8,128)(2,1)S(1)}, u32[]{:S(2)}, u32[]{:S(2)}) collective-permute-start(bf16[128,192]{1,0:T(8,128)(2,1)S(1)} %get-tuple-element.80), channel_id=1, source_target_pairs={{0,48},{16,32},{32,16},{48,0},{1,49},{17,33},{33,17},{49,1},{2,50}... | collective-permute-start | bytes 147464 | tf_op jit(solution)/shard_map/ppermute | solution.py:372

commit v3 on v2

--- a/solution.py
+++ b/solution.py
@@ -166,7 +166,8 @@
     qn_ref,
     go_ref,
     wk_ref,
-    dw_ref,
+    keep_ref,
+    give_ref,
     *refs,
 ):
     rows_refs, (query_low, out_low, nope) = refs[:TEAM], refs[TEAM:]
@@ -179,8 +180,11 @@
 
     wk = wk_ref[:, scaled(member(place_ref, 0), D_NOPE)]
     lat_low = query_low[:, :, :D_LAT].reshape(2 * ROWS, D_LAT)
-    dw_ref[0] = dot_tn(lat_low, qn_ref[...].reshape(2 * ROWS, D_NOPE)).astype(BF16)
-    dw_ref[1] = dot_tn(out_low[...].reshape(2 * ROWS, D_LAT), go_ref[...].reshape(2 * ROWS, D_V)).astype(BF16)
+    key_weight = dot_tn(lat_low, qn_ref[...].reshape(2 * ROWS, D_NOPE))
+    value_weight = dot_tn(out_low[...].reshape(2 * ROWS, D_LAT), go_ref[...].reshape(2 * ROWS, D_V))
+    even = place_ref[3] == 0
+    keep_ref[...] = jnp.where(even, key_weight, value_weight).astype(BF16)
+    give_ref[...] = jnp.where(even, value_weight, key_weight).astype(BF16)
     nope[...] = dot_nn(lat_low, wk).astype(BF16).reshape(2, ROWS, D_NOPE)
     for ahead, rows_ref in enumerate(rows_refs):
         late = low_half(order_ref, place_ref, ahead)
@@ -227,28 +231,33 @@
             rows = side[order_ref[2 * block + upper]].reshape(2, 4, SLICE, KEY_WIDTH).astype(BF16)
             apart = (upper + place_ref[2]) % 2
             for line in range(4):
-                ahead = (line + 4 - place_ref[3]) % 4
-                g_own_ref[ahead, apart, block] = rows[0, line]
-                g_other_ref[ahead, apart, block] = rows[1, line]
-
-
-def pair_kernel(own_ref, came_ref, *out_refs):
-    for ahead, out_ref in enumerate(out_refs):
-        out_ref[...] = (own_ref[ahead].astype(F32) + came_ref[ahead].astype(F32)).astype(BF16)
-
-
-def line_kernel(a_ref, b_ref, c_ref, d_ref, keep_ref, give_ref):
+                g_own_ref[line, apart, block] = rows[0, line]
+                g_other_ref[line, apart, block] = rows[1, line]
+
+
+def pair_kernel(own_ref, came_ref, out_ref):
+    total = own_ref[...].astype(F32) + came_ref[...].astype(F32)
+    out_ref[...] = total.astype(BF16)
+
+
+def line_kernel(lines_ref, keep_ref, give_ref):
     for apart, out_ref in enumerate((keep_ref, give_ref)):
-        total = a_ref[apart].astype(F32) + b_ref[apart].astype(F32)
-        total += c_ref[apart].astype(F32) + d_ref[apart].astype(F32)
+        total = lines_ref[0, apart].astype(F32)
+        for source in range(1, 4):
+            total += lines_ref[source, apart].astype(F32)
         out_ref[...] = total.astype(BF16)
+
+
+def weight_kernel(keep_ref, came_ref, out_ref):
+    total = keep_ref[...].astype(F32) + came_ref[...].astype(F32)
+    out_ref[...] = total.astype(BF16).reshape(out_ref.shape)
 
 
 def pack_kernel(columns_ref, keep_ref, came_ref, out_ref):
     pieces = []
     for head in range(TEAM):
         total = columns_ref[head].astype(F32)
-        for source in range(head + TEAM, 2 * N_CTX, TEAM):
+        for source in range(head + TEAM, N_CTX, TEAM):
             total += columns_ref[source].astype(F32)
         pieces.append(total)
     for target in range(N_CTX):
@@ -326,7 +335,7 @@
         "query_side",
         2,
         (order, place, keys, prob, score_grad, qn, go, wk),
-        ((2, D_LAT, D_NOPE),) + (rows,) * TEAM,
+        ((D_LAT, D_NOPE), (D_LAT, D_NOPE)) + (rows,) * TEAM,
         [pltpu.VMEM(QUERY_SHAPE, BF16), pltpu.VMEM(GRAD_SHAPE, BF16), pltpu.VMEM(HEAD_SHAPE, BF16)],
         2**31,
         2**23,
@@ -375,7 +384,7 @@
 
 def local(latent, q_nope, q_rope, grad_out, w_uk, w_uv, stretch_order):
     head = lax.axis_index(PLANE + ("c",))
-    places = (Z_AXES, "c", "yh", "x")
+    places = (Z_AXES, "c", "yh", "dp")
     place = jnp.stack([lax.axis_index(axis) for axis in places]).astype(jnp.int32)
 
     mine = lax.dynamic_slice_in_dim(latent[0], head * SLICE, SLICE, 0)
@@ -391,22 +400,21 @@
     g_own, g_other = side_sums(stretch_order, place, query, grad, prob, score_grad)
     came = flip(g_other, "c")
     prob, g_own = lax.optimization_barrier((prob, g_own))
-    dw, *rows = query_side(stretch_order, place, keys, prob, score_grad, qn, go, w_uk)
-
-    half = (2, N_CTX, SLICE, KEY_WIDTH)
-    parts = call(pair_kernel, "pair_sum", 0, (g_own, came), (half,) * 4)
-    dw, *parts = lax.optimization_barrier((dw, *parts))
-    lines = [parts[0]]
-    for ahead in (1, 3, 2):
-        lines.append(lax.ppermute(parts[ahead], "x", [(i, (i + ahead) % 4) for i in range(4)]))
-
-    columns = swap(dw.reshape(2 * N_CTX, 32, D_NOPE), ("dp", *Z_AXES))
-
-    keep, give = call(line_kernel, "line_sum", 0, lines, (half[1:],) * 2)
+    keep, give, *rows = query_side(stretch_order, place, keys, prob, score_grad, qn, go, w_uk)
+
+    (pair,) = call(pair_kernel, "pair_sum", 0, (g_own, came), (g_own.shape,))
+    give, pair = lax.optimization_barrier((give, pair))
+    lines = swap(pair, "x")
+    (weights,) = call(weight_kernel, "weight_sum", 0, (keep, flip(give, "dp")), ((N_CTX, 32, D_NOPE),))
+    rows = team_swap(rows)
+    lines, weights, rows = lax.optimization_barrier((lines, weights, rows))
+    keep, give = call(line_kernel, "line_sum", 0, (lines,), (pair.shape[2:],) * 2)
+    give, weights = lax.optimization_barrier((give, weights))
+    columns = swap(weights, Z_AXES)
     came = flip(give, "yh")
     (packed,) = call(pack_kernel, "pack", 0, (columns, keep, came), ((N_CTX, SLICE, 1024 + KEY_WIDTH),))
     packed = swap(packed, Z_AXES)
-    nope_grad, rope_grad = put_heads(place, team_swap(rows))
+    nope_grad, rope_grad = put_heads(place, rows)
     d_latent = jnp.sum(packed[:, :, 1024:].astype(F32), axis=0)
     whole = swap(jnp.broadcast_to(packed[:, :, :1024], (4, N_CTX, SLICE, 1024)), ("dp", "z0"))
     wide = (D_LAT, HEADS_DEV * D_NOPE)

time: 174 us -> 166 us (0.954)
  the two profiles are of different devices: /device:TPU:2 before, /device:TPU:64 now
where the time goes in v3:
time: 166 us; the launch traced here: 165 us
  blocking collectives  60 us (36%)
  starting transfers between devices  49.5 us (30%)
  waiting for transfers between devices  33.3 us (20%)
  Pallas kernels  17.1 us (10%)
  local copies, waits for them, and re-layouts  3.49 us (2%)
    all_to_all x2, blocking collectives, swap(): return lax.all_to_all(values, axes, 0, 0, tiled=True)  60 us
    all_to_all x4, starting transfers between devices, swap(): return lax.all_to_all(values, axes, 0, 0, tiled=True)  21.7 us
    ppermute x6, starting transfers between devices, team_swap(): lax.ppermute(parts[ahead], ('z1', 'z0'), [(i, i ^ ahead) for i in range(T...  18.7 us
    pallas_call x11, Pallas kernels, call(): pl.pallas_call(kernel, out_shape=shapes, in_specs=[SMEM] * n_smem + [VMEM...  17.1 us
    all_to_all x4, waiting for transfers between devices, swap(): return lax.all_to_all(values, axes, 0, 0, tiled=True)  16.6 us
    ppermute x4, starting transfers between devices, flip(): return lax.ppermute(values, axis, [(0, 1), (1, 0)])  9.14 us
    ppermute x6, waiting for transfers between devices, team_swap(): lax.ppermute(parts[ahead], ('z1', 'z0'), [(i, i ^ ahead) for i in range(T...  8.6 us
    ppermute x4, waiting for transfers between devices, flip(): return lax.ppermute(values, axis, [(0, 1), (1, 0)])  8.09 us
  transfers between devices with their start and end apart: 14, of which 10 were waited for; matrix products, arithmetic and copies ran while one was open for 0% of the time, Pallas kernels for 4%

profile of v3, /device:TPU:64, one launch (start us, length us, event | category | flops | bytes accessed | tf_op | source)
XLA Modules:
  0.0 165.1 jit_solution(3679852476963879988)
XLA Ops:
  1.8 29.4 %all_to_all.30 = bf16[16,8,576]{2,1,0:T(8,128)(2,1)S(1)} all-to-all(bf16[16,8,576]{2,1,0:T(8,128)(2,1)S(1)} %broadcast_in_dim.18), channel_id=1, replica_groups=mesh['dp'=2,'zq'=4,'z1'=2,'z0'=2,'yh'=2,'x'=4,'c'=2] {'zq','z1','z0'}, dimensions={0} | all-to-all | bytes 294912 | tf_op jit(solution)/shard_map/all_to_all | solution.py:371
  31.3 1.2 broadcast_in_dim.19
  32.5 7.1 %all-to-all-start.1 = ((bf16[8,16,8,576]{3,2,1,0:T(8,128)(2,1)}), bf16[8,16,8,576]{3,2,1,0:T(8,128)(2,1)S(1)}, u32[]{:S(2)}, u32[]{:S(2)}) async-start(bf16[8,16,8,576]{3,2,1,0:T(8,128)(2,1)} %broadcast_in_dim.19), calls=%async_computation.1 | async-start | bytes 2621440 | tf_op jit(solution)/shard_map/all_to_all | solution.py:371
  40.4 2.7 %collective-permute-start = (bf16[128,384]{1,0:T(8,128)(2,1)S(1)}, bf16[128,384]{1,0:T(8,128)(2,1)S(1)}, u32[]{:S(2)}, u32[]{:S(2)}) collective-permute-start(bf16[128,384]{1,0:T(8,128)(2,1)S(1)} %get-tuple-element.48), channel_id=1, source_target_pairs={{0,16},{16,0},{32,48},{48,32},{1,17},{17,1},{33,49},{49,33},{2,18}... | collective-permute-start | bytes 294920 | tf_op jit(solution)/shard_map/ppermute | solution.py:381
  43.2 3.1 %collective-permute-start.1 = (bf16[128,384]{1,0:T(8,128)(2,1)S(1)}, bf16[128,384]{1,0:T(8,128)(2,1)S(1)}, u32[]{:S(2)}, u32[]{:S(2)}) collective-permute-start(bf16[128,384]{1,0:T(8,128)(2,1)S(1)} %get-tuple-element.49), channel_id=1, source_target_pairs={{0,32},{16,48},{32,0},{48,16},{1,33},{17,49},{33,1},{49,17},{2,34}... | collective-permute-start | bytes 294920 | tf_op jit(solution)/shard_map/ppermute | solution.py:381
  46.2 3.4 %collective-permute-start.2 = (bf16[128,384]{1,0:T(8,128)(2,1)S(1)}, bf16[128,384]{1,0:T(8,128)(2,1)S(1)}, u32[]{:S(2)}, u32[]{:S(2)}) collective-permute-start(bf16[128,384]{1,0:T(8,128)(2,1)S(1)} %get-tuple-element.50), channel_id=1, source_target_pairs={{0,48},{16,32},{32,16},{48,0},{1,49},{17,33},{33,17},{49,1},{2,50}... | collective-permute-start | bytes 294920 | tf_op jit(solution)/shard_map/ppermute | solution.py:381
  49.7 1.3 collective-permute-done.1.refs_2_
  51.0 3.4 %collective-permute-done.2.refs_3_ = bf16[128,384]{1,0:T(8,128)(2,1)S(1)} collective-permute-done((bf16[128,384]{1,0:T(8,128)(2,1)S(1)}, bf16[128,384]{1,0:T(8,128)(2,1)S(1)}, u32[]{:S(2)}, u32[]{:S(2)}) %collective-permute-start.2) | collective-permute-done | bytes 98336 | tf_op jit(solution)/shard_map/ppermute | solution.py:381
  54.4 2.7 %all-to-all-done.1 = bf16[8,16,8,576]{3,2,1,0:T(8,128)(2,1)S(1)} async-done(((bf16[8,16,8,576]{3,2,1,0:T(8,128)(2,1)}), bf16[8,16,8,576]{3,2,1,0:T(8,128)(2,1)S(1)}, u32[]{:S(2)}, u32[]{:S(2)}) %all-to-all-start.1) | async-done | bytes 1179680 | tf_op jit(solution)/shard_map/all_to_all | solution.py:371
  57.1 1.9 %collective-permute-start.3 = (bf16[2,4,16,8,576]{4,3,2,1,0:T(8,128)(2,1)S(1)}, bf16[2,4,16,8,576]{4,3,2,1,0:T(8,128)(2,1)S(1)}, u32[]{:S(2)}, u32[]{:S(2)}) collective-permute-start(bf16[2,4,16,8,576]{4,3,2,1,0:T(8,128)(2,1)S(1)} %bitcast.12), channel_id=1, source_target_pairs={{0,1},{1,0},{2,3},{3,2},{4,5},{5,4},{6,7},{7,6},{8,9},{9,8},{10,11... | collective-permute-start | bytes 3538952 | tf_op jit(solution)/shard_map/ppermute | solution.py:375
  60.0 2.0 %collective-permute-done.3.other_ref = bf16[2,4,16,8,576]{4,3,2,1,0:T(8,128)(2,1)S(1)} collective-permute-done((bf16[2,4,16,8,576]{4,3,2,1,0:T(8,128)(2,1)S(1)}, bf16[2,4,16,8,576]{4,3,2,1,0:T(8,128)(2,1)S(1)}, u32[]{:S(2)}, u32[]{:S(2)}) %collective-permute-start.3) | collective-permute-done | bytes 1179680 | tf_op jit(solution)/shard_map/ppermute | solution.py:375
  62.0 4.0 %scores.1 = (bf16[256,3072]{1,0:T(8,128)(2,1)S(1)}, bf16[256,3072]{1,0:T(8,128)(2,1)S(1)}, bf16[32,64,576]{2,1,0:T(8,128)(2,1)S(1)}) custom-call(s32[32]{0:T(128)S(1)} %copy-done.6, s32[4]{0:T(128)S(1)} %pad_add_fusion.place_ref, bf16[2,4,16,8,576]{4,3,2,1,0:T(8,128)(2,1)S(1)} %bitcast.13, bf16[2,4,16,8,576]{4,3,2,1,0:T(8,128)(2,1)S(1)} %collective-permute-done.3.other_ref, ...), custom_call_target="tpu_custom_call" | custom-call | flops 2147483648 | bytes 8388608 | tf_op jit(solution)/shard_map/scores/pallas_call | solution.py:291
  66.0 3.1 %key_side.1 = (bf16[4,2,16,8,576]{4,3,2,1,0:T(8,128)(2,1)S(1)}, bf16[4,2,16,8,576]{4,3,2,1,0:T(8,128)(2,1)S(1)}) custom-call(s32[32]{0:T(128)S(1)} %copy-done.6, s32[4]{0:T(128)S(1)} %pad_add_fusion.place_ref, bf16[2,256,576]{2,1,0:T(8,128)(2,1)S(1)} %get-tuple-element.56.query, bf16[2,256,512]{2,1,0:T(8,128)(2,1)S(1)} %get-tuple-element.57.grad, ...), custom_call_target="tpu_custom_call" | custom-call | flops 2147483648 | bytes 8388608 | tf_op jit(solution)/shard_map/key_side/pallas_call | solution.py:291
  69.1 2.0 %collective-permute-start.4 = (bf16[4,2,16,8,576]{4,3,2,1,0:T(8,128)(2,1)S(1)}, bf16[4,2,16,8,576]{4,3,2,1,0:T(8,128)(2,1)S(1)}, u32[]{:S(2)}, u32[]{:S(2)}) collective-permute-start(bf16[4,2,16,8,576]{4,3,2,1,0:T(8,128)(2,1)S(1)} %get-tuple-element.67), channel_id=1, source_target_pairs={{0,1},{1,0},{2,3},{3,2},{4,5},{5,4},{6,7},{7,6},{8,9},{9,8},{10,11... | collective-permute-start | bytes 3538952 | tf_op jit(solution)/shard_map/ppermute | solution.py:375
  71.1 3.2 %query_side.1 = (bf16[512,128]{1,0:T(8,128)(2,1)S(1)}, bf16[512,128]{1,0:T(8,128)(2,1)S(1)}, bf16[128,192]{1,0:T(8,128)(2,1)S(1)}, bf16[128,192]{1,0:T(8,128)(2,...) custom-call(s32[32]{0:T(128)S(1)} %copy-done.6, s32[4]{0:T(128)S(1)} %pad_add_fusion.place_ref, ...), custom_call_target="tpu_custom_call" | custom-call | flops 2147483648 | bytes 8388608 | tf_op jit(solution)/shard_map/query_side/pallas_call | solution.py:291
  74.4 1.4 pair_sum.1
  75.8 3.5 %all-to-all-start.2 = ((bf16[4,2,16,8,576]{4,3,2,1,0:T(8,128)(2,1)}), bf16[4,2,16,8,576]{4,3,2,1,0:T(8,128)(2,1)S(1)}, u32[]{:S(2)}, u32[]{:S(2)}) async-start(bf16[4,2,16,8,576]{4,3,2,1,0:T(8,128)(2,1)} %pair_sum.1), calls=%async_computation.2 | async-start | bytes 2621440 | tf_op jit(solution)/shard_map/all_to_all | solution.py:371
  79.4 2.6 %collective-permute-start.5 = (bf16[512,128]{1,0:T(8,128)(2,1)S(1)}, bf16[512,128]{1,0:T(8,128)(2,1)S(1)}, u32[]{:S(2)}, u32[]{:S(2)}) collective-permute-start(bf16[512,128]{1,0:T(8,128)(2,1)S(1)} %get-tuple-element.70), channel_id=1, source_target_pairs={{0,256},{256,0},{1,257},{257,1},{2,258},{258,2},{3,259},{259,3},{4... | collective-permute-start | bytes 393224 | tf_op jit(solution)/shard_map/ppermute | solution.py:375
  82.0 4.2 %collective-permute-start.6 = (bf16[128,192]{1,0:T(8,128)(2,1)S(1)}, bf16[128,192]{1,0:T(8,128)(2,1)S(1)}, u32[]{:S(2)}, u32[]{:S(2)}) collective-permute-start(bf16[128,192]{1,0:T(8,128)(2,1)S(1)} %get-tuple-element.72), channel_id=1, source_target_pairs={{0,16},{16,0},{32,48},{48,32},{1,17},{17,1},{33,49},{49,33},{2,18}... | collective-permute-start | bytes 147464 | tf_op jit(solution)/shard_map/ppermute | solution.py:381
  86.2 2.5 %collective-permute-start.7 = (bf16[128,192]{1,0:T(8,128)(2,1)S(1)}, bf16[128,192]{1,0:T(8,128)(2,1)S(1)}, u32[]{:S(2)}, u32[]{:S(2)}) collective-permute-start(bf16[128,192]{1,0:T(8,128)(2,1)S(1)} %get-tuple-element.73), channel_id=1, source_target_pairs={{0,32},{16,48},{32,0},{48,16},{1,33},{17,49},{33,1},{49,17},{2,34}... | collective-permute-start | bytes 147464 | tf_op jit(solution)/shard_map/ppermute | solution.py:381
  88.6 2.8 %collective-permute-start.8 = (bf16[128,192]{1,0:T(8,128)(2,1)S(1)}, bf16[128,192]{1,0:T(8,128)(2,1)S(1)}, u32[]{:S(2)}, u32[]{:S(2)}) collective-permute-start(bf16[128,192]{1,0:T(8,128)(2,1)S(1)} %get-tuple-element.74), channel_id=1, source_target_pairs={{0,48},{16,32},{32,16},{48,0},{1,49},{17,33},{33,17},{49,1},{2,50}... | collective-permute-start | bytes 147464 | tf_op jit(solution)/shard_map/ppermute | solution.py:381
  93.3 2.7 %collective-permute-done.8.refs_3_ = bf16[128,192]{1,0:T(8,128)(2,1)S(1)} collective-permute-done((bf16[128,192]{1,0:T(8,128)(2,1)S(1)}, bf16[128,192]{1,0:T(8,128)(2,1)S(1)}, u32[]{:S(2)}, u32[]{:S(2)}) %collective-permute-start.8) | collective-permute-done | bytes 49184 | tf_op jit(solution)/shard_map/ppermute | solution.py:381
  96.0 2.0 %all-to-all-done.2.lines_ref = bf16[4,2,16,8,576]{4,3,2,1,0:T(8,128)(2,1)S(1)} async-done(((bf16[4,2,16,8,576]{4,3,2,1,0:T(8,128)(2,1)}), bf16[4,2,16,8,576]{4,3,2,1,0:T(8,128)(2,1)S(1)}, u32[]{:S(2)}, u32[]{:S(2)}) %all-to-all-start.2) | async-done | bytes 1179680 | tf_op jit(solution)/shard_map/all_to_all | solution.py:371
  98.2 7.6 %all-to-all-start.3 = ((bf16[16,32,128]{2,1,0:T(8,128)(2,1)}), bf16[16,32,128]{2,1,0:T(8,128)(2,1)S(1)}, u32[]{:S(2)}, u32[]{:S(2)}) async-start(bf16[16,32,128]{2,1,0:T(8,128)(2,1)} %weight_sum.1), calls=%async_computation.3 | async-start | bytes 262144 | tf_op jit(solution)/shard_map/all_to_all | solution.py:371
  105.8 2.6 %collective-permute-start.9 = (bf16[16,8,576]{2,1,0:T(8,128)(2,1)S(1)}, bf16[16,8,576]{2,1,0:T(8,128)(2,1)S(1)}, u32[]{:S(2)}, u32[]{:S(2)}) collective-permute-start(bf16[16,8,576]{2,1,0:T(8,128)(2,1)S(1)} %get-tuple-element.80), channel_id=1, source_target_pairs={{0,8},{8,0},{1,9},{9,1},{2,10},{10,2},{3,11},{11,3},{4,12},{12,4},... | collective-permute-start | bytes 442376 | tf_op jit(solution)/shard_map/ppermute | solution.py:375
  108.4 6.1 %collective-permute-done.9.came_ref = bf16[16,8,576]{2,1,0:T(8,128)(2,1)S(1)} collective-permute-done((bf16[16,8,576]{2,1,0:T(8,128)(2,1)S(1)}, bf16[16,8,576]{2,1,0:T(8,128)(2,1)S(1)}, u32[]{:S(2)}, u32[]{:S(2)}) %collective-permute-start.9) | collective-permute-done | bytes 147488 | tf_op jit(solution)/shard_map/ppermute | solution.py:375
  114.5 4.4 %all-to-all-done.3.columns_ref = bf16[16,32,128]{2,1,0:T(8,128)(2,1)S(1)} async-done(((bf16[16,32,128]{2,1,0:T(8,128)(2,1)}), bf16[16,32,128]{2,1,0:T(8,128)(2,1)S(1)}, u32[]{:S(2)}, u32[]{:S(2)}) %all-to-all-start.3) | async-done | bytes 131104 | tf_op jit(solution)/shard_map/all_to_all | solution.py:371
  119.0 30.6 %all_to_all.31 = bf16[16,8,1600]{2,1,0:T(8,128)(2,1)S(1)} all-to-all(bf16[16,8,1600]{2,1,0:T(8,128)(2,1)S(1)} %pack.1), channel_id=1, replica_groups=mesh['dp'=2,'zq'=4,'z1'=2,'z0'=2,'yh'=2,'x'=4,'c'=2] {'zq','z1','z0'}, dimensions={0} | all-to-all | bytes 819200 | tf_op jit(solution)/shard_map/all_to_all | solution.py:371
  150.7 3.5 %all-to-all-start.5 = ((bf16[4,16,8,1024]{3,2,1,0:T(8,128)(2,1)}), bf16[4,16,8,1024]{3,2,1,0:T(8,128)(2,1)S(1)}, u32[]{:S(2)}, u32[]{:S(2)}) async-start(bf16[4,16,8,1024]{3,2,1,0:T(8,128)(2,1)} %broadcast_in_dim.23), calls=%async_computation.5 | async-start | bytes 2097152 | tf_op jit(solution)/shard_map/all_to_all | solution.py:371
  154.2 1.3 put_heads.1
  156.2 7.5 %all-to-all-done.5.whole_ref = bf16[4,16,8,1024]{3,2,1,0:T(8,128)(2,1)S(1)} async-done(((bf16[4,16,8,1024]{3,2,1,0:T(8,128)(2,1)}), bf16[4,16,8,1024]{3,2,1,0:T(8,128)(2,1)S(1)}, u32[]{:S(2)}, u32[]{:S(2)}) %all-to-all-start.5) | async-done | bytes 1048608 | tf_op jit(solution)/shard_map/all_to_all | solution.py:371
  163.6 1.4 spread.1
  (31 shorter events, 6.8 us)
Async XLA Ops:
  0.6 0.9 copy-start
  32.4 7.2 %copy-start.3 = (bf16[1,128,512]{2,1,0:T(8,128)(2,1)S(1)}, bf16[1,128,512]{2,1,0:T(8,128)(2,1)}, u32[]{:S(2)}) copy-start(bf16[1,128,512]{2,1,0:T(8,128)(2,1)} %param.8) | copy-start | bytes 393220
  32.5 7.2 %copy-start.4 = (bf16[1,128,512]{2,1,0:T(8,128)(2,1)S(1)}, bf16[1,128,512]{2,1,0:T(8,128)(2,1)}, u32[]{:S(2)}) copy-start(bf16[1,128,512]{2,1,0:T(8,128)(2,1)} %param.10) | copy-start | bytes 393220
  32.5 7.2 %copy-start.5 = (bf16[1,128,256]{2,1,0:T(8,128)(2,1)S(1)}, bf16[1,128,256]{2,1,0:T(8,128)(2,1)}, u32[]{:S(2)}) copy-start(bf16[1,128,256]{2,1,0:T(8,128)(2,1)} %param.9) | copy-start | bytes 196612
  32.5 26.5 %copy-start.1 = (bf16[512,512]{1,0:T(8,128)(2,1)S(1)}, bf16[512,512]{1,0:T(8,128)(2,1)}, u32[]{:S(2)}) copy-start(bf16[512,512]{1,0:T(8,128)(2,1)} %refs_5_.1) | copy-start | bytes 1572868
  32.5 26.6 %copy-start.2 = (bf16[512,512]{1,0:T(8,128)(2,1)S(1)}, bf16[512,512]{1,0:T(8,128)(2,1)}, u32[]{:S(2)}) copy-start(bf16[512,512]{1,0:T(8,128)(2,1)} %wk_ref.1) | copy-start | bytes 1572868
  32.5 26.5 %copy-start.6 = (s32[32]{0:T(128)S(1)}, s32[32]{0:T(128)}, u32[]{:S(2)}) copy-start(s32[32]{0:T(128)} %order_ref.7) | copy-start | bytes 388
  32.5 24.6 %all-to-all-start.1 = ((bf16[8,16,8,576]{3,2,1,0:T(8,128)(2,1)}), bf16[8,16,8,576]{3,2,1,0:T(8,128)(2,1)S(1)}, u32[]{:S(2)}, u32[]{:S(2)}) async-start(bf16[8,16,8,576]{3,2,1,0:T(8,128)(2,1)} %broadcast_in_dim.19), calls=%async_computation.1 | async-start | bytes 2621440 | tf_op jit(solution)/shard_map/all_to_all | solution.py:371
  40.4 9.2 %collective-permute-start = (bf16[128,384]{1,0:T(8,128)(2,1)S(1)}, bf16[128,384]{1,0:T(8,128)(2,1)S(1)}, u32[]{:S(2)}, u32[]{:S(2)}) collective-permute-start(bf16[128,384]{1,0:T(8,128)(2,1)S(1)} %get-tuple-element.48), channel_id=1, source_target_pairs={{0,16},{16,0},{32,48},{48,32},{1,17},{17,1},{33,49},{49,33},{2,18}... | collective-permute-start | bytes 294920 | tf_op jit(solution)/shard_map/ppermute | solution.py:381
  43.2 7.8 %collective-permute-start.1 = (bf16[128,384]{1,0:T(8,128)(2,1)S(1)}, bf16[128,384]{1,0:T(8,128)(2,1)S(1)}, u32[]{:S(2)}, u32[]{:S(2)}) collective-permute-start(bf16[128,384]{1,0:T(8,128)(2,1)S(1)} %get-tuple-element.49), channel_id=1, source_target_pairs={{0,32},{16,48},{32,0},{48,16},{1,33},{17,49},{33,1},{49,17},{2,34}... | collective-permute-start | bytes 294920 | tf_op jit(solution)/shard_map/ppermute | solution.py:381
  46.2 8.2 %collective-permute-start.2 = (bf16[128,384]{1,0:T(8,128)(2,1)S(1)}, bf16[128,384]{1,0:T(8,128)(2,1)S(1)}, u32[]{:S(2)}, u32[]{:S(2)}) collective-permute-start(bf16[128,384]{1,0:T(8,128)(2,1)S(1)} %get-tuple-element.50), channel_id=1, source_target_pairs={{0,48},{16,32},{32,16},{48,0},{1,49},{17,33},{33,17},{49,1},{2,50}... | collective-permute-start | bytes 294920 | tf_op jit(solution)/shard_map/ppermute | solution.py:381
  57.1 4.9 %collective-permute-start.3 = (bf16[2,4,16,8,576]{4,3,2,1,0:T(8,128)(2,1)S(1)}, bf16[2,4,16,8,576]{4,3,2,1,0:T(8,128)(2,1)S(1)}, u32[]{:S(2)}, u32[]{:S(2)}) collective-permute-start(bf16[2,4,16,8,576]{4,3,2,1,0:T(8,128)(2,1)S(1)} %bitcast.12), channel_id=1, source_target_pairs={{0,1},{1,0},{2,3},{3,2},{4,5},{5,4},{6,7},{7,6},{8,9},{9,8},{10,11... | collective-permute-start | bytes 3538952 | tf_op jit(solution)/shard_map/ppermute | solution.py:375
  69.1 5.3 %collective-permute-start.4 = (bf16[4,2,16,8,576]{4,3,2,1,0:T(8,128)(2,1)S(1)}, bf16[4,2,16,8,576]{4,3,2,1,0:T(8,128)(2,1)S(1)}, u32[]{:S(2)}, u32[]{:S(2)}) collective-permute-start(bf16[4,2,16,8,576]{4,3,2,1,0:T(8,128)(2,1)S(1)} %get-tuple-element.67), channel_id=1, source_target_pairs={{0,1},{1,0},{2,3},{3,2},{4,5},{5,4},{6,7},{7,6},{8,9},{9,8},{10,11... | collective-permute-start | bytes 3538952 | tf_op jit(solution)/shard_map/ppermute | solution.py:375
  75.8 22.2 %all-to-all-start.2 = ((bf16[4,2,16,8,576]{4,3,2,1,0:T(8,128)(2,1)}), bf16[4,2,16,8,576]{4,3,2,1,0:T(8,128)(2,1)S(1)}, u32[]{:S(2)}, u32[]{:S(2)}) async-start(bf16[4,2,16,8,576]{4,3,2,1,0:T(8,128)(2,1)} %pair_sum.1), calls=%async_computation.2 | async-start | bytes 2621440 | tf_op jit(solution)/shard_map/all_to_all | solution.py:371
  79.4 12.1 %collective-permute-start.5 = (bf16[512,128]{1,0:T(8,128)(2,1)S(1)}, bf16[512,128]{1,0:T(8,128)(2,1)S(1)}, u32[]{:S(2)}, u32[]{:S(2)}) collective-permute-start(bf16[512,128]{1,0:T(8,128)(2,1)S(1)} %get-tuple-element.70), channel_id=1, source_target_pairs={{0,256},{256,0},{1,257},{257,1},{2,258},{258,2},{3,259},{259,3},{4... | collective-permute-start | bytes 393224 | tf_op jit(solution)/shard_map/ppermute | solution.py:375
  82.0 10.2 %collective-permute-start.6 = (bf16[128,192]{1,0:T(8,128)(2,1)S(1)}, bf16[128,192]{1,0:T(8,128)(2,1)S(1)}, u32[]{:S(2)}, u32[]{:S(2)}) collective-permute-start(bf16[128,192]{1,0:T(8,128)(2,1)S(1)} %get-tuple-element.72), channel_id=1, source_target_pairs={{0,16},{16,0},{32,48},{48,32},{1,17},{17,1},{33,49},{49,33},{2,18}... | collective-permute-start | bytes 147464 | tf_op jit(solution)/shard_map/ppermute | solution.py:381
  86.2 7.1 %collective-permute-start.7 = (bf16[128,192]{1,0:T(8,128)(2,1)S(1)}, bf16[128,192]{1,0:T(8,128)(2,1)S(1)}, u32[]{:S(2)}, u32[]{:S(2)}) collective-permute-start(bf16[128,192]{1,0:T(8,128)(2,1)S(1)} %get-tuple-element.73), channel_id=1, source_target_pairs={{0,32},{16,48},{32,0},{48,16},{1,33},{17,49},{33,1},{49,17},{2,34}... | collective-permute-start | bytes 147464 | tf_op jit(solution)/shard_map/ppermute | solution.py:381
  88.6 7.4 %collective-permute-start.8 = (bf16[128,192]{1,0:T(8,128)(2,1)S(1)}, bf16[128,192]{1,0:T(8,128)(2,1)S(1)}, u32[]{:S(2)}, u32[]{:S(2)}) collective-permute-start(bf16[128,192]{1,0:T(8,128)(2,1)S(1)} %get-tuple-element.74), channel_id=1, source_target_pairs={{0,48},{16,32},{32,16},{48,0},{1,49},{17,33},{33,17},{49,1},{2,50}... | collective-permute-start | bytes 147464 | tf_op jit(solution)/shard_map/ppermute | solution.py:381
  98.2 20.7 %all-to-all-start.3 = ((bf16[16,32,128]{2,1,0:T(8,128)(2,1)}), bf16[16,32,128]{2,1,0:T(8,128)(2,1)S(1)}, u32[]{:S(2)}, u32[]{:S(2)}) async-start(bf16[16,32,128]{2,1,0:T(8,128)(2,1)} %weight_sum.1), calls=%async_computation.3 | async-start | bytes 262144 | tf_op jit(solution)/shard_map/all_to_all | solution.py:371
  105.8 8.7 %collective-permute-start.9 = (bf16[16,8,576]{2,1,0:T(8,128)(2,1)S(1)}, bf16[16,8,576]{2,1,0:T(8,128)(2,1)S(1)}, u32[]{:S(2)}, u32[]{:S(2)}) collective-permute-start(bf16[16,8,576]{2,1,0:T(8,128)(2,1)S(1)} %get-tuple-element.80), channel_id=1, source_target_pairs={{0,8},{8,0},{1,9},{9,1},{2,10},{10,2},{3,11},{11,3},{4,12},{12,4},... | collective-permute-start | bytes 442376 | tf_op jit(solution)/shard_map/ppermute | solution.py:375
  150.7 12.9 %all-to-all-start.5 = ((bf16[4,16,8,1024]{3,2,1,0:T(8,128)(2,1)}), bf16[4,16,8,1024]{3,2,1,0:T(8,128)(2,1)S(1)}, u32[]{:S(2)}, u32[]{:S(2)}) async-start(bf16[4,16,8,1024]{3,2,1,0:T(8,128)(2,1)} %broadcast_in_dim.23), calls=%async_computation.5 | async-start | bytes 2097152 | tf_op jit(solution)/shard_map/all_to_all | solution.py:371

commit v4 on v3

--- a/solution.py
+++ b/solution.py
@@ -21,10 +21,13 @@
 TEAM = 4
 ROWS = TEAM * STRETCH
 CHUNK = 256
-PER_CHUNK = CHUNK // STRETCH
+HALF = STRETCH // 2
+PER_CHUNK = CHUNK // HALF
 CHUNKS = N_SLOT // PER_CHUNK
 LOW_CHUNKS = CHUNKS // 2
 STEPS = CHUNKS + LOW_CHUNKS
+PAIRS = N_CTX // 2
+WIDE = 2 * KEY_WIDTH
 SENT = D_NOPE + D_V + 128
 SLICE = 8
 NEG = -1e30
@@ -59,6 +62,14 @@
 def low_half(order_ref, place_ref, ahead):
     block = place_ref[0] ^ ahead
     return jnp.where(order_ref[2 * block] > order_ref[2 * block + 1], 1, 0)
+
+
+def lat_lanes(parity):
+    return slice(parity * D_LAT, (parity + 1) * D_LAT)
+
+
+def rope_lanes(parity):
+    return slice(2 * D_LAT + parity * D_ROPE, 2 * D_LAT + (parity + 1) * D_ROPE)
 
 
 def split_kernel(place_ref, qn_ref, qr_ref, go_ref, *out_refs):
@@ -93,31 +104,29 @@
             go[group, into, :] = out[toks]
 
 
-def score_kernel(
-    order_ref,
-    place_ref,
-    own_ref,
-    other_ref,
-    query,
-    grad,
-    prob_ref,
-    score_grad_ref,
-    keys,
-    score,
-    prob_grad,
-):
-    @pl.loop(0, N_CTX, unroll=4)
-    def _(block):
+def step_lanes(group, chunk):
+    step = chunk if group == 0 else LOW_CHUNKS + chunk
+    return slice(step * CHUNK, (step + 1) * CHUNK)
+
+
+def group_chunks(group):
+    return LOW_CHUNKS if group == 0 else CHUNKS
+
+
+def half_scores(order_ref, place_ref, half, rows_ref, query, grad, keys, score, prob_grad):
+    @pl.loop(0, PAIRS, unroll=4)
+    def _(pair):
         for upper in range(2):
-            rows = jnp.concatenate(
-                [own_ref[upper, :, block].astype(F32), other_ref[upper, :, block].astype(F32)], axis=0
-            )
-            keys[order_ref[2 * block + upper]] = rows.reshape(STRETCH, KEY_WIDTH).astype(BF16)
+            rows = rows_ref[upper, :, pair].astype(F32).reshape(HALF, WIDE).astype(BF16)
+            for parity in range(2):
+                place = order_ref[4 * pair + 2 * parity + upper]
+                keys[place, :, :D_LAT] = rows[:, lat_lanes(parity)]
+                keys[place, :, D_LAT:] = rows[:, rope_lanes(parity)]
 
     col = lax.broadcasted_iota(jnp.int32, (1, CHUNK), 1)
-    within = col % STRETCH
-    side_of = (within // 32 + place_ref[1]) % 2
-    key_pos = (col // STRETCH) * STRETCH + ((within % 32) // SLICE) * 16 + side_of * SLICE + within % SLICE
+    within = col % HALF
+    core = (place_ref[1] + half) % 2
+    key_pos = (col // HALF) * STRETCH + (within // SLICE) * 16 + core * SLICE + within % SLICE
 
     row = lax.broadcasted_iota(jnp.int32, (ROWS, 1), 0)
     row_pos = [row % STRETCH, row % STRETCH]
@@ -128,39 +137,73 @@
         row_pos[0] += jnp.where(mine, jnp.minimum(first, second) * STRETCH, 0)
         row_pos[1] += jnp.where(mine, jnp.maximum(first, second) * STRETCH, 0)
 
+    tops = []
     for group in range(2):
-        first_step, chunks = (0, LOW_CHUNKS) if group == 0 else (LOW_CHUNKS, CHUNKS)
         top = jnp.full((ROWS, 1), NEG, F32)
-        for chunk in range(chunks):
-            cols = slice((first_step + chunk) * CHUNK, (first_step + chunk + 1) * CHUNK)
+        for chunk in range(group_chunks(group)):
+            lanes = step_lanes(group, chunk)
             key_rows = keys[chunk * PER_CHUNK : (chunk + 1) * PER_CHUNK].reshape(CHUNK, KEY_WIDTH)
             raw = dot_nt(query[group], key_rows) * (SCALE * LOG2E)
             if group == 0 or chunk >= LOW_CHUNKS:
-                raw = jnp.where(key_pos + chunk * CHUNK <= row_pos[group], raw, NEG)
-            score[:, cols] = raw
-            prob_grad[:, cols] = dot_nt(grad[group], key_rows[:, :D_LAT])
+                raw = jnp.where(key_pos + chunk * PER_CHUNK * STRETCH <= row_pos[group], raw, NEG)
+            score[:, lanes] = raw
+            prob_grad[:, lanes] = dot_nt(grad[group], key_rows[:, :D_LAT])
             top = jnp.maximum(top, jnp.max(raw, axis=1, keepdims=True))
+        tops.append(top)
+    return tops
+
+
+def own_kernel(order_ref, place_ref, own_ref, query, grad, keys, score, prob_grad, top_ref):
+    tops = half_scores(order_ref, place_ref, 0, own_ref, query, grad, keys, score, prob_grad)
+    for group in range(2):
+        top_ref[group] = jnp.broadcast_to(tops[group], (ROWS, 128))
+
+
+def score_kernel(
+    order_ref,
+    place_ref,
+    other_ref,
+    query,
+    grad,
+    own_score,
+    own_prob_grad,
+    top_ref,
+    keys,
+    prob_ref,
+    score_grad_ref,
+    score,
+    prob_grad,
+    expo_ref,
+):
+    tops = half_scores(order_ref, place_ref, 1, other_ref, query, grad, keys, score, prob_grad)
+    halves = ((own_score, own_prob_grad), (score, prob_grad))
+    for group in range(2):
+        top = jnp.maximum(tops[group], top_ref[group, :, :1])
         total = jnp.zeros((ROWS, 1), F32)
         weight = jnp.zeros((ROWS, 1), F32)
-        for chunk in range(chunks):
-            cols = slice((first_step + chunk) * CHUNK, (first_step + chunk + 1) * CHUNK)
-            expo = jnp.exp2(score[:, cols] - top)
-            score[:, cols] = expo
-            total += jnp.sum(expo, axis=1, keepdims=True)
-            weight += jnp.sum(expo * prob_grad[:, cols], axis=1, keepdims=True)
+        for half, (raw_ref, grad_ref) in enumerate(halves):
+            for chunk in range(group_chunks(group)):
+                lanes = step_lanes(group, chunk)
+                expo = jnp.exp2(raw_ref[:, lanes] - top)
+                expo_ref[half, :, lanes] = expo
+                total += jnp.sum(expo, axis=1, keepdims=True)
+                weight += jnp.sum(expo * grad_ref[:, lanes], axis=1, keepdims=True)
         inverse = 1.0 / total
         delta = weight * inverse
-        for chunk in range(chunks):
-            cols = slice((first_step + chunk) * CHUNK, (first_step + chunk + 1) * CHUNK)
-            probability = score[:, cols] * inverse
-            prob_ref[:, cols] = probability.astype(BF16)
-            score_grad_ref[:, cols] = (SCALE * probability * (prob_grad[:, cols] - delta)).astype(BF16)
+        for half, (raw_ref, grad_ref) in enumerate(halves):
+            for chunk in range(group_chunks(group)):
+                lanes = step_lanes(group, chunk)
+                probability = expo_ref[half, :, lanes] * inverse
+                prob_ref[half, :, lanes] = probability.astype(BF16)
+                drift = grad_ref[:, lanes] - delta
+                score_grad_ref[half, :, lanes] = (SCALE * probability * drift).astype(BF16)
 
 
 def query_kernel(
     order_ref,
     place_ref,
-    keys,
+    own_keys,
+    other_keys,
     prob_ref,
     score_grad_ref,
     qn_ref,
@@ -172,11 +215,15 @@
 ):
     rows_refs, (query_low, out_low, nope) = refs[:TEAM], refs[TEAM:]
     for group in range(2):
-        cols = slice(0, LOW_CHUNKS * CHUNK) if group == 0 else slice(LOW_CHUNKS * CHUNK, STEPS * CHUNK)
-        count = N_SLOT // 2 if group == 0 else N_SLOT
-        key_rows = keys[:count].reshape(count * STRETCH, KEY_WIDTH)
-        out_low[group] = dot_nn(prob_ref[:, cols], key_rows[:, :D_LAT]).astype(BF16)
-        query_low[group] = dot_nn(score_grad_ref[:, cols], key_rows).astype(BF16)
+        lanes = slice(0, LOW_CHUNKS * CHUNK) if group == 0 else slice(LOW_CHUNKS * CHUNK, STEPS * CHUNK)
+        count = group_chunks(group) * PER_CHUNK
+        out, query_grad = [], []
+        for half, keys in enumerate((own_keys, other_keys)):
+            key_rows = keys[:count].reshape(count * HALF, KEY_WIDTH)
+            out.append(dot_nn(prob_ref[half, :, lanes], key_rows[:, :D_LAT]))
+            query_grad.append(dot_nn(score_grad_ref[half, :, lanes], key_rows))
+        out_low[group] = (out[0] + out[1]).astype(BF16)
+        query_low[group] = (query_grad[0] + query_grad[1]).astype(BF16)
 
     wk = wk_ref[:, scaled(member(place_ref, 0), D_NOPE)]
     lat_low = query_low[:, :, :D_LAT].reshape(2 * ROWS, D_LAT)
@@ -210,29 +257,33 @@
 ):
     both_query = query[...].reshape(2 * ROWS, KEY_WIDTH)
     both_grad = grad[...].reshape(2 * ROWS, D_LAT)
-    for chunk in range(CHUNKS):
-        late = slice((LOW_CHUNKS + chunk) * CHUNK, (LOW_CHUNKS + chunk + 1) * CHUNK)
-        early = slice(chunk * CHUNK, (chunk + 1) * CHUNK)
-        where = slice(chunk * PER_CHUNK, (chunk + 1) * PER_CHUNK)
-        if chunk < LOW_CHUNKS:
-            score_grad = jnp.concatenate([score_grad_ref[:, early], score_grad_ref[:, late]], axis=0)
-            prob = jnp.concatenate([prob_ref[:, early], prob_ref[:, late]], axis=0)
-            key_side, value_side = dot_tn(score_grad, both_query), dot_tn(prob, both_grad)
-        else:
-            key_side = dot_tn(score_grad_ref[:, late], query[1])
-            value_side = dot_tn(prob_ref[:, late], grad[1])
-        lat = key_side[:, :D_LAT] + value_side
-        side[where, :, :D_LAT] = lat.reshape(PER_CHUNK, STRETCH, D_LAT)
-        side[where, :, D_LAT:] = key_side[:, D_LAT:].reshape(PER_CHUNK, STRETCH, D_ROPE)
-
-    @pl.loop(0, N_CTX, unroll=4)
-    def _(block):
+    for half in range(2):
+        for chunk in range(CHUNKS):
+            late, where = step_lanes(1, chunk), slice(chunk * PER_CHUNK, (chunk + 1) * PER_CHUNK)
+            if chunk < LOW_CHUNKS:
+                early = step_lanes(0, chunk)
+                score_grad, prob = [
+                    jnp.concatenate([ref[half, :, early], ref[half, :, late]], axis=0)
+                    for ref in (score_grad_ref, prob_ref)
+                ]
+                key_side, value_side = dot_tn(score_grad, both_query), dot_tn(prob, both_grad)
+            else:
+                key_side = dot_tn(score_grad_ref[half, :, late], query[1])
+                value_side = dot_tn(prob_ref[half, :, late], grad[1])
+            lat = key_side[:, :D_LAT] + value_side
+            side[half, where, :, :D_LAT] = lat.reshape(PER_CHUNK, HALF, D_LAT)
+            side[half, where, :, D_LAT:] = key_side[:, D_LAT:].reshape(PER_CHUNK, HALF, D_ROPE)
+
+    @pl.loop(0, PAIRS, unroll=4)
+    def _(pair):
         for upper in range(2):
-            rows = side[order_ref[2 * block + upper]].reshape(2, 4, SLICE, KEY_WIDTH).astype(BF16)
             apart = (upper + place_ref[2]) % 2
-            for line in range(4):
-                g_own_ref[line, apart, block] = rows[0, line]
-                g_other_ref[line, apart, block] = rows[1, line]
+            for half, out_ref in enumerate((g_own_ref, g_other_ref)):
+                both = [side[half, order_ref[4 * pair + 2 * parity + upper]] for parity in range(2)]
+                rows = jnp.concatenate(
+                    [both[0][:, :D_LAT], both[1][:, :D_LAT], both[0][:, D_LAT:], both[1][:, D_LAT:]], axis=1
+                )
+                out_ref[:, apart, pair] = rows.reshape(4, SLICE, WIDE).astype(BF16)
 
 
 def pair_kernel(own_ref, came_ref, out_ref):
@@ -266,8 +317,11 @@
             for octet in range(4):
                 lanes = slice((4 * pick + octet) * 128, (4 * pick + octet + 1) * 128)
                 out_ref[target, :, lanes] = piece[octet * SLICE : (octet + 1) * SLICE].astype(BF16)
-    side = keep_ref[...].astype(F32) + came_ref[...].astype(F32)
-    out_ref[:, :, 1024:] = side.astype(BF16)
+    side = (keep_ref[...].astype(F32) + came_ref[...].astype(F32)).astype(BF16)
+    for pair in range(PAIRS):
+        for parity in range(2):
+            out_ref[2 * pair + parity, :, 1024 : 1024 + D_LAT] = side[pair, :, lat_lanes(parity)]
+            out_ref[2 * pair + parity, :, 1024 + D_LAT :] = side[pair, :, rope_lanes(parity)]
 
 
 def spread_kernel(whole_ref, key_ref, value_ref):
@@ -287,7 +341,8 @@
 
 
 def call(kernel, name, n_smem, args, outs, scratch=(), flops=2**20, moved=2**20, dtype=BF16):
-    shapes = tuple(jax.ShapeDtypeStruct(shape, dtype) for shape in outs)
+    types = dtype if isinstance(dtype, tuple) else (dtype,) * len(outs)
+    shapes = tuple(jax.ShapeDtypeStruct(shape, kind) for shape, kind in zip(outs, types))
     return pl.pallas_call(
         kernel,
         out_shape=shapes,
@@ -304,6 +359,7 @@
 GRAD_SHAPE = (2, ROWS, D_LAT)
 HEAD_SHAPE = (2, ROWS, D_NOPE)
 STEP_SHAPE = (ROWS, STEPS * CHUNK)
+KEY_SHAPE = (N_SLOT, HALF, KEY_WIDTH)
 
 
 def split(place, qn, qr, go):
@@ -315,26 +371,26 @@
     return call(prepare_kernel, "query_latents", 2, (order, place, *rows, wk, wv), outs, (), 2**28, 2**21)
 
 
-def scores(order, place, own, other, query, grad):
-    return call(
-        score_kernel,
-        "scores",
-        2,
-        (order, place, own, other, query, grad),
-        (STEP_SHAPE, STEP_SHAPE, (N_SLOT, STRETCH, KEY_WIDTH)),
-        [pltpu.VMEM(STEP_SHAPE, F32), pltpu.VMEM(STEP_SHAPE, F32)],
-        2**31,
-        2**23,
-    )
-
-
-def query_side(order, place, keys, prob, score_grad, qn, go, wk):
+def own_scores(order, place, own, query, grad):
+    args = (order, place, own, query, grad)
+    outs = (KEY_SHAPE, STEP_SHAPE, STEP_SHAPE, (2, ROWS, 128))
+    return call(own_kernel, "own_scores", 2, args, outs, (), 2**30, 2**22, (BF16, F32, F32, F32))
+
+
+def scores(order, place, other, query, grad, own):
+    args = (order, place, other, query, grad, *own)
+    outs = (KEY_SHAPE, (2, *STEP_SHAPE), (2, *STEP_SHAPE))
+    scratch = [pltpu.VMEM(STEP_SHAPE, F32), pltpu.VMEM(STEP_SHAPE, F32), pltpu.VMEM((2, *STEP_SHAPE), F32)]
+    return call(score_kernel, "scores", 2, args, outs, scratch, 2**31, 2**23)
+
+
+def query_side(order, place, own_keys, keys, prob, score_grad, qn, go, wk):
     rows = (TOK_DEV, D_NOPE + D_ROPE)
     return call(
         query_kernel,
         "query_side",
         2,
-        (order, place, keys, prob, score_grad, qn, go, wk),
+        (order, place, own_keys, keys, prob, score_grad, qn, go, wk),
         ((D_LAT, D_NOPE), (D_LAT, D_NOPE)) + (rows,) * TEAM,
         [pltpu.VMEM(QUERY_SHAPE, BF16), pltpu.VMEM(GRAD_SHAPE, BF16), pltpu.VMEM(HEAD_SHAPE, BF16)],
         2**31,
@@ -354,14 +410,14 @@
 
 
 def side_sums(order, place, query, grad, prob, score_grad):
-    part = (4, 2, N_CTX, SLICE, KEY_WIDTH)
+    part = (4, 2, PAIRS, SLICE, WIDE)
     return call(
         side_kernel,
         "key_side",
         2,
         (order, place, query, grad, prob, score_grad),
         (part, part),
-        [pltpu.VMEM((N_SLOT, STRETCH, KEY_WIDTH), F32)],
+        [pltpu.VMEM((2, *KEY_SHAPE), F32)],
         2**31,
         2**23,
     )
@@ -389,18 +445,24 @@
 
     mine = lax.dynamic_slice_in_dim(latent[0], head * SLICE, SLICE, 0)
     column = swap(jnp.broadcast_to(mine, (N_CTX, SLICE, KEY_WIDTH)), Z_AXES)
-    own = swap(jnp.broadcast_to(column, (8, N_CTX, SLICE, KEY_WIDTH)), PLANE)
+    wide = (PAIRS, SLICE, WIDE)
+    first, second = column.reshape(PAIRS, 2, SLICE, KEY_WIDTH).transpose(1, 0, 2, 3)
+    column = jnp.concatenate(
+        [first[..., :D_LAT], second[..., :D_LAT], first[..., D_LAT:], second[..., D_LAT:]], axis=-1
+    )
+    own = swap(jnp.broadcast_to(column, (8, *wide)), PLANE)
     rows = team_swap(split(place, q_nope[0], q_rope[0], grad_out[0]))
     own, *rows = lax.optimization_barrier((own, *rows))
     query, grad, qn, go = prepare(stretch_order, place, rows, w_uk, w_uv)
-    own = own.reshape(2, 4, N_CTX, SLICE, KEY_WIDTH)
+    own = own.reshape(2, 4, *wide)
     other = flip(own, "c")
 
-    prob, score_grad, keys = scores(stretch_order, place, own, other, query, grad)
+    own_keys, *own = own_scores(stretch_order, place, own, query, grad)
+    keys, prob, score_grad = scores(stretch_order, place, other, query, grad, own)
     g_own, g_other = side_sums(stretch_order, place, query, grad, prob, score_grad)
     came = flip(g_other, "c")
     prob, g_own = lax.optimization_barrier((prob, g_own))
-    keep, give, *rows = query_side(stretch_order, place, keys, prob, score_grad, qn, go, w_uk)
+    keep, give, *rows = query_side(stretch_order, place, own_keys, keys, prob, score_grad, qn, go, w_uk)
 
     (pair,) = call(pair_kernel, "pair_sum", 0, (g_own, came), (g_own.shape,))
     give, pair = lax.optimization_barrier((give, pair))

time: 166 us -> 162 us (0.976)
  waiting for transfers between devices: 33.3 us -> 26.6 us
    ppermute x4, waiting for transfers between devices: 8.09 us -> 4.75 us  [flip(): return lax.ppermute(values, axis, [(0, 1), (1, 0)])]
    all_to_all x4, waiting for transfers between devices: 16.6 us -> 14 us  [swap(): return lax.all_to_all(values, axes, 0, 0, tiled=True)]
    pallas_call x11 -> x12, Pallas kernels: 17.1 us -> 18.3 us  [call(): pl.pallas_call(kernel, out_shape=shapes, in_specs=[SMEM] * n_smem + [VMEM...]
  transfers between devices with their start and end apart: 14 -> 14, of which waited for: 10 -> 9; matrix products, arithmetic and copies ran while one was open for 0% -> 0% of each run, Pallas kernels for 4% -> 6%
where the time goes in v4:
time: 162 us; the launch traced here: 161 us
  blocking collectives  60.1 us (37%)
  starting transfers between devices  51 us (31%)
  waiting for transfers between devices  26.6 us (16%)
  Pallas kernels  18.3 us (11%)
  local copies, waits for them, and re-layouts  3.58 us (2%)
    all_to_all x2, blocking collectives, swap(): return lax.all_to_all(values, axes, 0, 0, tiled=True)  60.1 us
    all_to_all x4, starting transfers between devices, swap(): return lax.all_to_all(values, axes, 0, 0, tiled=True)  21.7 us
    ppermute x6, starting transfers between devices, team_swap(): lax.ppermute(parts[ahead], ('z1', 'z0'), [(i, i ^ ahead) for i in range(T...  18.6 us
    pallas_call x12, Pallas kernels, call(): pl.pallas_call(kernel, out_shape=shapes, in_specs=[SMEM] * n_smem + [VMEM...  18.3 us
    all_to_all x4, waiting for transfers between devices, swap(): return lax.all_to_all(values, axes, 0, 0, tiled=True)  14 us
    ppermute x4, starting transfers between devices, flip(): return lax.ppermute(values, axis, [(0, 1), (1, 0)])  10.7 us
    ppermute x6, waiting for transfers between devices, team_swap(): lax.ppermute(parts[ahead], ('z1', 'z0'), [(i, i ^ ahead) for i in range(T...  7.78 us
    ppermute x4, waiting for transfers between devices, flip(): return lax.ppermute(values, axis, [(0, 1), (1, 0)])  4.75 us
  transfers between devices with their start and end apart: 14, of which 9 were waited for; matrix products, arithmetic and copies ran while one was open for 0% of the time, Pallas kernels for 6%

profile of v4, /device:TPU:64, one launch (start us, length us, event | category | flops | bytes accessed | tf_op | source)
XLA Modules:
  0.0 161.2 jit_solution(10043874449772308101)
XLA Ops:
  1.8 29.4 %all_to_all.30 = bf16[16,8,576]{2,1,0:T(8,128)(2,1)S(1)} all-to-all(bf16[16,8,576]{2,1,0:T(8,128)(2,1)S(1)} %broadcast_in_dim.18), channel_id=1, replica_groups=mesh['dp'=2,'zq'=4,'z1'=2,'z0'=2,'yh'=2,'x'=4,'c'=2] {'zq','z1','z0'}, dimensions={0} | all-to-all | bytes 294912 | tf_op jit(solution)/shard_map/all_to_all | solution.py:427
  31.4 1.2 broadcast_in_dim.19
  32.6 7.1 %all-to-all-start.1 = ((bf16[8,8,8,1152]{3,2,1,0:T(8,128)(2,1)}), bf16[8,8,8,1152]{3,2,1,0:T(8,128)(2,1)S(1)}, u32[]{:S(2)}, u32[]{:S(2)}) async-start(bf16[8,8,8,1152]{3,2,1,0:T(8,128)(2,1)} %broadcast_in_dim.19), calls=%async_computation.1 | async-start | bytes 2359296 | tf_op jit(solution)/shard_map/all_to_all | solution.py:427
  40.6 2.7 %collective-permute-start = (bf16[128,384]{1,0:T(8,128)(2,1)S(1)}, bf16[128,384]{1,0:T(8,128)(2,1)S(1)}, u32[]{:S(2)}, u32[]{:S(2)}) collective-permute-start(bf16[128,384]{1,0:T(8,128)(2,1)S(1)} %get-tuple-element.52), channel_id=1, source_target_pairs={{0,16},{16,0},{32,48},{48,32},{1,17},{17,1},{33,49},{49,33},{2,18}... | collective-permute-start | bytes 294920 | tf_op jit(solution)/shard_map/ppermute | solution.py:437
  43.3 3.1 %collective-permute-start.1 = (bf16[128,384]{1,0:T(8,128)(2,1)S(1)}, bf16[128,384]{1,0:T(8,128)(2,1)S(1)}, u32[]{:S(2)}, u32[]{:S(2)}) collective-permute-start(bf16[128,384]{1,0:T(8,128)(2,1)S(1)} %get-tuple-element.53), channel_id=1, source_target_pairs={{0,32},{16,48},{32,0},{48,16},{1,33},{17,49},{33,1},{49,17},{2,34}... | collective-permute-start | bytes 294920 | tf_op jit(solution)/shard_map/ppermute | solution.py:437
  46.4 3.4 %collective-permute-start.2 = (bf16[128,384]{1,0:T(8,128)(2,1)S(1)}, bf16[128,384]{1,0:T(8,128)(2,1)S(1)}, u32[]{:S(2)}, u32[]{:S(2)}) collective-permute-start(bf16[128,384]{1,0:T(8,128)(2,1)S(1)} %get-tuple-element.54), channel_id=1, source_target_pairs={{0,48},{16,32},{32,16},{48,0},{1,49},{17,33},{33,17},{49,1},{2,50}... | collective-permute-start | bytes 294920 | tf_op jit(solution)/shard_map/ppermute | solution.py:437
  49.8 1.3 collective-permute-done.1.refs_2_
  51.1 3.4 %collective-permute-done.2.refs_3_ = bf16[128,384]{1,0:T(8,128)(2,1)S(1)} collective-permute-done((bf16[128,384]{1,0:T(8,128)(2,1)S(1)}, bf16[128,384]{1,0:T(8,128)(2,1)S(1)}, u32[]{:S(2)}, u32[]{:S(2)}) %collective-permute-start.2) | collective-permute-done | bytes 98336 | tf_op jit(solution)/shard_map/ppermute | solution.py:437
  54.5 1.4 all-to-all-done.1
  56.0 1.9 %collective-permute-start.3 = (bf16[2,4,8,8,1152]{4,3,2,1,0:T(8,128)(2,1)S(1)}, bf16[2,4,8,8,1152]{4,3,2,1,0:T(8,128)(2,1)S(1)}, u32[]{:S(2)}, u32[]{:S(2)}) collective-permute-start(bf16[2,4,8,8,1152]{4,3,2,1,0:T(8,128)(2,1)S(1)} %bitcast.21), channel_id=1, source_target_pairs={{0,1},{1,0},{2,3},{3,2},{4,5},{5,4},{6,7},{7,6},{8,9},{9,8},{10,11... | collective-permute-start | bytes 3538952 | tf_op jit(solution)/shard_map/ppermute | solution.py:431
  58.9 2.1 %own_scores.1 = (bf16[32,32,576]{2,1,0:T(8,128)(2,1)S(1)}, f32[256,1536]{1,0:T(8,128)S(1)}, f32[256,1536]{1,0:T(8,128)S(1)}, f32[2,256,128]{2,1,0:T(8,128)S(1)}) custom-call(s32[32]{0:T(128)S(1)} %copy-done.6, s32[4]{0:T(128)S(1)} %pad_add_fusion.place_ref, bf16[2,4,8,8,1152]{4,3,2,1,0:T(8,128)(2,1)S(1)} %bitcast.22, ...), custom_call_target="tpu_custom_call" | custom-call | flops 1073741824 | bytes 4194304 | tf_op jit(solution)/shard_map/own_scores/pallas_call | solution.py:346
  61.0 3.1 %scores.1 = (bf16[32,32,576]{2,1,0:T(8,128)(2,1)S(1)}, bf16[2,256,1536]{2,1,0:T(8,128)(2,1)S(1)}, bf16[2,256,1536]{2,1,0:T(8,128)(2,1)S(1)}) custom-call(s32[32]{0:T(128)S(1)} %copy-done.6, s32[4]{0:T(128)S(1)} %pad_add_fusion.place_ref, bf16[2,4,8,8,1152]{4,3,2,1,0:T(8,128)(2,1)S(1)} %collective-permute-done.3.other_ref, ...), custom_call_target="tpu_custom_call" | custom-call | flops 2147483648 | bytes 8388608 | tf_op jit(solution)/shard_map/scores/pallas_call | solution.py:346
  64.1 3.2 %key_side.1 = (bf16[4,2,8,8,1152]{4,3,2,1,0:T(8,128)(2,1)S(1)}, bf16[4,2,8,8,1152]{4,3,2,1,0:T(8,128)(2,1)S(1)}) custom-call(s32[32]{0:T(128)S(1)} %copy-done.6, s32[4]{0:T(128)S(1)} %pad_add_fusion.place_ref, bf16[2,256,576]{2,1,0:T(8,128)(2,1)S(1)} %get-tuple-element.60.query, bf16[2,256,512]{2,1,0:T(8,128)(2,1)S(1)} %get-tuple-element.61.grad, ...), custom_call_target="tpu_custom_call" | custom-call | flops 2147483648 | bytes 8388608 | tf_op jit(solution)/shard_map/key_side/pallas_call | solution.py:346
  67.2 2.4 %collective-permute-start.4 = (bf16[4,2,8,8,1152]{4,3,2,1,0:T(8,128)(2,1)S(1)}, bf16[4,2,8,8,1152]{4,3,2,1,0:T(8,128)(2,1)S(1)}, u32[]{:S(2)}, u32[]{:S(2)}) collective-permute-start(bf16[4,2,8,8,1152]{4,3,2,1,0:T(8,128)(2,1)S(1)} %get-tuple-element.75), channel_id=1, source_target_pairs={{0,1},{1,0},{2,3},{3,2},{4,5},{5,4},{6,7},{7,6},{8,9},{9,8},{10,11... | collective-permute-start | bytes 3538952 | tf_op jit(solution)/shard_map/ppermute | solution.py:431
  69.7 3.3 %query_side.1 = (bf16[512,128]{1,0:T(8,128)(2,1)S(1)}, bf16[512,128]{1,0:T(8,128)(2,1)S(1)}, bf16[128,192]{1,0:T(8,128)(2,1)S(1)}, bf16[128,192]{1,0:T(8,128)(2,...) custom-call(s32[32]{0:T(128)S(1)} %copy-done.6, s32[4]{0:T(128)S(1)} %pad_add_fusion.place_ref, ...), custom_call_target="tpu_custom_call" | custom-call | flops 2147483648 | bytes 8388608 | tf_op jit(solution)/shard_map/query_side/pallas_call | solution.py:346
  73.0 1.3 pair_sum.1
  74.3 3.5 %all-to-all-start.2 = ((bf16[4,2,8,8,1152]{4,3,2,1,0:T(8,128)(2,1)}), bf16[4,2,8,8,1152]{4,3,2,1,0:T(8,128)(2,1)S(1)}, u32[]{:S(2)}, u32[]{:S(2)}) async-start(bf16[4,2,8,8,1152]{4,3,2,1,0:T(8,128)(2,1)} %pair_sum.1), calls=%async_computation.2 | async-start | bytes 2359296 | tf_op jit(solution)/shard_map/all_to_all | solution.py:427
  77.8 2.6 %collective-permute-start.5 = (bf16[512,128]{1,0:T(8,128)(2,1)S(1)}, bf16[512,128]{1,0:T(8,128)(2,1)S(1)}, u32[]{:S(2)}, u32[]{:S(2)}) collective-permute-start(bf16[512,128]{1,0:T(8,128)(2,1)S(1)} %get-tuple-element.78), channel_id=1, source_target_pairs={{0,256},{256,0},{1,257},{257,1},{2,258},{258,2},{3,259},{259,3},{4... | collective-permute-start | bytes 393224 | tf_op jit(solution)/shard_map/ppermute | solution.py:431
  80.4 4.1 %collective-permute-start.6 = (bf16[128,192]{1,0:T(8,128)(2,1)S(1)}, bf16[128,192]{1,0:T(8,128)(2,1)S(1)}, u32[]{:S(2)}, u32[]{:S(2)}) collective-permute-start(bf16[128,192]{1,0:T(8,128)(2,1)S(1)} %get-tuple-element.80), channel_id=1, source_target_pairs={{0,16},{16,0},{32,48},{48,32},{1,17},{17,1},{33,49},{49,33},{2,18}... | collective-permute-start | bytes 147464 | tf_op jit(solution)/shard_map/ppermute | solution.py:437
  84.4 2.5 %collective-permute-start.7 = (bf16[128,192]{1,0:T(8,128)(2,1)S(1)}, bf16[128,192]{1,0:T(8,128)(2,1)S(1)}, u32[]{:S(2)}, u32[]{:S(2)}) collective-permute-start(bf16[128,192]{1,0:T(8,128)(2,1)S(1)} %get-tuple-element.81), channel_id=1, source_target_pairs={{0,32},{16,48},{32,0},{48,16},{1,33},{17,49},{33,1},{49,17},{2,34}... | collective-permute-start | bytes 147464 | tf_op jit(solution)/shard_map/ppermute | solution.py:437
  86.9 2.8 %collective-permute-start.8 = (bf16[128,192]{1,0:T(8,128)(2,1)S(1)}, bf16[128,192]{1,0:T(8,128)(2,1)S(1)}, u32[]{:S(2)}, u32[]{:S(2)}) collective-permute-start(bf16[128,192]{1,0:T(8,128)(2,1)S(1)} %get-tuple-element.82), channel_id=1, source_target_pairs={{0,48},{16,32},{32,16},{48,0},{1,49},{17,33},{33,17},{49,1},{2,50}... | collective-permute-start | bytes 147464 | tf_op jit(solution)/shard_map/ppermute | solution.py:437
  91.6 1.9 %collective-permute-done.8.refs_3_ = bf16[128,192]{1,0:T(8,128)(2,1)S(1)} collective-permute-done((bf16[128,192]{1,0:T(8,128)(2,1)S(1)}, bf16[128,192]{1,0:T(8,128)(2,1)S(1)}, u32[]{:S(2)}, u32[]{:S(2)}) %collective-permute-start.8) | collective-permute-done | bytes 49184 | tf_op jit(solution)/shard_map/ppermute | solution.py:437
  93.5 1.2 all-to-all-done.2.lines_ref
  94.9 7.6 %all-to-all-start.3 = ((bf16[16,32,128]{2,1,0:T(8,128)(2,1)}), bf16[16,32,128]{2,1,0:T(8,128)(2,1)S(1)}, u32[]{:S(2)}, u32[]{:S(2)}) async-start(bf16[16,32,128]{2,1,0:T(8,128)(2,1)} %weight_sum.1), calls=%async_computation.3 | async-start | bytes 262144 | tf_op jit(solution)/shard_map/all_to_all | solution.py:427
  102.5 3.8 %collective-permute-start.9 = (bf16[8,8,1152]{2,1,0:T(8,128)(2,1)S(1)}, bf16[8,8,1152]{2,1,0:T(8,128)(2,1)S(1)}, u32[]{:S(2)}, u32[]{:S(2)}) collective-permute-start(bf16[8,8,1152]{2,1,0:T(8,128)(2,1)S(1)} %get-tuple-element.88), channel_id=1, source_target_pairs={{0,8},{8,0},{1,9},{9,1},{2,10},{10,2},{3,11},{11,3},{4,12},{12,4},... | collective-permute-start | bytes 442376 | tf_op jit(solution)/shard_map/ppermute | solution.py:431
  106.3 4.7 %collective-permute-done.9.came_ref = bf16[8,8,1152]{2,1,0:T(8,128)(2,1)S(1)} collective-permute-done((bf16[8,8,1152]{2,1,0:T(8,128)(2,1)S(1)}, bf16[8,8,1152]{2,1,0:T(8,128)(2,1)S(1)}, u32[]{:S(2)}, u32[]{:S(2)}) %collective-permute-start.9) | collective-permute-done | bytes 147488 | tf_op jit(solution)/shard_map/ppermute | solution.py:431
  111.0 3.9 %all-to-all-done.3.columns_ref = bf16[16,32,128]{2,1,0:T(8,128)(2,1)S(1)} async-done(((bf16[16,32,128]{2,1,0:T(8,128)(2,1)}), bf16[16,32,128]{2,1,0:T(8,128)(2,1)S(1)}, u32[]{:S(2)}, u32[]{:S(2)}) %all-to-all-start.3) | async-done | bytes 131104 | tf_op jit(solution)/shard_map/all_to_all | solution.py:427
  115.1 30.6 %all_to_all.31 = bf16[16,8,1600]{2,1,0:T(8,128)(2,1)S(1)} all-to-all(bf16[16,8,1600]{2,1,0:T(8,128)(2,1)S(1)} %pack.1), channel_id=1, replica_groups=mesh['dp'=2,'zq'=4,'z1'=2,'z0'=2,'yh'=2,'x'=4,'c'=2] {'zq','z1','z0'}, dimensions={0} | all-to-all | bytes 819200 | tf_op jit(solution)/shard_map/all_to_all | solution.py:427
  146.8 3.5 %all-to-all-start.5 = ((bf16[4,16,8,1024]{3,2,1,0:T(8,128)(2,1)}), bf16[4,16,8,1024]{3,2,1,0:T(8,128)(2,1)S(1)}, u32[]{:S(2)}, u32[]{:S(2)}) async-start(bf16[4,16,8,1024]{3,2,1,0:T(8,128)(2,1)} %broadcast_in_dim.23), calls=%async_computation.5 | async-start | bytes 2097152 | tf_op jit(solution)/shard_map/all_to_all | solution.py:427
  150.4 1.3 put_heads.1
  152.3 7.5 %all-to-all-done.5.whole_ref = bf16[4,16,8,1024]{3,2,1,0:T(8,128)(2,1)S(1)} async-done(((bf16[4,16,8,1024]{3,2,1,0:T(8,128)(2,1)}), bf16[4,16,8,1024]{3,2,1,0:T(8,128)(2,1)S(1)}, u32[]{:S(2)}, u32[]{:S(2)}) %all-to-all-start.5) | async-done | bytes 1048608 | tf_op jit(solution)/shard_map/all_to_all | solution.py:427
  159.8 1.4 spread.1
  (38 shorter events, 7.0 us)
Async XLA Ops:
  0.6 0.9 copy-start
  32.6 7.2 %copy-start.3 = (bf16[1,128,512]{2,1,0:T(8,128)(2,1)S(1)}, bf16[1,128,512]{2,1,0:T(8,128)(2,1)}, u32[]{:S(2)}) copy-start(bf16[1,128,512]{2,1,0:T(8,128)(2,1)} %param.8) | copy-start | bytes 393220
  32.6 7.2 %copy-start.4 = (bf16[1,128,512]{2,1,0:T(8,128)(2,1)S(1)}, bf16[1,128,512]{2,1,0:T(8,128)(2,1)}, u32[]{:S(2)}) copy-start(bf16[1,128,512]{2,1,0:T(8,128)(2,1)} %param.10) | copy-start | bytes 393220
  32.6 7.2 %copy-start.5 = (bf16[1,128,256]{2,1,0:T(8,128)(2,1)S(1)}, bf16[1,128,256]{2,1,0:T(8,128)(2,1)}, u32[]{:S(2)}) copy-start(bf16[1,128,256]{2,1,0:T(8,128)(2,1)} %param.9) | copy-start | bytes 196612
  32.6 25.3 %copy-start.1 = (bf16[512,512]{1,0:T(8,128)(2,1)S(1)}, bf16[512,512]{1,0:T(8,128)(2,1)}, u32[]{:S(2)}) copy-start(bf16[512,512]{1,0:T(8,128)(2,1)} %refs_5_.1) | copy-start | bytes 1572868
  32.6 25.3 %copy-start.2 = (bf16[512,512]{1,0:T(8,128)(2,1)S(1)}, bf16[512,512]{1,0:T(8,128)(2,1)}, u32[]{:S(2)}) copy-start(bf16[512,512]{1,0:T(8,128)(2,1)} %wk_ref.1) | copy-start | bytes 1572868
  32.6 25.3 %copy-start.6 = (s32[32]{0:T(128)S(1)}, s32[32]{0:T(128)}, u32[]{:S(2)}) copy-start(s32[32]{0:T(128)} %order_ref.9) | copy-start | bytes 388
  32.6 23.3 %all-to-all-start.1 = ((bf16[8,8,8,1152]{3,2,1,0:T(8,128)(2,1)}), bf16[8,8,8,1152]{3,2,1,0:T(8,128)(2,1)S(1)}, u32[]{:S(2)}, u32[]{:S(2)}) async-start(bf16[8,8,8,1152]{3,2,1,0:T(8,128)(2,1)} %broadcast_in_dim.19), calls=%async_computation.1 | async-start | bytes 2359296 | tf_op jit(solution)/shard_map/all_to_all | solution.py:427
  40.6 9.2 %collective-permute-start = (bf16[128,384]{1,0:T(8,128)(2,1)S(1)}, bf16[128,384]{1,0:T(8,128)(2,1)S(1)}, u32[]{:S(2)}, u32[]{:S(2)}) collective-permute-start(bf16[128,384]{1,0:T(8,128)(2,1)S(1)} %get-tuple-element.52), channel_id=1, source_target_pairs={{0,16},{16,0},{32,48},{48,32},{1,17},{17,1},{33,49},{49,33},{2,18}... | collective-permute-start | bytes 294920 | tf_op jit(solution)/shard_map/ppermute | solution.py:437
  43.3 7.8 %collective-permute-start.1 = (bf16[128,384]{1,0:T(8,128)(2,1)S(1)}, bf16[128,384]{1,0:T(8,128)(2,1)S(1)}, u32[]{:S(2)}, u32[]{:S(2)}) collective-permute-start(bf16[128,384]{1,0:T(8,128)(2,1)S(1)} %get-tuple-element.53), channel_id=1, source_target_pairs={{0,32},{16,48},{32,0},{48,16},{1,33},{17,49},{33,1},{49,17},{2,34}... | collective-permute-start | bytes 294920 | tf_op jit(solution)/shard_map/ppermute | solution.py:437
  46.4 8.2 %collective-permute-start.2 = (bf16[128,384]{1,0:T(8,128)(2,1)S(1)}, bf16[128,384]{1,0:T(8,128)(2,1)S(1)}, u32[]{:S(2)}, u32[]{:S(2)}) collective-permute-start(bf16[128,384]{1,0:T(8,128)(2,1)S(1)} %get-tuple-element.54), channel_id=1, source_target_pairs={{0,48},{16,32},{32,16},{48,0},{1,49},{17,33},{33,17},{49,1},{2,50}... | collective-permute-start | bytes 294920 | tf_op jit(solution)/shard_map/ppermute | solution.py:437
  56.0 5.0 %collective-permute-start.3 = (bf16[2,4,8,8,1152]{4,3,2,1,0:T(8,128)(2,1)S(1)}, bf16[2,4,8,8,1152]{4,3,2,1,0:T(8,128)(2,1)S(1)}, u32[]{:S(2)}, u32[]{:S(2)}) collective-permute-start(bf16[2,4,8,8,1152]{4,3,2,1,0:T(8,128)(2,1)S(1)} %bitcast.21), channel_id=1, source_target_pairs={{0,1},{1,0},{2,3},{3,2},{4,5},{5,4},{6,7},{7,6},{8,9},{9,8},{10,11... | collective-permute-start | bytes 3538952 | tf_op jit(solution)/shard_map/ppermute | solution.py:431
  67.2 5.7 %collective-permute-start.4 = (bf16[4,2,8,8,1152]{4,3,2,1,0:T(8,128)(2,1)S(1)}, bf16[4,2,8,8,1152]{4,3,2,1,0:T(8,128)(2,1)S(1)}, u32[]{:S(2)}, u32[]{:S(2)}) collective-permute-start(bf16[4,2,8,8,1152]{4,3,2,1,0:T(8,128)(2,1)S(1)} %get-tuple-element.75), channel_id=1, source_target_pairs={{0,1},{1,0},{2,3},{3,2},{4,5},{5,4},{6,7},{7,6},{8,9},{9,8},{10,11... | collective-permute-start | bytes 3538952 | tf_op jit(solution)/shard_map/ppermute | solution.py:431
  74.3 20.5 %all-to-all-start.2 = ((bf16[4,2,8,8,1152]{4,3,2,1,0:T(8,128)(2,1)}), bf16[4,2,8,8,1152]{4,3,2,1,0:T(8,128)(2,1)S(1)}, u32[]{:S(2)}, u32[]{:S(2)}) async-start(bf16[4,2,8,8,1152]{4,3,2,1,0:T(8,128)(2,1)} %pair_sum.1), calls=%async_computation.2 | async-start | bytes 2359296 | tf_op jit(solution)/shard_map/all_to_all | solution.py:427
  77.8 11.9 %collective-permute-start.5 = (bf16[512,128]{1,0:T(8,128)(2,1)S(1)}, bf16[512,128]{1,0:T(8,128)(2,1)S(1)}, u32[]{:S(2)}, u32[]{:S(2)}) collective-permute-start(bf16[512,128]{1,0:T(8,128)(2,1)S(1)} %get-tuple-element.78), channel_id=1, source_target_pairs={{0,256},{256,0},{1,257},{257,1},{2,258},{258,2},{3,259},{259,3},{4... | collective-permute-start | bytes 393224 | tf_op jit(solution)/shard_map/ppermute | solution.py:431
  80.4 10.1 %collective-permute-start.6 = (bf16[128,192]{1,0:T(8,128)(2,1)S(1)}, bf16[128,192]{1,0:T(8,128)(2,1)S(1)}, u32[]{:S(2)}, u32[]{:S(2)}) collective-permute-start(bf16[128,192]{1,0:T(8,128)(2,1)S(1)} %get-tuple-element.80), channel_id=1, source_target_pairs={{0,16},{16,0},{32,48},{48,32},{1,17},{17,1},{33,49},{49,33},{2,18}... | collective-permute-start | bytes 147464 | tf_op jit(solution)/shard_map/ppermute | solution.py:437
  84.4 7.2 %collective-permute-start.7 = (bf16[128,192]{1,0:T(8,128)(2,1)S(1)}, bf16[128,192]{1,0:T(8,128)(2,1)S(1)}, u32[]{:S(2)}, u32[]{:S(2)}) collective-permute-start(bf16[128,192]{1,0:T(8,128)(2,1)S(1)} %get-tuple-element.81), channel_id=1, source_target_pairs={{0,32},{16,48},{32,0},{48,16},{1,33},{17,49},{33,1},{49,17},{2,34}... | collective-permute-start | bytes 147464 | tf_op jit(solution)/shard_map/ppermute | solution.py:437
  86.9 6.6 %collective-permute-start.8 = (bf16[128,192]{1,0:T(8,128)(2,1)S(1)}, bf16[128,192]{1,0:T(8,128)(2,1)S(1)}, u32[]{:S(2)}, u32[]{:S(2)}) collective-permute-start(bf16[128,192]{1,0:T(8,128)(2,1)S(1)} %get-tuple-element.82), channel_id=1, source_target_pairs={{0,48},{16,32},{32,16},{48,0},{1,49},{17,33},{33,17},{49,1},{2,50}... | collective-permute-start | bytes 147464 | tf_op jit(solution)/shard_map/ppermute | solution.py:437
  94.9 20.1 %all-to-all-start.3 = ((bf16[16,32,128]{2,1,0:T(8,128)(2,1)}), bf16[16,32,128]{2,1,0:T(8,128)(2,1)S(1)}, u32[]{:S(2)}, u32[]{:S(2)}) async-start(bf16[16,32,128]{2,1,0:T(8,128)(2,1)} %weight_sum.1), calls=%async_computation.3 | async-start | bytes 262144 | tf_op jit(solution)/shard_map/all_to_all | solution.py:427
  102.5 8.5 %collective-permute-start.9 = (bf16[8,8,1152]{2,1,0:T(8,128)(2,1)S(1)}, bf16[8,8,1152]{2,1,0:T(8,128)(2,1)S(1)}, u32[]{:S(2)}, u32[]{:S(2)}) collective-permute-start(bf16[8,8,1152]{2,1,0:T(8,128)(2,1)S(1)} %get-tuple-element.88), channel_id=1, source_target_pairs={{0,8},{8,0},{1,9},{9,1},{2,10},{10,2},{3,11},{11,3},{4,12},{12,4},... | collective-permute-start | bytes 442376 | tf_op jit(solution)/shard_map/ppermute | solution.py:431
  146.8 12.9 %all-to-all-start.5 = ((bf16[4,16,8,1024]{3,2,1,0:T(8,128)(2,1)}), bf16[4,16,8,1024]{3,2,1,0:T(8,128)(2,1)S(1)}, u32[]{:S(2)}, u32[]{:S(2)}) async-start(bf16[4,16,8,1024]{3,2,1,0:T(8,128)(2,1)} %broadcast_in_dim.23), calls=%async_computation.5 | async-start | bytes 2097152 | tf_op jit(solution)/shard_map/all_to_all | solution.py:427

commit v5 on v4

--- a/solution.py
+++ b/solution.py
@@ -28,7 +28,7 @@
 STEPS = CHUNKS + LOW_CHUNKS
 PAIRS = N_CTX // 2
 WIDE = 2 * KEY_WIDTH
-SENT = D_NOPE + D_V + 128
+QUART = TOK_DEV // 4
 SLICE = 8
 NEG = -1e30
 SCALE = 1.0 / math.sqrt(D_NOPE + D_ROPE)
@@ -75,33 +75,41 @@
 def split_kernel(place_ref, qn_ref, qr_ref, go_ref, *out_refs):
     for ahead, out_ref in enumerate(out_refs):
         head = member(place_ref, ahead)
-        out_ref[:, :D_NOPE] = qn_ref[:, scaled(head, D_NOPE)]
-        out_ref[:, D_NOPE : D_NOPE + D_V] = go_ref[:, scaled(head, D_V)]
+        out_ref[:TOK_DEV, :D_NOPE] = qn_ref[:, scaled(head, D_NOPE)]
+        out_ref[:TOK_DEV, D_NOPE:] = go_ref[:, scaled(head, D_V)]
         two = qr_ref[:, scaled(head // 2, 2 * D_ROPE)]
         one = jnp.where(head % 2 == 1, two[:, D_ROPE:].astype(F32), two[:, :D_ROPE].astype(F32))
-        out_ref[:, D_NOPE + D_V : D_NOPE + D_V + D_ROPE] = one.astype(BF16)
-        out_ref[:, D_NOPE + D_V + D_ROPE :] = jnp.zeros((TOK_DEV, D_ROPE), BF16)
+        out_ref[TOK_DEV:, :] = jnp.concatenate(
+            [one[part * QUART : (part + 1) * QUART] for part in range(4)], axis=1
+        ).astype(BF16)
 
 
 def prepare_kernel(order_ref, place_ref, *refs):
     rows_refs, (wk_ref, wv_ref, query, grad, qn, go) = refs[:TEAM], refs[TEAM:]
     head = scaled(member(place_ref, 0), D_NOPE)
     wk, wv = wk_ref[:, head], wv_ref[:, head]
+    nope_rows = jnp.concatenate([rows_ref[:TOK_DEV, :D_NOPE] for rows_ref in rows_refs], axis=0)
+    out_rows = jnp.concatenate([rows_ref[:TOK_DEV, D_NOPE:] for rows_ref in rows_refs], axis=0)
+    q_lat = dot_nt(nope_rows, wk).astype(BF16)
+    g_lat = dot_nt(out_rows, wv).astype(BF16)
     for ahead, rows_ref in enumerate(rows_refs):
-        nope, out = rows_ref[:, :D_NOPE], rows_ref[:, D_NOPE : D_NOPE + D_V]
-        rope = rows_ref[:, D_NOPE + D_V : D_NOPE + D_V + D_ROPE]
-        q_lat = dot_nt(nope, wk).astype(BF16)
-        g_lat = dot_nt(out, wv).astype(BF16)
         late = low_half(order_ref, place_ref, ahead)
         into = slice(ahead * STRETCH, (ahead + 1) * STRETCH)
         for half in range(2):
-            toks = slice(half * STRETCH, (half + 1) * STRETCH)
+            toks = slice(ahead * TOK_DEV + half * STRETCH, ahead * TOK_DEV + (half + 1) * STRETCH)
+            rope = jnp.concatenate(
+                [
+                    rows_ref[TOK_DEV:, part * D_ROPE : (part + 1) * D_ROPE]
+                    for part in (2 * half, 2 * half + 1)
+                ],
+                axis=0,
+            )
             group = half ^ late
             query[group, into, :D_LAT] = q_lat[toks]
-            query[group, into, D_LAT:] = rope[toks]
+            query[group, into, D_LAT:] = rope
             grad[group, into, :] = g_lat[toks]
-            qn[group, into, :] = nope[toks]
-            go[group, into, :] = out[toks]
+            qn[group, into, :] = nope_rows[toks]
+            go[group, into, :] = out_rows[toks]
 
 
 def step_lanes(group, chunk):
@@ -111,6 +119,10 @@
 
 def group_chunks(group):
     return LOW_CHUNKS if group == 0 else CHUNKS
+
+
+def by_lane(join, values):
+    return join(values[:, :128], values[:, 128:])
 
 
 def half_scores(order_ref, place_ref, half, rows_ref, query, grad, keys, score, prob_grad):
@@ -139,7 +151,7 @@
 
     tops = []
     for group in range(2):
-        top = jnp.full((ROWS, 1), NEG, F32)
+        top = jnp.full((ROWS, 128), NEG, F32)
         for chunk in range(group_chunks(group)):
             lanes = step_lanes(group, chunk)
             key_rows = keys[chunk * PER_CHUNK : (chunk + 1) * PER_CHUNK].reshape(CHUNK, KEY_WIDTH)
@@ -148,7 +160,7 @@
                 raw = jnp.where(key_pos + chunk * PER_CHUNK * STRETCH <= row_pos[group], raw, NEG)
             score[:, lanes] = raw
             prob_grad[:, lanes] = dot_nt(grad[group], key_rows[:, :D_LAT])
-            top = jnp.maximum(top, jnp.max(raw, axis=1, keepdims=True))
+            top = jnp.maximum(top, by_lane(jnp.maximum, raw))
         tops.append(top)
     return tops
 
@@ -156,7 +168,7 @@
 def own_kernel(order_ref, place_ref, own_ref, query, grad, keys, score, prob_grad, top_ref):
     tops = half_scores(order_ref, place_ref, 0, own_ref, query, grad, keys, score, prob_grad)
     for group in range(2):
-        top_ref[group] = jnp.broadcast_to(tops[group], (ROWS, 128))
+        top_ref[group] = tops[group]
 
 
 def score_kernel(
@@ -178,18 +190,18 @@
     tops = half_scores(order_ref, place_ref, 1, other_ref, query, grad, keys, score, prob_grad)
     halves = ((own_score, own_prob_grad), (score, prob_grad))
     for group in range(2):
-        top = jnp.maximum(tops[group], top_ref[group, :, :1])
-        total = jnp.zeros((ROWS, 1), F32)
-        weight = jnp.zeros((ROWS, 1), F32)
+        top = jnp.max(jnp.maximum(tops[group], top_ref[group]), axis=1, keepdims=True)
+        total = jnp.zeros((ROWS, 128), F32)
+        weight = jnp.zeros((ROWS, 128), F32)
         for half, (raw_ref, grad_ref) in enumerate(halves):
             for chunk in range(group_chunks(group)):
                 lanes = step_lanes(group, chunk)
                 expo = jnp.exp2(raw_ref[:, lanes] - top)
                 expo_ref[half, :, lanes] = expo
-                total += jnp.sum(expo, axis=1, keepdims=True)
-                weight += jnp.sum(expo * grad_ref[:, lanes], axis=1, keepdims=True)
-        inverse = 1.0 / total
-        delta = weight * inverse
+                total += by_lane(jnp.add, expo)
+                weight += by_lane(jnp.add, expo * grad_ref[:, lanes])
+        inverse = 1.0 / jnp.sum(total, axis=1, keepdims=True)
+        delta = jnp.sum(weight, axis=1, keepdims=True) * inverse
         for half, (raw_ref, grad_ref) in enumerate(halves):
             for chunk in range(group_chunks(group)):
                 lanes = step_lanes(group, chunk)
@@ -237,10 +249,12 @@
         late = low_half(order_ref, place_ref, ahead)
         rows = slice(ahead * STRETCH, (ahead + 1) * STRETCH)
         for half in range(2):
-            toks = slice(half * STRETCH, (half + 1) * STRETCH)
             group = half ^ late
-            rows_ref[toks, :D_NOPE] = nope[group, rows]
-            rows_ref[toks, D_NOPE:] = query_low[group, rows, D_LAT:]
+            rows_ref[:STRETCH, half * D_NOPE : (half + 1) * D_NOPE] = nope[group, rows]
+            rope = query_low[group, rows, D_LAT:]
+            rows_ref[STRETCH:, half * 2 * D_ROPE : (half + 1) * 2 * D_ROPE] = jnp.concatenate(
+                [rope[:QUART], rope[QUART:]], axis=1
+            )
 
 
 def heads_kernel(place_ref, *refs):
@@ -248,18 +262,24 @@
     for ahead, rows_ref in enumerate(rows_refs):
         store[member(place_ref, ahead)] = rows_ref[...]
     for head in range(TEAM):
-        nope_ref[:, head * D_NOPE : (head + 1) * D_NOPE] = store[head, :, :D_NOPE]
-        rope_ref[:, head * D_ROPE : (head + 1) * D_ROPE] = store[head, :, D_NOPE:]
+        for half in range(2):
+            toks = slice(half * STRETCH, (half + 1) * STRETCH)
+            nope = store[head, :STRETCH, half * D_NOPE : (half + 1) * D_NOPE]
+            nope_ref[toks, head * D_NOPE : (head + 1) * D_NOPE] = nope
+        rope = [store[head, STRETCH:, part * D_ROPE : (part + 1) * D_ROPE] for part in range(4)]
+        rope_ref[:, head * D_ROPE : (head + 1) * D_ROPE] = jnp.concatenate(rope, axis=0)
 
 
 def side_kernel(
-    order_ref, place_ref, query, grad, prob_ref, score_grad_ref, g_own_ref, g_other_ref, side
+    order_ref, place_ref, query, grad, prob_ref, score_grad_ref, g_own_ref, g_other_ref, rope, slot_of
 ):
+    for slot in range(N_SLOT):
+        slot_of[order_ref[slot]] = slot
     both_query = query[...].reshape(2 * ROWS, KEY_WIDTH)
     both_grad = grad[...].reshape(2 * ROWS, D_LAT)
-    for half in range(2):
+    for half, out_ref in enumerate((g_own_ref, g_other_ref)):
         for chunk in range(CHUNKS):
-            late, where = step_lanes(1, chunk), slice(chunk * PER_CHUNK, (chunk + 1) * PER_CHUNK)
+            late = step_lanes(1, chunk)
             if chunk < LOW_CHUNKS:
                 early = step_lanes(0, chunk)
                 score_grad, prob = [
@@ -271,19 +291,23 @@
                 key_side = dot_tn(score_grad_ref[half, :, late], query[1])
                 value_side = dot_tn(prob_ref[half, :, late], grad[1])
             lat = key_side[:, :D_LAT] + value_side
-            side[half, where, :, :D_LAT] = lat.reshape(PER_CHUNK, HALF, D_LAT)
-            side[half, where, :, D_LAT:] = key_side[:, D_LAT:].reshape(PER_CHUNK, HALF, D_ROPE)
+            for part in range(PER_CHUNK):
+                rows = slice(part * HALF, (part + 1) * HALF)
+                place = chunk * PER_CHUNK + part
+                slot = slot_of[place]
+                apart = (slot + place_ref[2]) % 2
+                lanes = scaled((slot // 2) % 2, D_LAT)
+                out_ref[:, apart, slot // 4, :, lanes] = lat[rows].reshape(4, SLICE, D_LAT).astype(BF16)
+                rope[half, place] = key_side[rows, D_LAT:]
 
     @pl.loop(0, PAIRS, unroll=4)
     def _(pair):
         for upper in range(2):
             apart = (upper + place_ref[2]) % 2
             for half, out_ref in enumerate((g_own_ref, g_other_ref)):
-                both = [side[half, order_ref[4 * pair + 2 * parity + upper]] for parity in range(2)]
-                rows = jnp.concatenate(
-                    [both[0][:, :D_LAT], both[1][:, :D_LAT], both[0][:, D_LAT:], both[1][:, D_LAT:]], axis=1
-                )
-                out_ref[:, apart, pair] = rows.reshape(4, SLICE, WIDE).astype(BF16)
+                both = [rope[half, order_ref[4 * pair + 2 * parity + upper]] for parity in range(2)]
+                rows = jnp.concatenate(both, axis=1).reshape(4, SLICE, 2 * D_ROPE)
+                out_ref[:, apart, pair, :, 2 * D_LAT :] = rows.astype(BF16)
 
 
 def pair_kernel(own_ref, came_ref, out_ref):
@@ -363,7 +387,7 @@
 
 
 def split(place, qn, qr, go):
-    return call(split_kernel, "split_heads", 1, (place, qn, qr, go), ((TOK_DEV, SENT),) * TEAM)
+    return call(split_kernel, "split_heads", 1, (place, qn, qr, go), ((TOK_DEV + QUART, D_NOPE + D_V),) * TEAM)
 
 
 def prepare(order, place, rows, wk, wv):
@@ -385,7 +409,7 @@
 
 
 def query_side(order, place, own_keys, keys, prob, score_grad, qn, go, wk):
-    rows = (TOK_DEV, D_NOPE + D_ROPE)
+    rows = (STRETCH + QUART, 2 * D_NOPE)
     return call(
         query_kernel,
         "query_side",
@@ -405,7 +429,7 @@
         1,
         (place, *rows),
         ((TOK_DEV, TEAM * D_NOPE), (TOK_DEV, TEAM * D_ROPE)),
-        [pltpu.VMEM((TEAM, TOK_DEV, D_NOPE + D_ROPE), BF16)],
+        [pltpu.VMEM((TEAM, STRETCH + QUART, 2 * D_NOPE), BF16)],
     )
 
 
@@ -417,7 +441,7 @@
         2,
         (order, place, query, grad, prob, score_grad),
         (part, part),
-        [pltpu.VMEM((2, *KEY_SHAPE), F32)],
+        [pltpu.VMEM((2, N_SLOT, HALF, D_ROPE), F32), pltpu.SMEM((N_SLOT,), jnp.int32)],
         2**31,
         2**23,
     )
@@ -431,10 +455,10 @@
     return lax.ppermute(values, axis, [(0, 1), (1, 0)])
 
 
-def team_swap(parts):
-    moved = [parts[0]]
-    for ahead in range(1, TEAM):
-        moved.append(lax.ppermute(parts[ahead], ("z1", "z0"), [(i, i ^ ahead) for i in range(TEAM)]))
+def team_swap(parts, mates=(2, 3, 1)):
+    moved = list(parts)
+    for ahead in mates:
+        moved[ahead] = lax.ppermute(parts[ahead], ("z1", "z0"), [(i, i ^ ahead) for i in range(TEAM)])
     return moved
 
 
@@ -468,12 +492,14 @@
     give, pair = lax.optimization_barrier((give, pair))
     lines = swap(pair, "x")
     (weights,) = call(weight_kernel, "weight_sum", 0, (keep, flip(give, "dp")), ((N_CTX, 32, D_NOPE),))
-    rows = team_swap(rows)
+    rows = team_swap(rows, (2, 3))
     lines, weights, rows = lax.optimization_barrier((lines, weights, rows))
     keep, give = call(line_kernel, "line_sum", 0, (lines,), (pair.shape[2:],) * 2)
     give, weights = lax.optimization_barrier((give, weights))
     columns = swap(weights, Z_AXES)
     came = flip(give, "yh")
+    rows = team_swap(rows, (1,))
+    columns, came, rows = lax.optimization_barrier((columns, came, rows))
     (packed,) = call(pack_kernel, "pack", 0, (columns, keep, came), ((N_CTX, SLICE, 1024 + KEY_WIDTH),))
     packed = swap(packed, Z_AXES)
     nope_grad, rope_grad = put_heads(place, rows)

time: 162 us -> 161 us (level)
    ppermute x4, waiting for transfers between devices: 4.75 us -> 0.01 us  [flip(): return lax.ppermute(values, axis, [(0, 1), (1, 0)])]
    all_to_all x4, waiting for transfers between devices: 14 us -> 17.5 us  [swap(): return lax.all_to_all(values, axes, 0, 0, tiled=True)]
  transfers between devices with their start and end apart: 14 -> 14, of which waited for: 9 -> 8; matrix products, arithmetic and copies ran while one was open for 0% -> 0% of each run, Pallas kernels for 6% -> 6%
where the time goes in v5:
time: 161 us
  blocking collectives  60.1 us (37%)
  starting transfers between devices  52.2 us (32%)
  waiting for transfers between devices  25.2 us (16%)
  Pallas kernels  17.9 us (11%)
  local copies, waits for them, and re-layouts  3.58 us (2%)
    all_to_all x2, blocking collectives, swap(): return lax.all_to_all(values, axes, 0, 0, tiled=True)  60.1 us
    all_to_all x4, starting transfers between devices, swap(): return lax.all_to_all(values, axes, 0, 0, tiled=True)  21.5 us
    ppermute x6, starting transfers between devices, team_swap(): lax.ppermute(parts[ahead], ('z1', 'z0'), [(i, i ^ ahead) for i in range(T...  20 us
    pallas_call x12, Pallas kernels, call(): pl.pallas_call(kernel, out_shape=shapes, in_specs=[SMEM] * n_smem + [VMEM...  17.9 us
    all_to_all x4, waiting for transfers between devices, swap(): return lax.all_to_all(values, axes, 0, 0, tiled=True)  17.5 us
    ppermute x4, starting transfers between devices, flip(): return lax.ppermute(values, axis, [(0, 1), (1, 0)])  10.7 us
    ppermute x6, waiting for transfers between devices, team_swap(): lax.ppermute(parts[ahead], ('z1', 'z0'), [(i, i ^ ahead) for i in range(T...  7.68 us
  transfers between devices with their start and end apart: 14, of which 8 were waited for; matrix products, arithmetic and copies ran while one was open for 0% of the time, Pallas kernels for 6%

profile of v5, /device:TPU:64, one launch (start us, length us, event | category | flops | bytes accessed | tf_op | source)
XLA Modules:
  0.0 160.7 jit_solution(774435559527019197)
XLA Ops:
  1.8 29.4 %all_to_all.30 = bf16[16,8,576]{2,1,0:T(8,128)(2,1)S(1)} all-to-all(bf16[16,8,576]{2,1,0:T(8,128)(2,1)S(1)} %broadcast_in_dim.18), channel_id=1, replica_groups=mesh['dp'=2,'zq'=4,'z1'=2,'z0'=2,'yh'=2,'x'=4,'c'=2] {'zq','z1','z0'}, dimensions={0} | all-to-all | bytes 294912 | tf_op jit(solution)/shard_map/all_to_all | solution.py:451
  31.4 1.2 broadcast_in_dim.19
  32.6 7.1 %all-to-all-start.1 = ((bf16[8,8,8,1152]{3,2,1,0:T(8,128)(2,1)}), bf16[8,8,8,1152]{3,2,1,0:T(8,128)(2,1)S(1)}, u32[]{:S(2)}, u32[]{:S(2)}) async-start(bf16[8,8,8,1152]{3,2,1,0:T(8,128)(2,1)} %broadcast_in_dim.19), calls=%async_computation.1 | async-start | bytes 2359296 | tf_op jit(solution)/shard_map/all_to_all | solution.py:451
  40.5 2.7 %collective-permute-start = (bf16[160,256]{1,0:T(8,128)(2,1)S(1)}, bf16[160,256]{1,0:T(8,128)(2,1)S(1)}, u32[]{:S(2)}, u32[]{:S(2)}) collective-permute-start(bf16[160,256]{1,0:T(8,128)(2,1)S(1)} %get-tuple-element.58), channel_id=1, source_target_pairs={{0,16},{16,0},{32,48},{48,32},{1,17},{17,1},{33,49},{49,33},{2,18}... | collective-permute-start | bytes 245768 | tf_op jit(solution)/shard_map/ppermute | solution.py:461
  43.3 3.1 %collective-permute-start.1 = (bf16[160,256]{1,0:T(8,128)(2,1)S(1)}, bf16[160,256]{1,0:T(8,128)(2,1)S(1)}, u32[]{:S(2)}, u32[]{:S(2)}) collective-permute-start(bf16[160,256]{1,0:T(8,128)(2,1)S(1)} %get-tuple-element.59), channel_id=1, source_target_pairs={{0,32},{16,48},{32,0},{48,16},{1,33},{17,49},{33,1},{49,17},{2,34}... | collective-permute-start | bytes 245768 | tf_op jit(solution)/shard_map/ppermute | solution.py:461
  46.4 3.4 %collective-permute-start.2 = (bf16[160,256]{1,0:T(8,128)(2,1)S(1)}, bf16[160,256]{1,0:T(8,128)(2,1)S(1)}, u32[]{:S(2)}, u32[]{:S(2)}) collective-permute-start(bf16[160,256]{1,0:T(8,128)(2,1)S(1)} %get-tuple-element.60), channel_id=1, source_target_pairs={{0,48},{16,32},{32,16},{48,0},{1,49},{17,33},{33,17},{49,1},{2,50}... | collective-permute-start | bytes 245768 | tf_op jit(solution)/shard_map/ppermute | solution.py:461
  50.7 2.0 %collective-permute-done.2.refs_3_ = bf16[160,256]{1,0:T(8,128)(2,1)S(1)} collective-permute-done((bf16[160,256]{1,0:T(8,128)(2,1)S(1)}, bf16[160,256]{1,0:T(8,128)(2,1)S(1)}, u32[]{:S(2)}, u32[]{:S(2)}) %collective-permute-start.2) | collective-permute-done | bytes 81952 | tf_op jit(solution)/shard_map/ppermute | solution.py:461
  52.7 3.3 %all-to-all-done.1 = bf16[8,8,8,1152]{3,2,1,0:T(8,128)(2,1)S(1)} async-done(((bf16[8,8,8,1152]{3,2,1,0:T(8,128)(2,1)}), bf16[8,8,8,1152]{3,2,1,0:T(8,128)(2,1)S(1)}, u32[]{:S(2)}, u32[]{:S(2)}) %all-to-all-start.1) | async-done | bytes 1179680 | tf_op jit(solution)/shard_map/all_to_all | solution.py:451
  56.0 1.9 %collective-permute-start.3 = (bf16[2,4,8,8,1152]{4,3,2,1,0:T(8,128)(2,1)S(1)}, bf16[2,4,8,8,1152]{4,3,2,1,0:T(8,128)(2,1)S(1)}, u32[]{:S(2)}, u32[]{:S(2)}) collective-permute-start(bf16[2,4,8,8,1152]{4,3,2,1,0:T(8,128)(2,1)S(1)} %bitcast.21), channel_id=1, source_target_pairs={{0,1},{1,0},{2,3},{3,2},{4,5},{5,4},{6,7},{7,6},{8,9},{9,8},{10,11... | collective-permute-start | bytes 3538952 | tf_op jit(solution)/shard_map/ppermute | solution.py:455
  58.9 2.0 %own_scores.1 = (bf16[32,32,576]{2,1,0:T(8,128)(2,1)S(1)}, f32[256,1536]{1,0:T(8,128)S(1)}, f32[256,1536]{1,0:T(8,128)S(1)}, f32[2,256,128]{2,1,0:T(8,128)S(1)}) custom-call(s32[32]{0:T(128)S(1)} %copy-done.6, s32[4]{0:T(128)S(1)} %pad_add_fusion.place_ref, bf16[2,4,8,8,1152]{4,3,2,1,0:T(8,128)(2,1)S(1)} %bitcast.22, ...), custom_call_target="tpu_custom_call" | custom-call | flops 1073741824 | bytes 4194304 | tf_op jit(solution)/shard_map/own_scores/pallas_call | solution.py:370
  60.9 2.9 %scores.1 = (bf16[32,32,576]{2,1,0:T(8,128)(2,1)S(1)}, bf16[2,256,1536]{2,1,0:T(8,128)(2,1)S(1)}, bf16[2,256,1536]{2,1,0:T(8,128)(2,1)S(1)}) custom-call(s32[32]{0:T(128)S(1)} %copy-done.6, s32[4]{0:T(128)S(1)} %pad_add_fusion.place_ref, bf16[2,4,8,8,1152]{4,3,2,1,0:T(8,128)(2,1)S(1)} %collective-permute-done.3.other_ref, ...), custom_call_target="tpu_custom_call" | custom-call | flops 2147483648 | bytes 8388608 | tf_op jit(solution)/shard_map/scores/pallas_call | solution.py:370
  63.9 3.0 %key_side.1 = (bf16[4,2,8,8,1152]{4,3,2,1,0:T(8,128)(2,1)S(1)}, bf16[4,2,8,8,1152]{4,3,2,1,0:T(8,128)(2,1)S(1)}) custom-call(s32[32]{0:T(128)S(1)} %copy-done.6, s32[4]{0:T(128)S(1)} %pad_add_fusion.place_ref, bf16[2,256,576]{2,1,0:T(8,128)(2,1)S(1)} %get-tuple-element.66.query, bf16[2,256,512]{2,1,0:T(8,128)(2,1)S(1)} %get-tuple-element.67.grad, ...), custom_call_target="tpu_custom_call" | custom-call | flops 2147483648 | bytes 8388608 | tf_op jit(solution)/shard_map/key_side/pallas_call | solution.py:370
  66.9 2.4 %collective-permute-start.4 = (bf16[4,2,8,8,1152]{4,3,2,1,0:T(8,128)(2,1)S(1)}, bf16[4,2,8,8,1152]{4,3,2,1,0:T(8,128)(2,1)S(1)}, u32[]{:S(2)}, u32[]{:S(2)}) collective-permute-start(bf16[4,2,8,8,1152]{4,3,2,1,0:T(8,128)(2,1)S(1)} %get-tuple-element.81), channel_id=1, source_target_pairs={{0,1},{1,0},{2,3},{3,2},{4,5},{5,4},{6,7},{7,6},{8,9},{9,8},{10,11... | collective-permute-start | bytes 3538952 | tf_op jit(solution)/shard_map/ppermute | solution.py:455
  69.3 3.2 %query_side.1 = (bf16[512,128]{1,0:T(8,128)(2,1)S(1)}, bf16[512,128]{1,0:T(8,128)(2,1)S(1)}, bf16[96,256]{1,0:T(8,128)(2,1)S(1)}, bf16[96,256]{1,0:T(8,128)(2,1)...) custom-call(s32[32]{0:T(128)S(1)} %copy-done.6, s32[4]{0:T(128)S(1)} %pad_add_fusion.place_ref, ...), custom_call_target="tpu_custom_call" | custom-call | flops 2147483648 | bytes 8388608 | tf_op jit(solution)/shard_map/query_side/pallas_call | solution.py:370
  72.5 1.3 pair_sum.1
  73.8 3.5 %all-to-all-start.2 = ((bf16[4,2,8,8,1152]{4,3,2,1,0:T(8,128)(2,1)}), bf16[4,2,8,8,1152]{4,3,2,1,0:T(8,128)(2,1)S(1)}, u32[]{:S(2)}, u32[]{:S(2)}) async-start(bf16[4,2,8,8,1152]{4,3,2,1,0:T(8,128)(2,1)} %pair_sum.1), calls=%async_computation.2 | async-start | bytes 2359296 | tf_op jit(solution)/shard_map/all_to_all | solution.py:451
  77.3 2.6 %collective-permute-start.5 = (bf16[512,128]{1,0:T(8,128)(2,1)S(1)}, bf16[512,128]{1,0:T(8,128)(2,1)S(1)}, u32[]{:S(2)}, u32[]{:S(2)}) collective-permute-start(bf16[512,128]{1,0:T(8,128)(2,1)S(1)} %get-tuple-element.84), channel_id=1, source_target_pairs={{0,256},{256,0},{1,257},{257,1},{2,258},{258,2},{3,259},{259,3},{4... | collective-permute-start | bytes 393224 | tf_op jit(solution)/shard_map/ppermute | solution.py:455
  79.9 3.5 %collective-permute-start.6 = (bf16[96,256]{1,0:T(8,128)(2,1)S(1)}, bf16[96,256]{1,0:T(8,128)(2,1)S(1)}, u32[]{:S(2)}, u32[]{:S(2)}) collective-permute-start(bf16[96,256]{1,0:T(8,128)(2,1)S(1)} %get-tuple-element.87), channel_id=1, source_target_pairs={{0,32},{16,48},{32,0},{48,16},{1,33},{17,49},{33,1},{49,17},{2,34}... | collective-permute-start | bytes 147464 | tf_op jit(solution)/shard_map/ppermute | solution.py:461
  83.4 3.9 %collective-permute-start.7 = (bf16[96,256]{1,0:T(8,128)(2,1)S(1)}, bf16[96,256]{1,0:T(8,128)(2,1)S(1)}, u32[]{:S(2)}, u32[]{:S(2)}) collective-permute-start(bf16[96,256]{1,0:T(8,128)(2,1)S(1)} %get-tuple-element.88), channel_id=1, source_target_pairs={{0,48},{16,32},{32,16},{48,0},{1,49},{17,33},{33,17},{49,1},{2,50}... | collective-permute-start | bytes 147464 | tf_op jit(solution)/shard_map/ppermute | solution.py:461
  88.1 1.8 %collective-permute-done.7.refs_3_ = bf16[96,256]{1,0:T(8,128)(2,1)S(1)} collective-permute-done((bf16[96,256]{1,0:T(8,128)(2,1)S(1)}, bf16[96,256]{1,0:T(8,128)(2,1)S(1)}, u32[]{:S(2)}, u32[]{:S(2)}) %collective-permute-start.7) | collective-permute-done | bytes 49184 | tf_op jit(solution)/shard_map/ppermute | solution.py:461
  89.9 4.4 %all-to-all-done.2.lines_ref = bf16[4,2,8,8,1152]{4,3,2,1,0:T(8,128)(2,1)S(1)} async-done(((bf16[4,2,8,8,1152]{4,3,2,1,0:T(8,128)(2,1)}), bf16[4,2,8,8,1152]{4,3,2,1,0:T(8,128)(2,1)S(1)}, u32[]{:S(2)}, u32[]{:S(2)}) %all-to-all-start.2) | async-done | bytes 1179680 | tf_op jit(solution)/shard_map/all_to_all | solution.py:451
  94.4 7.4 %all-to-all-start.3 = ((bf16[16,32,128]{2,1,0:T(8,128)(2,1)}), bf16[16,32,128]{2,1,0:T(8,128)(2,1)S(1)}, u32[]{:S(2)}, u32[]{:S(2)}) async-start(bf16[16,32,128]{2,1,0:T(8,128)(2,1)} %weight_sum.1), calls=%async_computation.3 | async-start | bytes 262144 | tf_op jit(solution)/shard_map/all_to_all | solution.py:451
  101.8 3.8 %collective-permute-start.8 = (bf16[8,8,1152]{2,1,0:T(8,128)(2,1)S(1)}, bf16[8,8,1152]{2,1,0:T(8,128)(2,1)S(1)}, u32[]{:S(2)}, u32[]{:S(2)}) collective-permute-start(bf16[8,8,1152]{2,1,0:T(8,128)(2,1)S(1)} %get-tuple-element.93), channel_id=1, source_target_pairs={{0,8},{8,0},{1,9},{9,1},{2,10},{10,2},{3,11},{11,3},{4,12},{12,4},... | collective-permute-start | bytes 442376 | tf_op jit(solution)/shard_map/ppermute | solution.py:455
  105.6 3.4 %collective-permute-start.9 = (bf16[96,256]{1,0:T(8,128)(2,1)S(1)}, bf16[96,256]{1,0:T(8,128)(2,1)S(1)}, u32[]{:S(2)}, u32[]{:S(2)}) collective-permute-start(bf16[96,256]{1,0:T(8,128)(2,1)S(1)} %get-tuple-element.95), channel_id=1, source_target_pairs={{0,16},{16,0},{32,48},{48,32},{1,17},{17,1},{33,49},{49,33},{2,18}... | collective-permute-start | bytes 147464 | tf_op jit(solution)/shard_map/ppermute | solution.py:461
  109.0 3.0 %collective-permute-done.9.refs_1_ = bf16[96,256]{1,0:T(8,128)(2,1)S(1)} collective-permute-done((bf16[96,256]{1,0:T(8,128)(2,1)S(1)}, bf16[96,256]{1,0:T(8,128)(2,1)S(1)}, u32[]{:S(2)}, u32[]{:S(2)}) %collective-permute-start.9) | collective-permute-done | bytes 49184 | tf_op jit(solution)/shard_map/ppermute | solution.py:461
  112.0 2.5 %all-to-all-done.3.columns_ref = bf16[16,32,128]{2,1,0:T(8,128)(2,1)S(1)} async-done(((bf16[16,32,128]{2,1,0:T(8,128)(2,1)}), bf16[16,32,128]{2,1,0:T(8,128)(2,1)S(1)}, u32[]{:S(2)}, u32[]{:S(2)}) %all-to-all-start.3) | async-done | bytes 131104 | tf_op jit(solution)/shard_map/all_to_all | solution.py:451
  114.6 30.7 %all_to_all.31 = bf16[16,8,1600]{2,1,0:T(8,128)(2,1)S(1)} all-to-all(bf16[16,8,1600]{2,1,0:T(8,128)(2,1)S(1)} %pack.1), channel_id=1, replica_groups=mesh['dp'=2,'zq'=4,'z1'=2,'z0'=2,'yh'=2,'x'=4,'c'=2] {'zq','z1','z0'}, dimensions={0} | all-to-all | bytes 819200 | tf_op jit(solution)/shard_map/all_to_all | solution.py:451
  145.3 1.1 broadcast_in_dim.23
  146.4 3.5 %all-to-all-start.5 = ((bf16[4,16,8,1024]{3,2,1,0:T(8,128)(2,1)}), bf16[4,16,8,1024]{3,2,1,0:T(8,128)(2,1)S(1)}, u32[]{:S(2)}, u32[]{:S(2)}) async-start(bf16[4,16,8,1024]{3,2,1,0:T(8,128)(2,1)} %broadcast_in_dim.23), calls=%async_computation.5 | async-start | bytes 2097152 | tf_op jit(solution)/shard_map/all_to_all | solution.py:451
  149.9 1.4 put_heads.1
  151.9 7.4 %all-to-all-done.5.whole_ref = bf16[4,16,8,1024]{3,2,1,0:T(8,128)(2,1)S(1)} async-done(((bf16[4,16,8,1024]{3,2,1,0:T(8,128)(2,1)}), bf16[4,16,8,1024]{3,2,1,0:T(8,128)(2,1)S(1)}, u32[]{:S(2)}, u32[]{:S(2)}) %all-to-all-start.5) | async-done | bytes 1048608 | tf_op jit(solution)/shard_map/all_to_all | solution.py:451
  159.3 1.4 spread.1
  (38 shorter events, 5.7 us)
Async XLA Ops:
  0.6 0.9 copy-start
  32.6 7.2 %copy-start.3 = (bf16[1,128,512]{2,1,0:T(8,128)(2,1)S(1)}, bf16[1,128,512]{2,1,0:T(8,128)(2,1)}, u32[]{:S(2)}) copy-start(bf16[1,128,512]{2,1,0:T(8,128)(2,1)} %param.8) | copy-start | bytes 393220
  32.6 7.2 %copy-start.4 = (bf16[1,128,512]{2,1,0:T(8,128)(2,1)S(1)}, bf16[1,128,512]{2,1,0:T(8,128)(2,1)}, u32[]{:S(2)}) copy-start(bf16[1,128,512]{2,1,0:T(8,128)(2,1)} %param.10) | copy-start | bytes 393220
  32.6 7.2 %copy-start.5 = (bf16[1,128,256]{2,1,0:T(8,128)(2,1)S(1)}, bf16[1,128,256]{2,1,0:T(8,128)(2,1)}, u32[]{:S(2)}) copy-start(bf16[1,128,256]{2,1,0:T(8,128)(2,1)} %param.9) | copy-start | bytes 196612
  32.6 25.3 %copy-start.1 = (bf16[512,512]{1,0:T(8,128)(2,1)S(1)}, bf16[512,512]{1,0:T(8,128)(2,1)}, u32[]{:S(2)}) copy-start(bf16[512,512]{1,0:T(8,128)(2,1)} %refs_5_.1) | copy-start | bytes 1572868
  32.6 25.3 %copy-start.2 = (bf16[512,512]{1,0:T(8,128)(2,1)S(1)}, bf16[512,512]{1,0:T(8,128)(2,1)}, u32[]{:S(2)}) copy-start(bf16[512,512]{1,0:T(8,128)(2,1)} %wk_ref.1) | copy-start | bytes 1572868
  32.6 25.3 %copy-start.6 = (s32[32]{0:T(128)S(1)}, s32[32]{0:T(128)}, u32[]{:S(2)}) copy-start(s32[32]{0:T(128)} %order_ref.9) | copy-start | bytes 388
  32.6 23.3 %all-to-all-start.1 = ((bf16[8,8,8,1152]{3,2,1,0:T(8,128)(2,1)}), bf16[8,8,8,1152]{3,2,1,0:T(8,128)(2,1)S(1)}, u32[]{:S(2)}, u32[]{:S(2)}) async-start(bf16[8,8,8,1152]{3,2,1,0:T(8,128)(2,1)} %broadcast_in_dim.19), calls=%async_computation.1 | async-start | bytes 2359296 | tf_op jit(solution)/shard_map/all_to_all | solution.py:451
  40.5 9.2 %collective-permute-start = (bf16[160,256]{1,0:T(8,128)(2,1)S(1)}, bf16[160,256]{1,0:T(8,128)(2,1)S(1)}, u32[]{:S(2)}, u32[]{:S(2)}) collective-permute-start(bf16[160,256]{1,0:T(8,128)(2,1)S(1)} %get-tuple-element.58), channel_id=1, source_target_pairs={{0,16},{16,0},{32,48},{48,32},{1,17},{17,1},{33,49},{49,33},{2,18}... | collective-permute-start | bytes 245768 | tf_op jit(solution)/shard_map/ppermute | solution.py:461
  43.3 7.4 %collective-permute-start.1 = (bf16[160,256]{1,0:T(8,128)(2,1)S(1)}, bf16[160,256]{1,0:T(8,128)(2,1)S(1)}, u32[]{:S(2)}, u32[]{:S(2)}) collective-permute-start(bf16[160,256]{1,0:T(8,128)(2,1)S(1)} %get-tuple-element.59), channel_id=1, source_target_pairs={{0,32},{16,48},{32,0},{48,16},{1,33},{17,49},{33,1},{49,17},{2,34}... | collective-permute-start | bytes 245768 | tf_op jit(solution)/shard_map/ppermute | solution.py:461
  46.4 6.3 %collective-permute-start.2 = (bf16[160,256]{1,0:T(8,128)(2,1)S(1)}, bf16[160,256]{1,0:T(8,128)(2,1)S(1)}, u32[]{:S(2)}, u32[]{:S(2)}) collective-permute-start(bf16[160,256]{1,0:T(8,128)(2,1)S(1)} %get-tuple-element.60), channel_id=1, source_target_pairs={{0,48},{16,32},{32,16},{48,0},{1,49},{17,33},{33,17},{49,1},{2,50}... | collective-permute-start | bytes 245768 | tf_op jit(solution)/shard_map/ppermute | solution.py:461
  56.0 5.0 %collective-permute-start.3 = (bf16[2,4,8,8,1152]{4,3,2,1,0:T(8,128)(2,1)S(1)}, bf16[2,4,8,8,1152]{4,3,2,1,0:T(8,128)(2,1)S(1)}, u32[]{:S(2)}, u32[]{:S(2)}) collective-permute-start(bf16[2,4,8,8,1152]{4,3,2,1,0:T(8,128)(2,1)S(1)} %bitcast.21), channel_id=1, source_target_pairs={{0,1},{1,0},{2,3},{3,2},{4,5},{5,4},{6,7},{7,6},{8,9},{9,8},{10,11... | collective-permute-start | bytes 3538952 | tf_op jit(solution)/shard_map/ppermute | solution.py:455
  66.9 5.6 %collective-permute-start.4 = (bf16[4,2,8,8,1152]{4,3,2,1,0:T(8,128)(2,1)S(1)}, bf16[4,2,8,8,1152]{4,3,2,1,0:T(8,128)(2,1)S(1)}, u32[]{:S(2)}, u32[]{:S(2)}) collective-permute-start(bf16[4,2,8,8,1152]{4,3,2,1,0:T(8,128)(2,1)S(1)} %get-tuple-element.81), channel_id=1, source_target_pairs={{0,1},{1,0},{2,3},{3,2},{4,5},{5,4},{6,7},{7,6},{8,9},{9,8},{10,11... | collective-permute-start | bytes 3538952 | tf_op jit(solution)/shard_map/ppermute | solution.py:455
  73.8 20.5 %all-to-all-start.2 = ((bf16[4,2,8,8,1152]{4,3,2,1,0:T(8,128)(2,1)}), bf16[4,2,8,8,1152]{4,3,2,1,0:T(8,128)(2,1)S(1)}, u32[]{:S(2)}, u32[]{:S(2)}) async-start(bf16[4,2,8,8,1152]{4,3,2,1,0:T(8,128)(2,1)} %pair_sum.1), calls=%async_computation.2 | async-start | bytes 2359296 | tf_op jit(solution)/shard_map/all_to_all | solution.py:451
  77.3 10.0 %collective-permute-start.5 = (bf16[512,128]{1,0:T(8,128)(2,1)S(1)}, bf16[512,128]{1,0:T(8,128)(2,1)S(1)}, u32[]{:S(2)}, u32[]{:S(2)}) collective-permute-start(bf16[512,128]{1,0:T(8,128)(2,1)S(1)} %get-tuple-element.84), channel_id=1, source_target_pairs={{0,256},{256,0},{1,257},{257,1},{2,258},{258,2},{3,259},{259,3},{4... | collective-permute-start | bytes 393224 | tf_op jit(solution)/shard_map/ppermute | solution.py:455
  79.9 8.1 %collective-permute-start.6 = (bf16[96,256]{1,0:T(8,128)(2,1)S(1)}, bf16[96,256]{1,0:T(8,128)(2,1)S(1)}, u32[]{:S(2)}, u32[]{:S(2)}) collective-permute-start(bf16[96,256]{1,0:T(8,128)(2,1)S(1)} %get-tuple-element.87), channel_id=1, source_target_pairs={{0,32},{16,48},{32,0},{48,16},{1,33},{17,49},{33,1},{49,17},{2,34}... | collective-permute-start | bytes 147464 | tf_op jit(solution)/shard_map/ppermute | solution.py:461
  83.4 6.5 %collective-permute-start.7 = (bf16[96,256]{1,0:T(8,128)(2,1)S(1)}, bf16[96,256]{1,0:T(8,128)(2,1)S(1)}, u32[]{:S(2)}, u32[]{:S(2)}) collective-permute-start(bf16[96,256]{1,0:T(8,128)(2,1)S(1)} %get-tuple-element.88), channel_id=1, source_target_pairs={{0,48},{16,32},{32,16},{48,0},{1,49},{17,33},{33,17},{49,1},{2,50}... | collective-permute-start | bytes 147464 | tf_op jit(solution)/shard_map/ppermute | solution.py:461
  94.4 20.0 %all-to-all-start.3 = ((bf16[16,32,128]{2,1,0:T(8,128)(2,1)}), bf16[16,32,128]{2,1,0:T(8,128)(2,1)S(1)}, u32[]{:S(2)}, u32[]{:S(2)}) async-start(bf16[16,32,128]{2,1,0:T(8,128)(2,1)} %weight_sum.1), calls=%async_computation.3 | async-start | bytes 262144 | tf_op jit(solution)/shard_map/all_to_all | solution.py:451
  101.8 10.1 %collective-permute-start.8 = (bf16[8,8,1152]{2,1,0:T(8,128)(2,1)S(1)}, bf16[8,8,1152]{2,1,0:T(8,128)(2,1)S(1)}, u32[]{:S(2)}, u32[]{:S(2)}) collective-permute-start(bf16[8,8,1152]{2,1,0:T(8,128)(2,1)S(1)} %get-tuple-element.93), channel_id=1, source_target_pairs={{0,8},{8,0},{1,9},{9,1},{2,10},{10,2},{3,11},{11,3},{4,12},{12,4},... | collective-permute-start | bytes 442376 | tf_op jit(solution)/shard_map/ppermute | solution.py:455
  105.6 6.3 %collective-permute-start.9 = (bf16[96,256]{1,0:T(8,128)(2,1)S(1)}, bf16[96,256]{1,0:T(8,128)(2,1)S(1)}, u32[]{:S(2)}, u32[]{:S(2)}) collective-permute-start(bf16[96,256]{1,0:T(8,128)(2,1)S(1)} %get-tuple-element.95), channel_id=1, source_target_pairs={{0,16},{16,0},{32,48},{48,32},{1,17},{17,1},{33,49},{49,33},{2,18}... | collective-permute-start | bytes 147464 | tf_op jit(solution)/shard_map/ppermute | solution.py:461
  146.4 12.9 %all-to-all-start.5 = ((bf16[4,16,8,1024]{3,2,1,0:T(8,128)(2,1)}), bf16[4,16,8,1024]{3,2,1,0:T(8,128)(2,1)S(1)}, u32[]{:S(2)}, u32[]{:S(2)}) async-start(bf16[4,16,8,1024]{3,2,1,0:T(8,128)(2,1)} %broadcast_in_dim.23), calls=%async_computation.5 | async-start | bytes 2097152 | tf_op jit(solution)/shard_map/all_to_all | solution.py:451

commit v6 on v5

--- a/solution.py
+++ b/solution.py
@@ -223,9 +223,14 @@
     wk_ref,
     keep_ref,
     give_ref,
-    *refs,
+    kept_ref,
+    far_ref,
+    near_ref,
+    query_low,
+    out_low,
+    nope,
 ):
-    rows_refs, (query_low, out_low, nope) = refs[:TEAM], refs[TEAM:]
+    rows_refs = (kept_ref, near_ref.at[0], far_ref, near_ref.at[1])
     for group in range(2):
         lanes = slice(0, LOW_CHUNKS * CHUNK) if group == 0 else slice(LOW_CHUNKS * CHUNK, STEPS * CHUNK)
         count = group_chunks(group) * PER_CHUNK
@@ -257,10 +262,14 @@
             )
 
 
-def heads_kernel(place_ref, *refs):
-    rows_refs, (nope_ref, rope_ref, store) = refs[:TEAM], refs[TEAM:]
-    for ahead, rows_ref in enumerate(rows_refs):
-        store[member(place_ref, ahead)] = rows_ref[...]
+def relay_kernel(far_ref, near_ref, out_ref):
+    out_ref[0] = far_ref[...]
+    out_ref[1] = near_ref[1]
+
+
+def heads_kernel(place_ref, kept_ref, near_ref, far_ref, nope_ref, rope_ref, store):
+    for ahead, rows in enumerate((kept_ref[...], near_ref[0], far_ref[0], far_ref[1])):
+        store[member(place_ref, ahead)] = rows
     for head in range(TEAM):
         for half in range(2):
             toks = slice(half * STRETCH, (half + 1) * STRETCH)
@@ -297,7 +306,10 @@
                 slot = slot_of[place]
                 apart = (slot + place_ref[2]) % 2
                 lanes = scaled((slot // 2) % 2, D_LAT)
-                out_ref[:, apart, slot // 4, :, lanes] = lat[rows].reshape(4, SLICE, D_LAT).astype(BF16)
+                parts = lat[rows].reshape(4, SLICE, D_LAT).astype(BF16)
+                for line in range(4):
+                    ahead = (line + 4 - place_ref[4]) % 4
+                    out_ref[ahead, apart, slot // 4, :, lanes] = parts[line]
                 rope[half, place] = key_side[rows, D_LAT:]
 
     @pl.loop(0, PAIRS, unroll=4)
@@ -307,19 +319,20 @@
             for half, out_ref in enumerate((g_own_ref, g_other_ref)):
                 both = [rope[half, order_ref[4 * pair + 2 * parity + upper]] for parity in range(2)]
                 rows = jnp.concatenate(both, axis=1).reshape(4, SLICE, 2 * D_ROPE)
-                out_ref[:, apart, pair, :, 2 * D_LAT :] = rows.astype(BF16)
-
-
-def pair_kernel(own_ref, came_ref, out_ref):
-    total = own_ref[...].astype(F32) + came_ref[...].astype(F32)
-    out_ref[...] = total.astype(BF16)
-
-
-def line_kernel(lines_ref, keep_ref, give_ref):
+                for line in range(4):
+                    ahead = (line + 4 - place_ref[4]) % 4
+                    out_ref[ahead, apart, pair, :, 2 * D_LAT :] = rows[line].astype(BF16)
+
+
+def pair_kernel(own_ref, came_ref, *out_refs):
+    for ahead, out_ref in enumerate(out_refs):
+        out_ref[...] = (own_ref[ahead].astype(F32) + came_ref[ahead].astype(F32)).astype(BF16)
+
+
+def line_kernel(a_ref, b_ref, c_ref, d_ref, keep_ref, give_ref):
     for apart, out_ref in enumerate((keep_ref, give_ref)):
-        total = lines_ref[0, apart].astype(F32)
-        for source in range(1, 4):
-            total += lines_ref[source, apart].astype(F32)
+        total = a_ref[apart].astype(F32) + b_ref[apart].astype(F32)
+        total += c_ref[apart].astype(F32) + d_ref[apart].astype(F32)
         out_ref[...] = total.astype(BF16)
 
 
@@ -379,6 +392,7 @@
     )(*args)
 
 
+LATE = 2**35
 QUERY_SHAPE = (2, ROWS, KEY_WIDTH)
 GRAD_SHAPE = (2, ROWS, D_LAT)
 HEAD_SHAPE = (2, ROWS, D_NOPE)
@@ -415,7 +429,7 @@
         "query_side",
         2,
         (order, place, own_keys, keys, prob, score_grad, qn, go, wk),
-        ((D_LAT, D_NOPE), (D_LAT, D_NOPE)) + (rows,) * TEAM,
+        ((D_LAT, D_NOPE), (D_LAT, D_NOPE), rows, rows, (2, *rows)),
         [pltpu.VMEM(QUERY_SHAPE, BF16), pltpu.VMEM(GRAD_SHAPE, BF16), pltpu.VMEM(HEAD_SHAPE, BF16)],
         2**31,
         2**23,
@@ -464,7 +478,7 @@
 
 def local(latent, q_nope, q_rope, grad_out, w_uk, w_uv, stretch_order):
     head = lax.axis_index(PLANE + ("c",))
-    places = (Z_AXES, "c", "yh", "dp")
+    places = (Z_AXES, "c", "yh", "dp", "x")
     place = jnp.stack([lax.axis_index(axis) for axis in places]).astype(jnp.int32)
 
     mine = lax.dynamic_slice_in_dim(latent[0], head * SLICE, SLICE, 0)
@@ -486,20 +500,22 @@
     g_own, g_other = side_sums(stretch_order, place, query, grad, prob, score_grad)
     came = flip(g_other, "c")
     prob, g_own = lax.optimization_barrier((prob, g_own))
-    keep, give, *rows = query_side(stretch_order, place, own_keys, keys, prob, score_grad, qn, go, w_uk)
-
-    (pair,) = call(pair_kernel, "pair_sum", 0, (g_own, came), (g_own.shape,))
-    give, pair = lax.optimization_barrier((give, pair))
-    lines = swap(pair, "x")
-    (weights,) = call(weight_kernel, "weight_sum", 0, (keep, flip(give, "dp")), ((N_CTX, 32, D_NOPE),))
-    rows = team_swap(rows, (2, 3))
-    lines, weights, rows = lax.optimization_barrier((lines, weights, rows))
-    keep, give = call(line_kernel, "line_sum", 0, (lines,), (pair.shape[2:],) * 2)
-    give, weights = lax.optimization_barrier((give, weights))
+    keep, give, kept, far, near = query_side(stretch_order, place, own_keys, keys, prob, score_grad, qn, go, w_uk)
+
+    part = g_own.shape[1:]
+    parts = call(pair_kernel, "pair_sum", 0, (g_own, came), (part,) * 4)
+    give, near, *parts = lax.optimization_barrier((give, near, *parts))
+    near = flip(near, "z0")
+    lines = [parts[0]]
+    for ahead in (2, 1, 3):
+        lines.append(lax.ppermute(parts[ahead], "x", [(i, (i + ahead) % 4) for i in range(4)]))
+    sums = (keep, flip(give, "dp"))
+    (weights,) = call(weight_kernel, "weight_sum", 0, sums, ((N_CTX, 32, D_NOPE),), flops=LATE)
     columns = swap(weights, Z_AXES)
+    keep, give = call(line_kernel, "line_sum", 0, lines, (part[1:],) * 2, flops=LATE)
+    (relay,) = call(relay_kernel, "relay", 0, (far, near), (near.shape,))
     came = flip(give, "yh")
-    rows = team_swap(rows, (1,))
-    columns, came, rows = lax.optimization_barrier((columns, came, rows))
+    columns, came, *rows = lax.optimization_barrier((columns, came, kept, near, flip(relay, "z1")))
     (packed,) = call(pack_kernel, "pack", 0, (columns, keep, came), ((N_CTX, SLICE, 1024 + KEY_WIDTH),))
     packed = swap(packed, Z_AXES)
     nope_grad, rope_grad = put_heads(place, rows)

time: 161 us -> 161 us (level)
  waiting for transfers between devices: 25.2 us -> 20.2 us
  blocking collectives: 60.1 us -> 63.8 us
    ppermute x6 -> x3, starting transfers between devices: 20 us -> 9.21 us  [team_swap(): lax.ppermute(parts[ahead], ('z1', 'z0'), [(i, i ^ ahead) for i in range(T...]
    ppermute x0 -> x3, starting transfers between devices: none -> 9.83 us  [local(): lax.ppermute(parts[ahead], 'x', [(i, (i + ahead) % 4) for i in range(4)])]
    all_to_all x4 -> x3, waiting for transfers between devices: 17.5 us -> 10.7 us  [swap(): return lax.all_to_all(values, axes, 0, 0, tiled=True)]
    ppermute x4 -> x6, starting transfers between devices: 10.7 us -> 17.4 us  [flip(): return lax.ppermute(values, axis, [(0, 1), (1, 0)])]
    ppermute x4 -> x6, waiting for transfers between devices: 0.01 us -> 5.46 us  [flip(): return lax.ppermute(values, axis, [(0, 1), (1, 0)])]
    ppermute x6 -> x3, waiting for transfers between devices: 7.68 us -> 2.91 us  [team_swap(): lax.ppermute(parts[ahead], ('z1', 'z0'), [(i, i ^ ahead) for i in range(T...]
    all_to_all x4 -> x3, starting transfers between devices: 21.5 us -> 17 us  [swap(): return lax.all_to_all(values, axes, 0, 0, tiled=True)]
    all_to_all x2, blocking collectives: 60.1 us -> 63.8 us  [swap(): return lax.all_to_all(values, axes, 0, 0, tiled=True)]
  transfers between devices with their start and end apart: 14 -> 15, of which waited for: 8 -> 6; matrix products, arithmetic and copies ran while one was open for 0% -> 0% of each run, Pallas kernels for 6% -> 6%
where the time goes in v6:
time: 161 us; the launch traced here: 160 us
  blocking collectives  63.8 us (40%)
  starting transfers between devices  53.4 us (33%)
  waiting for transfers between devices  20.2 us (13%)
  Pallas kernels  17.3 us (11%)
  local copies, waits for them, and re-layouts  3.67 us (2%)
    all_to_all x2, blocking collectives, swap(): return lax.all_to_all(values, axes, 0, 0, tiled=True)  63.8 us
    ppermute x6, starting transfers between devices, flip(): return lax.ppermute(values, axis, [(0, 1), (1, 0)])  17.4 us
    pallas_call x13, Pallas kernels, call(): pl.pallas_call(kernel, out_shape=shapes, in_specs=[SMEM] * n_smem + [VMEM...  17.3 us
    all_to_all x3, starting transfers between devices, swap(): return lax.all_to_all(values, axes, 0, 0, tiled=True)  17 us
    all_to_all x3, waiting for transfers between devices, swap(): return lax.all_to_all(values, axes, 0, 0, tiled=True)  10.7 us
    ppermute x3, starting transfers between devices, local(): lax.ppermute(parts[ahead], 'x', [(i, (i + ahead) % 4) for i in range(4)])  9.83 us
    ppermute x3, starting transfers between devices, team_swap(): lax.ppermute(parts[ahead], ('z1', 'z0'), [(i, i ^ ahead) for i in range(T...  9.21 us
    ppermute x6, waiting for transfers between devices, flip(): return lax.ppermute(values, axis, [(0, 1), (1, 0)])  5.46 us
  transfers between devices with their start and end apart: 15, of which 6 were waited for; matrix products, arithmetic and copies ran while one was open for 0% of the time, Pallas kernels for 6%

profile of v6, /device:TPU:64, one launch (start us, length us, event | category | flops | bytes accessed | tf_op | source)
XLA Modules:
  0.0 159.9 jit_solution(5952861877394441285)
XLA Ops:
  1.8 29.4 %all_to_all.25 = bf16[16,8,576]{2,1,0:T(8,128)(2,1)S(1)} all-to-all(bf16[16,8,576]{2,1,0:T(8,128)(2,1)S(1)} %broadcast_in_dim.18), channel_id=1, replica_groups=mesh['dp'=2,'zq'=4,'z1'=2,'z0'=2,'yh'=2,'x'=4,'c'=2] {'zq','z1','z0'}, dimensions={0} | all-to-all | bytes 294912 | tf_op jit(solution)/shard_map/all_to_all | solution.py:465
  31.4 1.2 broadcast_in_dim.19
  32.6 7.1 %all-to-all-start.1 = ((bf16[8,8,8,1152]{3,2,1,0:T(8,128)(2,1)}), bf16[8,8,8,1152]{3,2,1,0:T(8,128)(2,1)S(1)}, u32[]{:S(2)}, u32[]{:S(2)}) async-start(bf16[8,8,8,1152]{3,2,1,0:T(8,128)(2,1)} %broadcast_in_dim.19), calls=%async_computation.1 | async-start | bytes 2359296 | tf_op jit(solution)/shard_map/all_to_all | solution.py:465
  40.6 2.7 %collective-permute-start = (bf16[160,256]{1,0:T(8,128)(2,1)S(1)}, bf16[160,256]{1,0:T(8,128)(2,1)S(1)}, u32[]{:S(2)}, u32[]{:S(2)}) collective-permute-start(bf16[160,256]{1,0:T(8,128)(2,1)S(1)} %get-tuple-element.56), channel_id=1, source_target_pairs={{0,16},{16,0},{32,48},{48,32},{1,17},{17,1},{33,49},{49,33},{2,18}... | collective-permute-start | bytes 245768 | tf_op jit(solution)/shard_map/ppermute | solution.py:475
  43.3 3.1 %collective-permute-start.1 = (bf16[160,256]{1,0:T(8,128)(2,1)S(1)}, bf16[160,256]{1,0:T(8,128)(2,1)S(1)}, u32[]{:S(2)}, u32[]{:S(2)}) collective-permute-start(bf16[160,256]{1,0:T(8,128)(2,1)S(1)} %get-tuple-element.57), channel_id=1, source_target_pairs={{0,32},{16,48},{32,0},{48,16},{1,33},{17,49},{33,1},{49,17},{2,34}... | collective-permute-start | bytes 245768 | tf_op jit(solution)/shard_map/ppermute | solution.py:475
  46.4 3.4 %collective-permute-start.2 = (bf16[160,256]{1,0:T(8,128)(2,1)S(1)}, bf16[160,256]{1,0:T(8,128)(2,1)S(1)}, u32[]{:S(2)}, u32[]{:S(2)}) collective-permute-start(bf16[160,256]{1,0:T(8,128)(2,1)S(1)} %get-tuple-element.58), channel_id=1, source_target_pairs={{0,48},{16,32},{32,16},{48,0},{1,49},{17,33},{33,17},{49,1},{2,50}... | collective-permute-start | bytes 245768 | tf_op jit(solution)/shard_map/ppermute | solution.py:475
  49.8 0.9 collective-permute-done.1.refs_2_
  50.7 2.0 %collective-permute-done.2.refs_3_ = bf16[160,256]{1,0:T(8,128)(2,1)S(1)} collective-permute-done((bf16[160,256]{1,0:T(8,128)(2,1)S(1)}, bf16[160,256]{1,0:T(8,128)(2,1)S(1)}, u32[]{:S(2)}, u32[]{:S(2)}) %collective-permute-start.2) | collective-permute-done | bytes 81952 | tf_op jit(solution)/shard_map/ppermute | solution.py:475
  52.7 3.3 %all-to-all-done.1 = bf16[8,8,8,1152]{3,2,1,0:T(8,128)(2,1)S(1)} async-done(((bf16[8,8,8,1152]{3,2,1,0:T(8,128)(2,1)}), bf16[8,8,8,1152]{3,2,1,0:T(8,128)(2,1)S(1)}, u32[]{:S(2)}, u32[]{:S(2)}) %all-to-all-start.1) | async-done | bytes 1179680 | tf_op jit(solution)/shard_map/all_to_all | solution.py:465
  56.0 1.9 %collective-permute-start.3 = (bf16[2,4,8,8,1152]{4,3,2,1,0:T(8,128)(2,1)S(1)}, bf16[2,4,8,8,1152]{4,3,2,1,0:T(8,128)(2,1)S(1)}, u32[]{:S(2)}, u32[]{:S(2)}) collective-permute-start(bf16[2,4,8,8,1152]{4,3,2,1,0:T(8,128)(2,1)S(1)} %bitcast.22), channel_id=1, source_target_pairs={{0,1},{1,0},{2,3},{3,2},{4,5},{5,4},{6,7},{7,6},{8,9},{9,8},{10,11... | collective-permute-start | bytes 3538952 | tf_op jit(solution)/shard_map/ppermute | solution.py:469
  57.9 1.0 query_latents.1
  58.9 2.0 %own_scores.1 = (bf16[32,32,576]{2,1,0:T(8,128)(2,1)S(1)}, f32[256,1536]{1,0:T(8,128)S(1)}, f32[256,1536]{1,0:T(8,128)S(1)}, f32[2,256,128]{2,1,0:T(8,128)S(1)}) custom-call(s32[32]{0:T(128)S(1)} %copy-done.6, s32[5]{0:T(128)S(1)} %stack.23.place_ref, bf16[2,4,8,8,1152]{4,3,2,1,0:T(8,128)(2,1)S(1)} %bitcast.23, ...), custom_call_target="tpu_custom_call" | custom-call | flops 1073741824 | bytes 4194304 | tf_op jit(solution)/shard_map/own_scores/pallas_call | solution.py:383
  60.9 3.1 %scores.1 = (bf16[32,32,576]{2,1,0:T(8,128)(2,1)S(1)}, bf16[2,256,1536]{2,1,0:T(8,128)(2,1)S(1)}, bf16[2,256,1536]{2,1,0:T(8,128)(2,1)S(1)}) custom-call(s32[32]{0:T(128)S(1)} %copy-done.6, s32[5]{0:T(128)S(1)} %stack.23.place_ref, bf16[2,4,8,8,1152]{4,3,2,1,0:T(8,128)(2,1)S(1)} %collective-permute-done.3.other_ref, ...), custom_call_target="tpu_custom_call" | custom-call | flops 2147483648 | bytes 8388608 | tf_op jit(solution)/shard_map/scores/pallas_call | solution.py:383
  64.1 3.2 %key_side.1 = (bf16[4,2,8,8,1152]{4,3,2,1,0:T(8,128)(2,1)S(1)}, bf16[4,2,8,8,1152]{4,3,2,1,0:T(8,128)(2,1)S(1)}) custom-call(s32[32]{0:T(128)S(1)} %copy-done.6, s32[5]{0:T(128)S(1)} %stack.23.place_ref, bf16[2,256,576]{2,1,0:T(8,128)(2,1)S(1)} %get-tuple-element.64.query, bf16[2,256,512]{2,1,0:T(8,128)(2,1)S(1)} %get-tuple-element.65.grad, ...), custom_call_target="tpu_custom_call" | custom-call | flops 2147483648 | bytes 8388608 | tf_op jit(solution)/shard_map/key_side/pallas_call | solution.py:383
  67.2 2.4 %collective-permute-start.4 = (bf16[4,2,8,8,1152]{4,3,2,1,0:T(8,128)(2,1)S(1)}, bf16[4,2,8,8,1152]{4,3,2,1,0:T(8,128)(2,1)S(1)}, u32[]{:S(2)}, u32[]{:S(2)}) collective-permute-start(bf16[4,2,8,8,1152]{4,3,2,1,0:T(8,128)(2,1)S(1)} %get-tuple-element.81), channel_id=1, source_target_pairs={{0,1},{1,0},{2,3},{3,2},{4,5},{5,4},{6,7},{7,6},{8,9},{9,8},{10,11... | collective-permute-start | bytes 3538952 | tf_op jit(solution)/shard_map/ppermute | solution.py:469
  69.6 3.2 %query_side.1 = (bf16[512,128]{1,0:T(8,128)(2,1)S(1)}, bf16[512,128]{1,0:T(8,128)(2,1)S(1)}, bf16[96,256]{1,0:T(8,128)(2,1)S(1)}, bf16[96,256]{1,0:T(8,128)(2,1)S(1)}, bf16[2,96,256]{2,1,0:T(8,128)(2,1)S(1)}) custom-call(s32[32]{0:T(128)S(1)} %copy-done.6, s32[5]{0:T(128)S(1)} %stack.23.place_ref, bf16[32,32,576]{2,1,0:T(8,128)(2,1)S(1)} %get-tuple-element.66.own_keys, ...), custom_call_target="tpu_custom_call" | custom-call | flops 2147483648 | bytes 8388608 | tf_op jit(solution)/shard_map/query_side/pallas_call | solution.py:383
  73.2 2.6 %collective-permute-start.5 = (bf16[512,128]{1,0:T(8,128)(2,1)S(1)}, bf16[512,128]{1,0:T(8,128)(2,1)S(1)}, u32[]{:S(2)}, u32[]{:S(2)}) collective-permute-start(bf16[512,128]{1,0:T(8,128)(2,1)S(1)} %get-tuple-element.86), channel_id=1, source_target_pairs={{0,256},{256,0},{1,257},{257,1},{2,258},{258,2},{3,259},{259,3},{4... | collective-permute-start | bytes 393224 | tf_op jit(solution)/shard_map/ppermute | solution.py:469
  75.8 4.0 %collective-permute-start.10 = (bf16[2,96,256]{2,1,0:T(8,128)(2,1)S(1)}, bf16[2,96,256]{2,1,0:T(8,128)(2,1)S(1)}, u32[]{:S(2)}, u32[]{:S(2)}) collective-permute-start(bf16[2,96,256]{2,1,0:T(8,128)(2,1)S(1)} %get-tuple-element.93), channel_id=1, source_target_pairs={{0,16},{16,0},{1,17},{17,1},{2,18},{18,2},{3,19},{19,3},{4,20},{20... | collective-permute-start | bytes 294920 | tf_op jit(solution)/shard_map/ppermute | solution.py:469
  79.8 2.8 %collective-permute-start.6 = (bf16[2,8,8,1152]{3,2,1,0:T(8,128)(2,1)S(1)}, bf16[2,8,8,1152]{3,2,1,0:T(8,128)(2,1)S(1)}, u32[]{:S(2)}, u32[]{:S(2)}) collective-permute-start(bf16[2,8,8,1152]{3,2,1,0:T(8,128)(2,1)S(1)} %get-tuple-element.88), channel_id=1, source_target_pairs={{0,4},{2,6},{4,0},{6,2},{1,5},{3,7},{5,1},{7,3},{8,12},{10,14},{12... | collective-permute-start | bytes 884744 | tf_op jit(solution)/shard_map/ppermute | solution.py:511
  82.6 2.5 %collective-permute-start.7 = (bf16[2,8,8,1152]{3,2,1,0:T(8,128)(2,1)S(1)}, bf16[2,8,8,1152]{3,2,1,0:T(8,128)(2,1)S(1)}, u32[]{:S(2)}, u32[]{:S(2)}) collective-permute-start(bf16[2,8,8,1152]{3,2,1,0:T(8,128)(2,1)S(1)} %get-tuple-element.89), channel_id=1, source_target_pairs={{0,2},{2,4},{4,6},{6,0},{1,3},{3,5},{5,7},{7,1},{8,10},{10,12},{12... | collective-permute-start | bytes 884744 | tf_op jit(solution)/shard_map/ppermute | solution.py:511
  85.1 4.6 %collective-permute-start.8 = (bf16[2,8,8,1152]{3,2,1,0:T(8,128)(2,1)S(1)}, bf16[2,8,8,1152]{3,2,1,0:T(8,128)(2,1)S(1)}, u32[]{:S(2)}, u32[]{:S(2)}) collective-permute-start(bf16[2,8,8,1152]{3,2,1,0:T(8,128)(2,1)S(1)} %get-tuple-element.90), channel_id=1, source_target_pairs={{0,6},{2,0},{4,2},{6,4},{1,7},{3,1},{5,3},{7,5},{8,14},{10,8},{12,... | collective-permute-start | bytes 884744 | tf_op jit(solution)/shard_map/ppermute | solution.py:511
  90.4 6.4 %all-to-all-start.2 = ((bf16[16,32,128]{2,1,0:T(8,128)(2,1)}), bf16[16,32,128]{2,1,0:T(8,128)(2,1)S(1)}, u32[]{:S(2)}, u32[]{:S(2)}) async-start(bf16[16,32,128]{2,1,0:T(8,128)(2,1)} %weight_sum.1), calls=%async_computation.2 | async-start | bytes 262144 | tf_op jit(solution)/shard_map/all_to_all | solution.py:465
  96.8 1.1 collective-permute-done.7.c_ref
  98.1 4.4 %collective-permute-start.9 = (bf16[8,8,1152]{2,1,0:T(8,128)(2,1)S(1)}, bf16[8,8,1152]{2,1,0:T(8,128)(2,1)S(1)}, u32[]{:S(2)}, u32[]{:S(2)}) collective-permute-start(bf16[8,8,1152]{2,1,0:T(8,128)(2,1)S(1)} %get-tuple-element.91), channel_id=1, source_target_pairs={{0,8},{8,0},{1,9},{9,1},{2,10},{10,2},{3,11},{11,3},{4,12},{12,4},... | collective-permute-start | bytes 442376 | tf_op jit(solution)/shard_map/ppermute | solution.py:469
  102.5 2.1 %collective-permute-start.11 = (bf16[2,96,256]{2,1,0:T(8,128)(2,1)S(1)}, bf16[2,96,256]{2,1,0:T(8,128)(2,1)S(1)}, u32[]{:S(2)}, u32[]{:S(2)}) collective-permute-start(bf16[2,96,256]{2,1,0:T(8,128)(2,1)S(1)} %relay.1), channel_id=1, source_target_pairs={{0,32},{32,0},{1,33},{33,1},{2,34},{34,2},{3,35},{35,3},{4,36},{36... | collective-permute-start | bytes 294920 | tf_op jit(solution)/shard_map/ppermute | solution.py:469
  104.6 5.4 %collective-permute-done.11.far_ref = bf16[2,96,256]{2,1,0:T(8,128)(2,1)S(1)} collective-permute-done((bf16[2,96,256]{2,1,0:T(8,128)(2,1)S(1)}, bf16[2,96,256]{2,1,0:T(8,128)(2,1)S(1)}, u32[]{:S(2)}, u32[]{:S(2)}) %collective-permute-start.11) | collective-permute-done | bytes 98336 | tf_op jit(solution)/shard_map/ppermute | solution.py:469
  110.1 34.3 %all_to_all.26 = bf16[16,8,1600]{2,1,0:T(8,128)(2,1)S(1)} all-to-all(bf16[16,8,1600]{2,1,0:T(8,128)(2,1)S(1)} %pack.1), channel_id=1, replica_groups=mesh['dp'=2,'zq'=4,'z1'=2,'z0'=2,'yh'=2,'x'=4,'c'=2] {'zq','z1','z0'}, dimensions={0} | all-to-all | bytes 819200 | tf_op jit(solution)/shard_map/all_to_all | solution.py:465
  144.5 1.1 broadcast_in_dim.23
  145.6 3.5 %all-to-all-start.4 = ((bf16[4,16,8,1024]{3,2,1,0:T(8,128)(2,1)}), bf16[4,16,8,1024]{3,2,1,0:T(8,128)(2,1)S(1)}, u32[]{:S(2)}, u32[]{:S(2)}) async-start(bf16[4,16,8,1024]{3,2,1,0:T(8,128)(2,1)} %broadcast_in_dim.23), calls=%async_computation.4 | async-start | bytes 2097152 | tf_op jit(solution)/shard_map/all_to_all | solution.py:465
  149.1 1.4 put_heads.1
  151.1 7.4 %all-to-all-done.4.whole_ref = bf16[4,16,8,1024]{3,2,1,0:T(8,128)(2,1)S(1)} async-done(((bf16[4,16,8,1024]{3,2,1,0:T(8,128)(2,1)}), bf16[4,16,8,1024]{3,2,1,0:T(8,128)(2,1)S(1)}, u32[]{:S(2)}, u32[]{:S(2)}) %all-to-all-start.4) | async-done | bytes 1048608 | tf_op jit(solution)/shard_map/all_to_all | solution.py:465
  158.5 1.4 spread.1
  (41 shorter events, 4.1 us)
Async XLA Ops:
  0.6 0.9 copy-start
  32.6 7.2 %copy-start.3 = (bf16[1,128,512]{2,1,0:T(8,128)(2,1)S(1)}, bf16[1,128,512]{2,1,0:T(8,128)(2,1)}, u32[]{:S(2)}) copy-start(bf16[1,128,512]{2,1,0:T(8,128)(2,1)} %param.8) | copy-start | bytes 393220
  32.6 7.2 %copy-start.4 = (bf16[1,128,512]{2,1,0:T(8,128)(2,1)S(1)}, bf16[1,128,512]{2,1,0:T(8,128)(2,1)}, u32[]{:S(2)}) copy-start(bf16[1,128,512]{2,1,0:T(8,128)(2,1)} %param.10) | copy-start | bytes 393220
  32.6 7.2 %copy-start.5 = (bf16[1,128,256]{2,1,0:T(8,128)(2,1)S(1)}, bf16[1,128,256]{2,1,0:T(8,128)(2,1)}, u32[]{:S(2)}) copy-start(bf16[1,128,256]{2,1,0:T(8,128)(2,1)} %param.9) | copy-start | bytes 196612
  32.6 25.3 %copy-start.1 = (bf16[512,512]{1,0:T(8,128)(2,1)S(1)}, bf16[512,512]{1,0:T(8,128)(2,1)}, u32[]{:S(2)}) copy-start(bf16[512,512]{1,0:T(8,128)(2,1)} %refs_5_.1) | copy-start | bytes 1572868
  32.6 25.3 %copy-start.2 = (bf16[512,512]{1,0:T(8,128)(2,1)S(1)}, bf16[512,512]{1,0:T(8,128)(2,1)}, u32[]{:S(2)}) copy-start(bf16[512,512]{1,0:T(8,128)(2,1)} %wk_ref.1) | copy-start | bytes 1572868
  32.6 25.3 %copy-start.6 = (s32[32]{0:T(128)S(1)}, s32[32]{0:T(128)}, u32[]{:S(2)}) copy-start(s32[32]{0:T(128)} %order_ref.9) | copy-start | bytes 388
  32.6 23.3 %all-to-all-start.1 = ((bf16[8,8,8,1152]{3,2,1,0:T(8,128)(2,1)}), bf16[8,8,8,1152]{3,2,1,0:T(8,128)(2,1)S(1)}, u32[]{:S(2)}, u32[]{:S(2)}) async-start(bf16[8,8,8,1152]{3,2,1,0:T(8,128)(2,1)} %broadcast_in_dim.19), calls=%async_computation.1 | async-start | bytes 2359296 | tf_op jit(solution)/shard_map/all_to_all | solution.py:465
  40.6 9.2 %collective-permute-start = (bf16[160,256]{1,0:T(8,128)(2,1)S(1)}, bf16[160,256]{1,0:T(8,128)(2,1)S(1)}, u32[]{:S(2)}, u32[]{:S(2)}) collective-permute-start(bf16[160,256]{1,0:T(8,128)(2,1)S(1)} %get-tuple-element.56), channel_id=1, source_target_pairs={{0,16},{16,0},{32,48},{48,32},{1,17},{17,1},{33,49},{49,33},{2,18}... | collective-permute-start | bytes 245768 | tf_op jit(solution)/shard_map/ppermute | solution.py:475
  43.3 7.4 %collective-permute-start.1 = (bf16[160,256]{1,0:T(8,128)(2,1)S(1)}, bf16[160,256]{1,0:T(8,128)(2,1)S(1)}, u32[]{:S(2)}, u32[]{:S(2)}) collective-permute-start(bf16[160,256]{1,0:T(8,128)(2,1)S(1)} %get-tuple-element.57), channel_id=1, source_target_pairs={{0,32},{16,48},{32,0},{48,16},{1,33},{17,49},{33,1},{49,17},{2,34}... | collective-permute-start | bytes 245768 | tf_op jit(solution)/shard_map/ppermute | solution.py:475
  46.4 6.3 %collective-permute-start.2 = (bf16[160,256]{1,0:T(8,128)(2,1)S(1)}, bf16[160,256]{1,0:T(8,128)(2,1)S(1)}, u32[]{:S(2)}, u32[]{:S(2)}) collective-permute-start(bf16[160,256]{1,0:T(8,128)(2,1)S(1)} %get-tuple-element.58), channel_id=1, source_target_pairs={{0,48},{16,32},{32,16},{48,0},{1,49},{17,33},{33,17},{49,1},{2,50}... | collective-permute-start | bytes 245768 | tf_op jit(solution)/shard_map/ppermute | solution.py:475
  56.0 5.0 %collective-permute-start.3 = (bf16[2,4,8,8,1152]{4,3,2,1,0:T(8,128)(2,1)S(1)}, bf16[2,4,8,8,1152]{4,3,2,1,0:T(8,128)(2,1)S(1)}, u32[]{:S(2)}, u32[]{:S(2)}) collective-permute-start(bf16[2,4,8,8,1152]{4,3,2,1,0:T(8,128)(2,1)S(1)} %bitcast.22), channel_id=1, source_target_pairs={{0,1},{1,0},{2,3},{3,2},{4,5},{5,4},{6,7},{7,6},{8,9},{9,8},{10,11... | collective-permute-start | bytes 3538952 | tf_op jit(solution)/shard_map/ppermute | solution.py:469
  67.2 5.6 %collective-permute-start.4 = (bf16[4,2,8,8,1152]{4,3,2,1,0:T(8,128)(2,1)S(1)}, bf16[4,2,8,8,1152]{4,3,2,1,0:T(8,128)(2,1)S(1)}, u32[]{:S(2)}, u32[]{:S(2)}) collective-permute-start(bf16[4,2,8,8,1152]{4,3,2,1,0:T(8,128)(2,1)S(1)} %get-tuple-element.81), channel_id=1, source_target_pairs={{0,1},{1,0},{2,3},{3,2},{4,5},{5,4},{6,7},{7,6},{8,9},{9,8},{10,11... | collective-permute-start | bytes 3538952 | tf_op jit(solution)/shard_map/ppermute | solution.py:469
  73.2 16.5 %collective-permute-start.5 = (bf16[512,128]{1,0:T(8,128)(2,1)S(1)}, bf16[512,128]{1,0:T(8,128)(2,1)S(1)}, u32[]{:S(2)}, u32[]{:S(2)}) collective-permute-start(bf16[512,128]{1,0:T(8,128)(2,1)S(1)} %get-tuple-element.86), channel_id=1, source_target_pairs={{0,256},{256,0},{1,257},{257,1},{2,258},{258,2},{3,259},{259,3},{4... | collective-permute-start | bytes 393224 | tf_op jit(solution)/shard_map/ppermute | solution.py:469
  75.8 26.7 %collective-permute-start.10 = (bf16[2,96,256]{2,1,0:T(8,128)(2,1)S(1)}, bf16[2,96,256]{2,1,0:T(8,128)(2,1)S(1)}, u32[]{:S(2)}, u32[]{:S(2)}) collective-permute-start(bf16[2,96,256]{2,1,0:T(8,128)(2,1)S(1)} %get-tuple-element.93), channel_id=1, source_target_pairs={{0,16},{16,0},{1,17},{17,1},{2,18},{18,2},{3,19},{19,3},{4,20},{20... | collective-permute-start | bytes 294920 | tf_op jit(solution)/shard_map/ppermute | solution.py:469
  79.8 17.0 %collective-permute-start.6 = (bf16[2,8,8,1152]{3,2,1,0:T(8,128)(2,1)S(1)}, bf16[2,8,8,1152]{3,2,1,0:T(8,128)(2,1)S(1)}, u32[]{:S(2)}, u32[]{:S(2)}) collective-permute-start(bf16[2,8,8,1152]{3,2,1,0:T(8,128)(2,1)S(1)} %get-tuple-element.88), channel_id=1, source_target_pairs={{0,4},{2,6},{4,0},{6,2},{1,5},{3,7},{5,1},{7,3},{8,12},{10,14},{12... | collective-permute-start | bytes 884744 | tf_op jit(solution)/shard_map/ppermute | solution.py:511
  82.6 15.3 %collective-permute-start.7 = (bf16[2,8,8,1152]{3,2,1,0:T(8,128)(2,1)S(1)}, bf16[2,8,8,1152]{3,2,1,0:T(8,128)(2,1)S(1)}, u32[]{:S(2)}, u32[]{:S(2)}) collective-permute-start(bf16[2,8,8,1152]{3,2,1,0:T(8,128)(2,1)S(1)} %get-tuple-element.89), channel_id=1, source_target_pairs={{0,2},{2,4},{4,6},{6,0},{1,3},{3,5},{5,7},{7,1},{8,10},{10,12},{12... | collective-permute-start | bytes 884744 | tf_op jit(solution)/shard_map/ppermute | solution.py:511
  85.1 12.8 %collective-permute-start.8 = (bf16[2,8,8,1152]{3,2,1,0:T(8,128)(2,1)S(1)}, bf16[2,8,8,1152]{3,2,1,0:T(8,128)(2,1)S(1)}, u32[]{:S(2)}, u32[]{:S(2)}) collective-permute-start(bf16[2,8,8,1152]{3,2,1,0:T(8,128)(2,1)S(1)} %get-tuple-element.90), channel_id=1, source_target_pairs={{0,6},{2,0},{4,2},{6,4},{1,7},{3,1},{5,3},{7,5},{8,14},{10,8},{12,... | collective-permute-start | bytes 884744 | tf_op jit(solution)/shard_map/ppermute | solution.py:511
  90.4 19.6 %all-to-all-start.2 = ((bf16[16,32,128]{2,1,0:T(8,128)(2,1)}), bf16[16,32,128]{2,1,0:T(8,128)(2,1)S(1)}, u32[]{:S(2)}, u32[]{:S(2)}) async-start(bf16[16,32,128]{2,1,0:T(8,128)(2,1)} %weight_sum.1), calls=%async_computation.2 | async-start | bytes 262144 | tf_op jit(solution)/shard_map/all_to_all | solution.py:465
  98.1 11.9 %collective-permute-start.9 = (bf16[8,8,1152]{2,1,0:T(8,128)(2,1)S(1)}, bf16[8,8,1152]{2,1,0:T(8,128)(2,1)S(1)}, u32[]{:S(2)}, u32[]{:S(2)}) collective-permute-start(bf16[8,8,1152]{2,1,0:T(8,128)(2,1)S(1)} %get-tuple-element.91), channel_id=1, source_target_pairs={{0,8},{8,0},{1,9},{9,1},{2,10},{10,2},{3,11},{11,3},{4,12},{12,4},... | collective-permute-start | bytes 442376 | tf_op jit(solution)/shard_map/ppermute | solution.py:469
  102.5 7.5 %collective-permute-start.11 = (bf16[2,96,256]{2,1,0:T(8,128)(2,1)S(1)}, bf16[2,96,256]{2,1,0:T(8,128)(2,1)S(1)}, u32[]{:S(2)}, u32[]{:S(2)}) collective-permute-start(bf16[2,96,256]{2,1,0:T(8,128)(2,1)S(1)} %relay.1), channel_id=1, source_target_pairs={{0,32},{32,0},{1,33},{33,1},{2,34},{34,2},{3,35},{35,3},{4,36},{36... | collective-permute-start | bytes 294920 | tf_op jit(solution)/shard_map/ppermute | solution.py:469
  145.6 12.9 %all-to-all-start.4 = ((bf16[4,16,8,1024]{3,2,1,0:T(8,128)(2,1)}), bf16[4,16,8,1024]{3,2,1,0:T(8,128)(2,1)S(1)}, u32[]{:S(2)}, u32[]{:S(2)}) async-start(bf16[4,16,8,1024]{3,2,1,0:T(8,128)(2,1)} %broadcast_in_dim.23), calls=%async_computation.4 | async-start | bytes 2097152 | tf_op jit(solution)/shard_map/all_to_all | solution.py:465

commit v7 on v6

--- a/solution.py
+++ b/solution.py
@@ -308,8 +308,8 @@
                 lanes = scaled((slot // 2) % 2, D_LAT)
                 parts = lat[rows].reshape(4, SLICE, D_LAT).astype(BF16)
                 for line in range(4):
-                    ahead = (line + 4 - place_ref[4]) % 4
-                    out_ref[ahead, apart, slot // 4, :, lanes] = parts[line]
+                    ahead = line ^ place_ref[4]
+                    out_ref[ahead % 2, ahead // 2, apart, slot // 4, :, lanes] = parts[line]
                 rope[half, place] = key_side[rows, D_LAT:]
 
     @pl.loop(0, PAIRS, unroll=4)
@@ -320,8 +320,8 @@
                 both = [rope[half, order_ref[4 * pair + 2 * parity + upper]] for parity in range(2)]
                 rows = jnp.concatenate(both, axis=1).reshape(4, SLICE, 2 * D_ROPE)
                 for line in range(4):
-                    ahead = (line + 4 - place_ref[4]) % 4
-                    out_ref[ahead, apart, pair, :, 2 * D_LAT :] = rows[line].astype(BF16)
+                    ahead = line ^ place_ref[4]
+                    out_ref[ahead % 2, ahead // 2, apart, pair, :, 2 * D_LAT :] = rows[line].astype(BF16)
 
 
 def pair_kernel(own_ref, came_ref, *out_refs):
@@ -329,10 +329,10 @@
         out_ref[...] = (own_ref[ahead].astype(F32) + came_ref[ahead].astype(F32)).astype(BF16)
 
 
-def line_kernel(a_ref, b_ref, c_ref, d_ref, keep_ref, give_ref):
-    for apart, out_ref in enumerate((keep_ref, give_ref)):
-        total = a_ref[apart].astype(F32) + b_ref[apart].astype(F32)
-        total += c_ref[apart].astype(F32) + d_ref[apart].astype(F32)
+def line_kernel(keep_ref, came_ref, *out_refs):
+    for index, out_ref in enumerate(out_refs):
+        across, apart = index // 2, index % 2
+        total = keep_ref[across, apart].astype(F32) + came_ref[across, apart].astype(F32)
         out_ref[...] = total.astype(BF16)
 
 
@@ -341,7 +341,7 @@
     out_ref[...] = total.astype(BF16).reshape(out_ref.shape)
 
 
-def pack_kernel(columns_ref, keep_ref, came_ref, out_ref):
+def pack_kernel(columns_ref, a_ref, b_ref, c_ref, d_ref, out_ref):
     pieces = []
     for head in range(TEAM):
         total = columns_ref[head].astype(F32)
@@ -354,7 +354,8 @@
             for octet in range(4):
                 lanes = slice((4 * pick + octet) * 128, (4 * pick + octet + 1) * 128)
                 out_ref[target, :, lanes] = piece[octet * SLICE : (octet + 1) * SLICE].astype(BF16)
-    side = (keep_ref[...].astype(F32) + came_ref[...].astype(F32)).astype(BF16)
+    side = a_ref[...].astype(F32) + b_ref[...].astype(F32)
+    side = (side + c_ref[...].astype(F32) + d_ref[...].astype(F32)).astype(BF16)
     for pair in range(PAIRS):
         for parity in range(2):
             out_ref[2 * pair + parity, :, 1024 : 1024 + D_LAT] = side[pair, :, lat_lanes(parity)]
@@ -448,7 +449,7 @@
 
 
 def side_sums(order, place, query, grad, prob, score_grad):
-    part = (4, 2, PAIRS, SLICE, WIDE)
+    part = (2, 2, 2, PAIRS, SLICE, WIDE)
     return call(
         side_kernel,
         "key_side",
@@ -503,20 +504,21 @@
     keep, give, kept, far, near = query_side(stretch_order, place, own_keys, keys, prob, score_grad, qn, go, w_uk)
 
     part = g_own.shape[1:]
-    parts = call(pair_kernel, "pair_sum", 0, (g_own, came), (part,) * 4)
+    parts = call(pair_kernel, "pair_sum", 0, (g_own, came), (part,) * 2)
     give, near, *parts = lax.optimization_barrier((give, near, *parts))
+    beside = lax.ppermute(parts[1], "x", [(i, i ^ 1) for i in range(4)])
     near = flip(near, "z0")
-    lines = [parts[0]]
-    for ahead in (2, 1, 3):
-        lines.append(lax.ppermute(parts[ahead], "x", [(i, (i + ahead) % 4) for i in range(4)]))
     sums = (keep, flip(give, "dp"))
     (weights,) = call(weight_kernel, "weight_sum", 0, sums, ((N_CTX, 32, D_NOPE),), flops=LATE)
     columns = swap(weights, Z_AXES)
-    keep, give = call(line_kernel, "line_sum", 0, lines, (part[1:],) * 2, flops=LATE)
+    lines = call(line_kernel, "line_sum", 0, (parts[0], beside), (part[2:],) * 4, flops=LATE)
     (relay,) = call(relay_kernel, "relay", 0, (far, near), (near.shape,))
-    came = flip(give, "yh")
-    columns, came, *rows = lax.optimization_barrier((columns, came, kept, near, flip(relay, "z1")))
-    (packed,) = call(pack_kernel, "pack", 0, (columns, keep, came), ((N_CTX, SLICE, 1024 + KEY_WIDTH),))
+    sides = [lines[0]]
+    for ahead, share in ((6, lines[3]), (2, lines[2]), (4, lines[1])):
+        sides.append(lax.ppermute(share, PLANE, [(i, i ^ ahead) for i in range(8)]))
+    columns, *rest = lax.optimization_barrier((columns, *sides, kept, near, flip(relay, "z1")))
+    sides, rows = rest[:4], rest[4:]
+    (packed,) = call(pack_kernel, "pack", 0, (columns, *sides), ((N_CTX, SLICE, 1024 + KEY_WIDTH),))
     packed = swap(packed, Z_AXES)
     nope_grad, rope_grad = put_heads(place, rows)
     d_latent = jnp.sum(packed[:, :, 1024:].astype(F32), axis=0)

time: 161 us -> 161 us (level)
  the two profiles are of different devices: /device:TPU:64 before, /device:TPU:8 now
where the time goes in v7:
time: 161 us
  starting transfers between devices  57.5 us (36%)
  blocking collectives  57.1 us (35%)
  waiting for transfers between devices  23.2 us (14%)
  Pallas kernels  17.6 us (11%)
  local copies, waits for them, and re-layouts  3.67 us (2%)
    all_to_all x2, blocking collectives, swap(): return lax.all_to_all(values, axes, 0, 0, tiled=True)  57.1 us
    pallas_call x13, Pallas kernels, call(): pl.pallas_call(kernel, out_shape=shapes, in_specs=[SMEM] * n_smem + [VMEM...  17.6 us
    all_to_all x3, starting transfers between devices, swap(): return lax.all_to_all(values, axes, 0, 0, tiled=True)  16.2 us
    ppermute x5, starting transfers between devices, flip(): return lax.ppermute(values, axis, [(0, 1), (1, 0)])  16.1 us
    ppermute x3, starting transfers between devices, local(): sides.append(lax.ppermute(share, PLANE, [(i, i ^ ahead) for i in range(8)]))  12.2 us
    ppermute x3, starting transfers between devices, team_swap(): lax.ppermute(parts[ahead], ('z1', 'z0'), [(i, i ^ ahead) for i in range(T...  10.1 us
    ppermute x1, waiting for transfers between devices, local(): beside = lax.ppermute(parts[1], 'x', [(i, i ^ 1) for i in range(4)])  7.61 us
    all_to_all x3, waiting for transfers between devices, swap(): return lax.all_to_all(values, axes, 0, 0, tiled=True)  6.89 us
  transfers between devices with their start and end apart: 15, of which 5 were waited for; matrix products, arithmetic and copies ran while one was open for 0% of the time, Pallas kernels for 6%

profile of v7, /device:TPU:8, one launch (start us, length us, event | category | flops | bytes accessed | tf_op | source)
XLA Modules:
  0.0 160.6 jit_solution(1189012099888364582)
XLA Ops:
  0.7 0.9 copy-done
  1.8 30.6 %all_to_all.25 = bf16[16,8,576]{2,1,0:T(8,128)(2,1)S(1)} all-to-all(bf16[16,8,576]{2,1,0:T(8,128)(2,1)S(1)} %broadcast_in_dim.18), channel_id=1, replica_groups=mesh['dp'=2,'zq'=4,'z1'=2,'z0'=2,'yh'=2,'x'=4,'c'=2] {'zq','z1','z0'}, dimensions={0} | all-to-all | bytes 294912 | tf_op jit(solution)/shard_map/all_to_all | solution.py:466
  32.6 1.2 broadcast_in_dim.19
  33.8 6.2 %all-to-all-start.1 = ((bf16[8,8,8,1152]{3,2,1,0:T(8,128)(2,1)}), bf16[8,8,8,1152]{3,2,1,0:T(8,128)(2,1)S(1)}, u32[]{:S(2)}, u32[]{:S(2)}) async-start(bf16[8,8,8,1152]{3,2,1,0:T(8,128)(2,1)} %broadcast_in_dim.19), calls=%async_computation.1 | async-start | bytes 2359296 | tf_op jit(solution)/shard_map/all_to_all | solution.py:466
  40.8 3.1 %collective-permute-start = (bf16[160,256]{1,0:T(8,128)(2,1)S(1)}, bf16[160,256]{1,0:T(8,128)(2,1)S(1)}, u32[]{:S(2)}, u32[]{:S(2)}) collective-permute-start(bf16[160,256]{1,0:T(8,128)(2,1)S(1)} %get-tuple-element.57), channel_id=1, source_target_pairs={{0,16},{16,0},{32,48},{48,32},{1,17},{17,1},{33,49},{49,33},{2,18}... | collective-permute-start | bytes 245768 | tf_op jit(solution)/shard_map/ppermute | solution.py:476
  43.9 3.7 %collective-permute-start.1 = (bf16[160,256]{1,0:T(8,128)(2,1)S(1)}, bf16[160,256]{1,0:T(8,128)(2,1)S(1)}, u32[]{:S(2)}, u32[]{:S(2)}) collective-permute-start(bf16[160,256]{1,0:T(8,128)(2,1)S(1)} %get-tuple-element.58), channel_id=1, source_target_pairs={{0,32},{16,48},{32,0},{48,16},{1,33},{17,49},{33,1},{49,17},{2,34}... | collective-permute-start | bytes 245768 | tf_op jit(solution)/shard_map/ppermute | solution.py:476
  47.6 3.4 %collective-permute-start.2 = (bf16[160,256]{1,0:T(8,128)(2,1)S(1)}, bf16[160,256]{1,0:T(8,128)(2,1)S(1)}, u32[]{:S(2)}, u32[]{:S(2)}) collective-permute-start(bf16[160,256]{1,0:T(8,128)(2,1)S(1)} %get-tuple-element.59), channel_id=1, source_target_pairs={{0,48},{16,32},{32,16},{48,0},{1,49},{17,33},{33,17},{49,1},{2,50}... | collective-permute-start | bytes 245768 | tf_op jit(solution)/shard_map/ppermute | solution.py:476
  51.0 2.3 %collective-permute-done.1.refs_2_ = bf16[160,256]{1,0:T(8,128)(2,1)S(1)} collective-permute-done((bf16[160,256]{1,0:T(8,128)(2,1)S(1)}, bf16[160,256]{1,0:T(8,128)(2,1)S(1)}, u32[]{:S(2)}, u32[]{:S(2)}) %collective-permute-start.1) | collective-permute-done | bytes 81952 | tf_op jit(solution)/shard_map/ppermute | solution.py:476
  53.3 2.5 %collective-permute-done.2.refs_3_ = bf16[160,256]{1,0:T(8,128)(2,1)S(1)} collective-permute-done((bf16[160,256]{1,0:T(8,128)(2,1)S(1)}, bf16[160,256]{1,0:T(8,128)(2,1)S(1)}, u32[]{:S(2)}, u32[]{:S(2)}) %collective-permute-start.2) | collective-permute-done | bytes 81952 | tf_op jit(solution)/shard_map/ppermute | solution.py:476
  55.7 1.9 %collective-permute-start.3 = (bf16[2,4,8,8,1152]{4,3,2,1,0:T(8,128)(2,1)S(1)}, bf16[2,4,8,8,1152]{4,3,2,1,0:T(8,128)(2,1)S(1)}, u32[]{:S(2)}, u32[]{:S(2)}) collective-permute-start(bf16[2,4,8,8,1152]{4,3,2,1,0:T(8,128)(2,1)S(1)} %bitcast.22), channel_id=1, source_target_pairs={{0,1},{1,0},{2,3},{3,2},{4,5},{5,4},{6,7},{7,6},{8,9},{9,8},{10,11... | collective-permute-start | bytes 3538952 | tf_op jit(solution)/shard_map/ppermute | solution.py:470
  57.7 1.0 query_latents.1
  58.7 2.0 %own_scores.1 = (bf16[32,32,576]{2,1,0:T(8,128)(2,1)S(1)}, f32[256,1536]{1,0:T(8,128)S(1)}, f32[256,1536]{1,0:T(8,128)S(1)}, f32[2,256,128]{2,1,0:T(8,128)S(1)}) custom-call(s32[32]{0:T(128)S(1)} %copy-done.6, s32[5]{0:T(128)S(1)} %stack.23.place_ref, bf16[2,4,8,8,1152]{4,3,2,1,0:T(8,128)(2,1)S(1)} %bitcast.23, ...), custom_call_target="tpu_custom_call" | custom-call | flops 1073741824 | bytes 4194304 | tf_op jit(solution)/shard_map/own_scores/pallas_call | solution.py:384
  60.7 3.1 %scores.1 = (bf16[32,32,576]{2,1,0:T(8,128)(2,1)S(1)}, bf16[2,256,1536]{2,1,0:T(8,128)(2,1)S(1)}, bf16[2,256,1536]{2,1,0:T(8,128)(2,1)S(1)}) custom-call(s32[32]{0:T(128)S(1)} %copy-done.6, s32[5]{0:T(128)S(1)} %stack.23.place_ref, bf16[2,4,8,8,1152]{4,3,2,1,0:T(8,128)(2,1)S(1)} %collective-permute-done.3.other_ref, ...), custom_call_target="tpu_custom_call" | custom-call | flops 2147483648 | bytes 8388608 | tf_op jit(solution)/shard_map/scores/pallas_call | solution.py:384
  63.9 3.5 %key_side.1 = (bf16[2,2,2,8,8,1152]{5,4,3,2,1,0:T(8,128)(2,1)S(1)}, bf16[2,2,2,8,8,1152]{5,4,3,2,1,0:T(8,128)(2,1)S(1)}) custom-call(s32[32]{0:T(128)S(1)} %copy-done.6, s32[5]{0:T(128)S(1)} %stack.23.place_ref, bf16[2,256,576]{2,1,0:T(8,128)(2,1)S(1)} %get-tuple-element.65.query, bf16[2,256,512]{2,1,0:T(8,128)(2,1)S(1)} %get-tuple-element.66.grad, ...), custom_call_target="tpu_custom_call" | custom-call | flops 2147483648 | bytes 8388608 | tf_op jit(solution)/shard_map/key_side/pallas_call | solution.py:384
  67.3 2.4 %collective-permute-start.4 = (bf16[2,2,2,8,8,1152]{5,4,3,2,1,0:T(8,128)(2,1)S(1)}, bf16[2,2,2,8,8,1152]{5,4,3,2,1,0:T(8,128)(2,1)S(1)}, u32[]{:S(2)}, u32[]{:S(2)}) collective-permute-start(bf16[2,2,2,8,8,1152]{5,4,3,2,1,0:T(8,128)(2,1)S(1)} %get-tuple-element.82), channel_id=1, source_target_pairs={{0,1},{1,0},{2,3},{3,2},{4,5},{5,4},{6,7},{7,6},{8,9},{9,8},{10,11... | collective-permute-start | bytes 3538952 | tf_op jit(solution)/shard_map/ppermute | solution.py:470
  69.7 3.2 %query_side.1 = (bf16[512,128]{1,0:T(8,128)(2,1)S(1)}, bf16[512,128]{1,0:T(8,128)(2,1)S(1)}, bf16[96,256]{1,0:T(8,128)(2,1)S(1)}, bf16[96,256]{1,0:T(8,128)(2,1)S(1)}, bf16[2,96,256]{2,1,0:T(8,128)(2,1)S(1)}) custom-call(s32[32]{0:T(128)S(1)} %copy-done.6, s32[5]{0:T(128)S(1)} %stack.23.place_ref, bf16[32,32,576]{2,1,0:T(8,128)(2,1)S(1)} %get-tuple-element.67.own_keys, ...), custom_call_target="tpu_custom_call" | custom-call | flops 2147483648 | bytes 8388608 | tf_op jit(solution)/shard_map/query_side/pallas_call | solution.py:384
  73.2 3.2 %collective-permute-start.5 = (bf16[512,128]{1,0:T(8,128)(2,1)S(1)}, bf16[512,128]{1,0:T(8,128)(2,1)S(1)}, u32[]{:S(2)}, u32[]{:S(2)}) collective-permute-start(bf16[512,128]{1,0:T(8,128)(2,1)S(1)} %get-tuple-element.85), channel_id=1, source_target_pairs={{0,256},{256,0},{1,257},{257,1},{2,258},{258,2},{3,259},{259,3},{4... | collective-permute-start | bytes 393224 | tf_op jit(solution)/shard_map/ppermute | solution.py:470
  76.5 4.3 %collective-permute-start.10 = (bf16[2,96,256]{2,1,0:T(8,128)(2,1)S(1)}, bf16[2,96,256]{2,1,0:T(8,128)(2,1)S(1)}, u32[]{:S(2)}, u32[]{:S(2)}) collective-permute-start(bf16[2,96,256]{2,1,0:T(8,128)(2,1)S(1)} %get-tuple-element.93), channel_id=1, source_target_pairs={{0,16},{16,0},{1,17},{17,1},{2,18},{18,2},{3,19},{19,3},{4,20},{20... | collective-permute-start | bytes 294920 | tf_op jit(solution)/shard_map/ppermute | solution.py:470
  80.8 2.8 %collective-permute-start.6 = (bf16[2,2,8,8,1152]{4,3,2,1,0:T(8,128)(2,1)S(1)}, bf16[2,2,8,8,1152]{4,3,2,1,0:T(8,128)(2,1)S(1)}, u32[]{:S(2)}, u32[]{:S(2)}) collective-permute-start(bf16[2,2,8,8,1152]{4,3,2,1,0:T(8,128)(2,1)S(1)} %get-tuple-element.87), channel_id=1, source_target_pairs={{0,2},{2,0},{4,6},{6,4},{1,3},{3,1},{5,7},{7,5},{8,10},{10,8},{12,... | collective-permute-start | bytes 1769480 | tf_op jit(solution)/shard_map/ppermute | solution.py:509
  84.3 5.5 %all-to-all-start.2 = ((bf16[16,32,128]{2,1,0:T(8,128)(2,1)}), bf16[16,32,128]{2,1,0:T(8,128)(2,1)S(1)}, u32[]{:S(2)}, u32[]{:S(2)}) async-start(bf16[16,32,128]{2,1,0:T(8,128)(2,1)} %weight_sum.1), calls=%async_computation.2 | async-start | bytes 262144 | tf_op jit(solution)/shard_map/all_to_all | solution.py:466
  89.8 7.6 %collective-permute-done.6.came_ref = bf16[2,2,8,8,1152]{4,3,2,1,0:T(8,128)(2,1)S(1)} collective-permute-done((bf16[2,2,8,8,1152]{4,3,2,1,0:T(8,128)(2,1)S(1)}, bf16[2,2,8,8,1152]{4,3,2,1,0:T(8,128)(2,1)S(1)}, u32[]{:S(2)}, u32[]{:S(2)}) %collective-permute-start.6) | collective-permute-done | bytes 589856 | tf_op jit(solution)/shard_map/ppermute | solution.py:509
  97.5 5.2 %collective-permute-start.7 = (bf16[8,8,1152]{2,1,0:T(8,128)(2,1)S(1)}, bf16[8,8,1152]{2,1,0:T(8,128)(2,1)S(1)}, u32[]{:S(2)}, u32[]{:S(2)}) collective-permute-start(bf16[8,8,1152]{2,1,0:T(8,128)(2,1)S(1)} %get-tuple-element.89), channel_id=1, source_target_pairs={{0,12},{2,14},{4,8},{6,10},{8,4},{10,6},{12,0},{14,2},{1,13},{3,15... | collective-permute-start | bytes 442376 | tf_op jit(solution)/shard_map/ppermute | solution.py:518
  102.7 2.5 %collective-permute-start.8 = (bf16[8,8,1152]{2,1,0:T(8,128)(2,1)S(1)}, bf16[8,8,1152]{2,1,0:T(8,128)(2,1)S(1)}, u32[]{:S(2)}, u32[]{:S(2)}) collective-permute-start(bf16[8,8,1152]{2,1,0:T(8,128)(2,1)S(1)} %get-tuple-element.90), channel_id=1, source_target_pairs={{0,4},{2,6},{4,0},{6,2},{8,12},{10,14},{12,8},{14,10},{1,5},{3,7},... | collective-permute-start | bytes 442376 | tf_op jit(solution)/shard_map/ppermute | solution.py:518
  105.2 4.6 %collective-permute-start.9 = (bf16[8,8,1152]{2,1,0:T(8,128)(2,1)S(1)}, bf16[8,8,1152]{2,1,0:T(8,128)(2,1)S(1)}, u32[]{:S(2)}, u32[]{:S(2)}) collective-permute-start(bf16[8,8,1152]{2,1,0:T(8,128)(2,1)S(1)} %get-tuple-element.91), channel_id=1, source_target_pairs={{0,8},{2,10},{4,12},{6,14},{8,0},{10,2},{12,4},{14,6},{1,9},{3,11}... | collective-permute-start | bytes 442376 | tf_op jit(solution)/shard_map/ppermute | solution.py:518
  109.8 4.3 %collective-permute-start.11 = (bf16[2,96,256]{2,1,0:T(8,128)(2,1)S(1)}, bf16[2,96,256]{2,1,0:T(8,128)(2,1)S(1)}, u32[]{:S(2)}, u32[]{:S(2)}) collective-permute-start(bf16[2,96,256]{2,1,0:T(8,128)(2,1)S(1)} %relay.1), channel_id=1, source_target_pairs={{0,32},{32,0},{1,33},{33,1},{2,34},{34,2},{3,35},{35,3},{4,36},{36... | collective-permute-start | bytes 294920 | tf_op jit(solution)/shard_map/ppermute | solution.py:470
  114.1 3.9 %collective-permute-done.11.far_ref = bf16[2,96,256]{2,1,0:T(8,128)(2,1)S(1)} collective-permute-done((bf16[2,96,256]{2,1,0:T(8,128)(2,1)S(1)}, bf16[2,96,256]{2,1,0:T(8,128)(2,1)S(1)}, u32[]{:S(2)}, u32[]{:S(2)}) %collective-permute-start.11) | collective-permute-done | bytes 98336 | tf_op jit(solution)/shard_map/ppermute | solution.py:470
  118.2 26.4 %all_to_all.26 = bf16[16,8,1600]{2,1,0:T(8,128)(2,1)S(1)} all-to-all(bf16[16,8,1600]{2,1,0:T(8,128)(2,1)S(1)} %pack.1), channel_id=1, replica_groups=mesh['dp'=2,'zq'=4,'z1'=2,'z0'=2,'yh'=2,'x'=4,'c'=2] {'zq','z1','z0'}, dimensions={0} | all-to-all | bytes 819200 | tf_op jit(solution)/shard_map/all_to_all | solution.py:466
  144.6 1.1 broadcast_in_dim.23
  145.7 4.6 %all-to-all-start.4 = ((bf16[4,16,8,1024]{3,2,1,0:T(8,128)(2,1)}), bf16[4,16,8,1024]{3,2,1,0:T(8,128)(2,1)S(1)}, u32[]{:S(2)}, u32[]{:S(2)}) async-start(bf16[4,16,8,1024]{3,2,1,0:T(8,128)(2,1)} %broadcast_in_dim.23), calls=%async_computation.4 | async-start | bytes 2097152 | tf_op jit(solution)/shard_map/all_to_all | solution.py:466
  150.3 1.3 put_heads.1
  152.3 6.9 %all-to-all-done.4.whole_ref = bf16[4,16,8,1024]{3,2,1,0:T(8,128)(2,1)S(1)} async-done(((bf16[4,16,8,1024]{3,2,1,0:T(8,128)(2,1)}), bf16[4,16,8,1024]{3,2,1,0:T(8,128)(2,1)S(1)}, u32[]{:S(2)}, u32[]{:S(2)}) %all-to-all-start.4) | async-done | bytes 1048608 | tf_op jit(solution)/shard_map/all_to_all | solution.py:466
  159.2 1.4 spread.1
  (41 shorter events, 3.2 us)
Async XLA Ops:
  0.6 0.9 copy-start
  33.8 6.3 %copy-start.3 = (bf16[1,128,512]{2,1,0:T(8,128)(2,1)S(1)}, bf16[1,128,512]{2,1,0:T(8,128)(2,1)}, u32[]{:S(2)}) copy-start(bf16[1,128,512]{2,1,0:T(8,128)(2,1)} %param.8) | copy-start | bytes 393220
  33.8 6.3 %copy-start.4 = (bf16[1,128,512]{2,1,0:T(8,128)(2,1)S(1)}, bf16[1,128,512]{2,1,0:T(8,128)(2,1)}, u32[]{:S(2)}) copy-start(bf16[1,128,512]{2,1,0:T(8,128)(2,1)} %param.10) | copy-start | bytes 393220
  33.8 6.3 %copy-start.5 = (bf16[1,128,256]{2,1,0:T(8,128)(2,1)S(1)}, bf16[1,128,256]{2,1,0:T(8,128)(2,1)}, u32[]{:S(2)}) copy-start(bf16[1,128,256]{2,1,0:T(8,128)(2,1)} %param.9) | copy-start | bytes 196612
  33.8 23.9 %copy-start.1 = (bf16[512,512]{1,0:T(8,128)(2,1)S(1)}, bf16[512,512]{1,0:T(8,128)(2,1)}, u32[]{:S(2)}) copy-start(bf16[512,512]{1,0:T(8,128)(2,1)} %refs_5_.1) | copy-start | bytes 1572868
  33.8 23.9 %copy-start.2 = (bf16[512,512]{1,0:T(8,128)(2,1)S(1)}, bf16[512,512]{1,0:T(8,128)(2,1)}, u32[]{:S(2)}) copy-start(bf16[512,512]{1,0:T(8,128)(2,1)} %wk_ref.1) | copy-start | bytes 1572868
  33.8 23.9 %copy-start.6 = (s32[32]{0:T(128)S(1)}, s32[32]{0:T(128)}, u32[]{:S(2)}) copy-start(s32[32]{0:T(128)} %order_ref.9) | copy-start | bytes 388
  33.8 21.9 %all-to-all-start.1 = ((bf16[8,8,8,1152]{3,2,1,0:T(8,128)(2,1)}), bf16[8,8,8,1152]{3,2,1,0:T(8,128)(2,1)S(1)}, u32[]{:S(2)}, u32[]{:S(2)}) async-start(bf16[8,8,8,1152]{3,2,1,0:T(8,128)(2,1)} %broadcast_in_dim.19), calls=%async_computation.1 | async-start | bytes 2359296 | tf_op jit(solution)/shard_map/all_to_all | solution.py:466
  40.8 10.1 %collective-permute-start = (bf16[160,256]{1,0:T(8,128)(2,1)S(1)}, bf16[160,256]{1,0:T(8,128)(2,1)S(1)}, u32[]{:S(2)}, u32[]{:S(2)}) collective-permute-start(bf16[160,256]{1,0:T(8,128)(2,1)S(1)} %get-tuple-element.57), channel_id=1, source_target_pairs={{0,16},{16,0},{32,48},{48,32},{1,17},{17,1},{33,49},{49,33},{2,18}... | collective-permute-start | bytes 245768 | tf_op jit(solution)/shard_map/ppermute | solution.py:476
  43.9 9.3 %collective-permute-start.1 = (bf16[160,256]{1,0:T(8,128)(2,1)S(1)}, bf16[160,256]{1,0:T(8,128)(2,1)S(1)}, u32[]{:S(2)}, u32[]{:S(2)}) collective-permute-start(bf16[160,256]{1,0:T(8,128)(2,1)S(1)} %get-tuple-element.58), channel_id=1, source_target_pairs={{0,32},{16,48},{32,0},{48,16},{1,33},{17,49},{33,1},{49,17},{2,34}... | collective-permute-start | bytes 245768 | tf_op jit(solution)/shard_map/ppermute | solution.py:476
  47.6 8.1 %collective-permute-start.2 = (bf16[160,256]{1,0:T(8,128)(2,1)S(1)}, bf16[160,256]{1,0:T(8,128)(2,1)S(1)}, u32[]{:S(2)}, u32[]{:S(2)}) collective-permute-start(bf16[160,256]{1,0:T(8,128)(2,1)S(1)} %get-tuple-element.59), channel_id=1, source_target_pairs={{0,48},{16,32},{32,16},{48,0},{1,49},{17,33},{33,17},{49,1},{2,50}... | collective-permute-start | bytes 245768 | tf_op jit(solution)/shard_map/ppermute | solution.py:476
  55.7 5.0 %collective-permute-start.3 = (bf16[2,4,8,8,1152]{4,3,2,1,0:T(8,128)(2,1)S(1)}, bf16[2,4,8,8,1152]{4,3,2,1,0:T(8,128)(2,1)S(1)}, u32[]{:S(2)}, u32[]{:S(2)}) collective-permute-start(bf16[2,4,8,8,1152]{4,3,2,1,0:T(8,128)(2,1)S(1)} %bitcast.22), channel_id=1, source_target_pairs={{0,1},{1,0},{2,3},{3,2},{4,5},{5,4},{6,7},{7,6},{8,9},{9,8},{10,11... | collective-permute-start | bytes 3538952 | tf_op jit(solution)/shard_map/ppermute | solution.py:470
  67.3 5.6 %collective-permute-start.4 = (bf16[2,2,2,8,8,1152]{5,4,3,2,1,0:T(8,128)(2,1)S(1)}, bf16[2,2,2,8,8,1152]{5,4,3,2,1,0:T(8,128)(2,1)S(1)}, u32[]{:S(2)}, u32[]{:S(2)}) collective-permute-start(bf16[2,2,2,8,8,1152]{5,4,3,2,1,0:T(8,128)(2,1)S(1)} %get-tuple-element.82), channel_id=1, source_target_pairs={{0,1},{1,0},{2,3},{3,2},{4,5},{5,4},{6,7},{7,6},{8,9},{9,8},{10,11... | collective-permute-start | bytes 3538952 | tf_op jit(solution)/shard_map/ppermute | solution.py:470
  73.2 10.3 %collective-permute-start.5 = (bf16[512,128]{1,0:T(8,128)(2,1)S(1)}, bf16[512,128]{1,0:T(8,128)(2,1)S(1)}, u32[]{:S(2)}, u32[]{:S(2)}) collective-permute-start(bf16[512,128]{1,0:T(8,128)(2,1)S(1)} %get-tuple-element.85), channel_id=1, source_target_pairs={{0,256},{256,0},{1,257},{257,1},{2,258},{258,2},{3,259},{259,3},{4... | collective-permute-start | bytes 393224 | tf_op jit(solution)/shard_map/ppermute | solution.py:470
  76.5 33.3 %collective-permute-start.10 = (bf16[2,96,256]{2,1,0:T(8,128)(2,1)S(1)}, bf16[2,96,256]{2,1,0:T(8,128)(2,1)S(1)}, u32[]{:S(2)}, u32[]{:S(2)}) collective-permute-start(bf16[2,96,256]{2,1,0:T(8,128)(2,1)S(1)} %get-tuple-element.93), channel_id=1, source_target_pairs={{0,16},{16,0},{1,17},{17,1},{2,18},{18,2},{3,19},{19,3},{4,20},{20... | collective-permute-start | bytes 294920 | tf_op jit(solution)/shard_map/ppermute | solution.py:470
  80.8 16.6 %collective-permute-start.6 = (bf16[2,2,8,8,1152]{4,3,2,1,0:T(8,128)(2,1)S(1)}, bf16[2,2,8,8,1152]{4,3,2,1,0:T(8,128)(2,1)S(1)}, u32[]{:S(2)}, u32[]{:S(2)}) collective-permute-start(bf16[2,2,8,8,1152]{4,3,2,1,0:T(8,128)(2,1)S(1)} %get-tuple-element.87), channel_id=1, source_target_pairs={{0,2},{2,0},{4,6},{6,4},{1,3},{3,1},{5,7},{7,5},{8,10},{10,8},{12,... | collective-permute-start | bytes 1769480 | tf_op jit(solution)/shard_map/ppermute | solution.py:509
  84.3 33.7 %all-to-all-start.2 = ((bf16[16,32,128]{2,1,0:T(8,128)(2,1)}), bf16[16,32,128]{2,1,0:T(8,128)(2,1)S(1)}, u32[]{:S(2)}, u32[]{:S(2)}) async-start(bf16[16,32,128]{2,1,0:T(8,128)(2,1)} %weight_sum.1), calls=%async_computation.2 | async-start | bytes 262144 | tf_op jit(solution)/shard_map/all_to_all | solution.py:466
  97.5 20.5 %collective-permute-start.7 = (bf16[8,8,1152]{2,1,0:T(8,128)(2,1)S(1)}, bf16[8,8,1152]{2,1,0:T(8,128)(2,1)S(1)}, u32[]{:S(2)}, u32[]{:S(2)}) collective-permute-start(bf16[8,8,1152]{2,1,0:T(8,128)(2,1)S(1)} %get-tuple-element.89), channel_id=1, source_target_pairs={{0,12},{2,14},{4,8},{6,10},{8,4},{10,6},{12,0},{14,2},{1,13},{3,15... | collective-permute-start | bytes 442376 | tf_op jit(solution)/shard_map/ppermute | solution.py:518
  102.7 15.3 %collective-permute-start.8 = (bf16[8,8,1152]{2,1,0:T(8,128)(2,1)S(1)}, bf16[8,8,1152]{2,1,0:T(8,128)(2,1)S(1)}, u32[]{:S(2)}, u32[]{:S(2)}) collective-permute-start(bf16[8,8,1152]{2,1,0:T(8,128)(2,1)S(1)} %get-tuple-element.90), channel_id=1, source_target_pairs={{0,4},{2,6},{4,0},{6,2},{8,12},{10,14},{12,8},{14,10},{1,5},{3,7},... | collective-permute-start | bytes 442376 | tf_op jit(solution)/shard_map/ppermute | solution.py:518
  105.2 12.8 %collective-permute-start.9 = (bf16[8,8,1152]{2,1,0:T(8,128)(2,1)S(1)}, bf16[8,8,1152]{2,1,0:T(8,128)(2,1)S(1)}, u32[]{:S(2)}, u32[]{:S(2)}) collective-permute-start(bf16[8,8,1152]{2,1,0:T(8,128)(2,1)S(1)} %get-tuple-element.91), channel_id=1, source_target_pairs={{0,8},{2,10},{4,12},{6,14},{8,0},{10,2},{12,4},{14,6},{1,9},{3,11}... | collective-permute-start | bytes 442376 | tf_op jit(solution)/shard_map/ppermute | solution.py:518
  109.8 8.2 %collective-permute-start.11 = (bf16[2,96,256]{2,1,0:T(8,128)(2,1)S(1)}, bf16[2,96,256]{2,1,0:T(8,128)(2,1)S(1)}, u32[]{:S(2)}, u32[]{:S(2)}) collective-permute-start(bf16[2,96,256]{2,1,0:T(8,128)(2,1)S(1)} %relay.1), channel_id=1, source_target_pairs={{0,32},{32,0},{1,33},{33,1},{2,34},{34,2},{3,35},{35,3},{4,36},{36... | collective-permute-start | bytes 294920 | tf_op jit(solution)/shard_map/ppermute | solution.py:470
  145.7 13.5 %all-to-all-start.4 = ((bf16[4,16,8,1024]{3,2,1,0:T(8,128)(2,1)}), bf16[4,16,8,1024]{3,2,1,0:T(8,128)(2,1)S(1)}, u32[]{:S(2)}, u32[]{:S(2)}) async-start(bf16[4,16,8,1024]{3,2,1,0:T(8,128)(2,1)} %broadcast_in_dim.23), calls=%async_computation.4 | async-start | bytes 2097152 | tf_op jit(solution)/shard_map/all_to_all | solution.py:466

commit v8 on v7

--- a/solution.py
+++ b/solution.py
@@ -509,7 +509,7 @@
     beside = lax.ppermute(parts[1], "x", [(i, i ^ 1) for i in range(4)])
     near = flip(near, "z0")
     sums = (keep, flip(give, "dp"))
-    (weights,) = call(weight_kernel, "weight_sum", 0, sums, ((N_CTX, 32, D_NOPE),), flops=LATE)
+    (weights,) = call(weight_kernel, "weight_sum", 0, sums, ((N_CTX, 32, D_NOPE),))
     columns = swap(weights, Z_AXES)
     lines = call(line_kernel, "line_sum", 0, (parts[0], beside), (part[2:],) * 4, flops=LATE)
     (relay,) = call(relay_kernel, "relay", 0, (far, near), (near.shape,))

time: 161 us -> 162 us (level)
  the two profiles are of different devices: /device:TPU:8 before, /device:TPU:64 now
where the time goes in v8:
time: 162 us; the launch traced here: 161 us
  blocking collectives  63.7 us (39%)
  starting transfers between devices  55.3 us (34%)
  waiting for transfers between devices  19.3 us (12%)
  Pallas kernels  17.6 us (11%)
  local copies, waits for them, and re-layouts  3.67 us (2%)
    all_to_all x2, blocking collectives, swap(): return lax.all_to_all(values, axes, 0, 0, tiled=True)  63.7 us
    all_to_all x3, starting transfers between devices, swap(): return lax.all_to_all(values, axes, 0, 0, tiled=True)  18.1 us
    pallas_call x13, Pallas kernels, call(): pl.pallas_call(kernel, out_shape=shapes, in_specs=[SMEM] * n_smem + [VMEM...  17.6 us
    ppermute x5, starting transfers between devices, flip(): return lax.ppermute(values, axis, [(0, 1), (1, 0)])  13.1 us
    ppermute x3, starting transfers between devices, local(): sides.append(lax.ppermute(share, PLANE, [(i, i ^ ahead) for i in range(8)]))  12.2 us
    all_to_all x3, waiting for transfers between devices, swap(): return lax.all_to_all(values, axes, 0, 0, tiled=True)  10.7 us
    ppermute x3, starting transfers between devices, team_swap(): lax.ppermute(parts[ahead], ('z1', 'z0'), [(i, i ^ ahead) for i in range(T...  9.21 us
    ppermute x5, waiting for transfers between devices, flip(): return lax.ppermute(values, axis, [(0, 1), (1, 0)])  5.75 us
  transfers between devices with their start and end apart: 15, of which 6 were waited for; matrix products, arithmetic and copies ran while one was open for 0% of the time, Pallas kernels for 6%

profile of v8, /device:TPU:64, one launch (start us, length us, event | category | flops | bytes accessed | tf_op | source)
XLA Modules:
  0.0 161.2 jit_solution(16162405909583235070)
XLA Ops:
  0.7 0.9 copy-done
  1.8 29.4 %all_to_all.25 = bf16[16,8,576]{2,1,0:T(8,128)(2,1)S(1)} all-to-all(bf16[16,8,576]{2,1,0:T(8,128)(2,1)S(1)} %broadcast_in_dim.18), channel_id=1, replica_groups=mesh['dp'=2,'zq'=4,'z1'=2,'z0'=2,'yh'=2,'x'=4,'c'=2] {'zq','z1','z0'}, dimensions={0} | all-to-all | bytes 294912 | tf_op jit(solution)/shard_map/all_to_all | solution.py:466
  31.4 1.2 broadcast_in_dim.19
  32.6 7.1 %all-to-all-start.1 = ((bf16[8,8,8,1152]{3,2,1,0:T(8,128)(2,1)}), bf16[8,8,8,1152]{3,2,1,0:T(8,128)(2,1)S(1)}, u32[]{:S(2)}, u32[]{:S(2)}) async-start(bf16[8,8,8,1152]{3,2,1,0:T(8,128)(2,1)} %broadcast_in_dim.19), calls=%async_computation.1 | async-start | bytes 2359296 | tf_op jit(solution)/shard_map/all_to_all | solution.py:466
  40.6 2.7 %collective-permute-start = (bf16[160,256]{1,0:T(8,128)(2,1)S(1)}, bf16[160,256]{1,0:T(8,128)(2,1)S(1)}, u32[]{:S(2)}, u32[]{:S(2)}) collective-permute-start(bf16[160,256]{1,0:T(8,128)(2,1)S(1)} %get-tuple-element.57), channel_id=1, source_target_pairs={{0,16},{16,0},{32,48},{48,32},{1,17},{17,1},{33,49},{49,33},{2,18}... | collective-permute-start | bytes 245768 | tf_op jit(solution)/shard_map/ppermute | solution.py:476
  43.3 3.1 %collective-permute-start.1 = (bf16[160,256]{1,0:T(8,128)(2,1)S(1)}, bf16[160,256]{1,0:T(8,128)(2,1)S(1)}, u32[]{:S(2)}, u32[]{:S(2)}) collective-permute-start(bf16[160,256]{1,0:T(8,128)(2,1)S(1)} %get-tuple-element.58), channel_id=1, source_target_pairs={{0,32},{16,48},{32,0},{48,16},{1,33},{17,49},{33,1},{49,17},{2,34}... | collective-permute-start | bytes 245768 | tf_op jit(solution)/shard_map/ppermute | solution.py:476
  46.4 3.4 %collective-permute-start.2 = (bf16[160,256]{1,0:T(8,128)(2,1)S(1)}, bf16[160,256]{1,0:T(8,128)(2,1)S(1)}, u32[]{:S(2)}, u32[]{:S(2)}) collective-permute-start(bf16[160,256]{1,0:T(8,128)(2,1)S(1)} %get-tuple-element.59), channel_id=1, source_target_pairs={{0,48},{16,32},{32,16},{48,0},{1,49},{17,33},{33,17},{49,1},{2,50}... | collective-permute-start | bytes 245768 | tf_op jit(solution)/shard_map/ppermute | solution.py:476
  49.8 0.9 collective-permute-done.1.refs_2_
  50.7 2.0 %collective-permute-done.2.refs_3_ = bf16[160,256]{1,0:T(8,128)(2,1)S(1)} collective-permute-done((bf16[160,256]{1,0:T(8,128)(2,1)S(1)}, bf16[160,256]{1,0:T(8,128)(2,1)S(1)}, u32[]{:S(2)}, u32[]{:S(2)}) %collective-permute-start.2) | collective-permute-done | bytes 81952 | tf_op jit(solution)/shard_map/ppermute | solution.py:476
  52.7 3.3 %all-to-all-done.1 = bf16[8,8,8,1152]{3,2,1,0:T(8,128)(2,1)S(1)} async-done(((bf16[8,8,8,1152]{3,2,1,0:T(8,128)(2,1)}), bf16[8,8,8,1152]{3,2,1,0:T(8,128)(2,1)S(1)}, u32[]{:S(2)}, u32[]{:S(2)}) %all-to-all-start.1) | async-done | bytes 1179680 | tf_op jit(solution)/shard_map/all_to_all | solution.py:466
  56.0 1.9 %collective-permute-start.3 = (bf16[2,4,8,8,1152]{4,3,2,1,0:T(8,128)(2,1)S(1)}, bf16[2,4,8,8,1152]{4,3,2,1,0:T(8,128)(2,1)S(1)}, u32[]{:S(2)}, u32[]{:S(2)}) collective-permute-start(bf16[2,4,8,8,1152]{4,3,2,1,0:T(8,128)(2,1)S(1)} %bitcast.22), channel_id=1, source_target_pairs={{0,1},{1,0},{2,3},{3,2},{4,5},{5,4},{6,7},{7,6},{8,9},{9,8},{10,11... | collective-permute-start | bytes 3538952 | tf_op jit(solution)/shard_map/ppermute | solution.py:470
  57.9 1.0 query_latents.1
  58.9 2.0 %own_scores.1 = (bf16[32,32,576]{2,1,0:T(8,128)(2,1)S(1)}, f32[256,1536]{1,0:T(8,128)S(1)}, f32[256,1536]{1,0:T(8,128)S(1)}, f32[2,256,128]{2,1,0:T(8,128)S(1)}) custom-call(s32[32]{0:T(128)S(1)} %copy-done.6, s32[5]{0:T(128)S(1)} %stack.23.place_ref, bf16[2,4,8,8,1152]{4,3,2,1,0:T(8,128)(2,1)S(1)} %bitcast.23, ...), custom_call_target="tpu_custom_call" | custom-call | flops 1073741824 | bytes 4194304 | tf_op jit(solution)/shard_map/own_scores/pallas_call | solution.py:384
  60.9 3.1 %scores.1 = (bf16[32,32,576]{2,1,0:T(8,128)(2,1)S(1)}, bf16[2,256,1536]{2,1,0:T(8,128)(2,1)S(1)}, bf16[2,256,1536]{2,1,0:T(8,128)(2,1)S(1)}) custom-call(s32[32]{0:T(128)S(1)} %copy-done.6, s32[5]{0:T(128)S(1)} %stack.23.place_ref, bf16[2,4,8,8,1152]{4,3,2,1,0:T(8,128)(2,1)S(1)} %collective-permute-done.3.other_ref, ...), custom_call_target="tpu_custom_call" | custom-call | flops 2147483648 | bytes 8388608 | tf_op jit(solution)/shard_map/scores/pallas_call | solution.py:384
  64.1 3.5 %key_side.1 = (bf16[2,2,2,8,8,1152]{5,4,3,2,1,0:T(8,128)(2,1)S(1)}, bf16[2,2,2,8,8,1152]{5,4,3,2,1,0:T(8,128)(2,1)S(1)}) custom-call(s32[32]{0:T(128)S(1)} %copy-done.6, s32[5]{0:T(128)S(1)} %stack.23.place_ref, bf16[2,256,576]{2,1,0:T(8,128)(2,1)S(1)} %get-tuple-element.65.query, bf16[2,256,512]{2,1,0:T(8,128)(2,1)S(1)} %get-tuple-element.66.grad, ...), custom_call_target="tpu_custom_call" | custom-call | flops 2147483648 | bytes 8388608 | tf_op jit(solution)/shard_map/key_side/pallas_call | solution.py:384
  67.5 2.4 %collective-permute-start.4 = (bf16[2,2,2,8,8,1152]{5,4,3,2,1,0:T(8,128)(2,1)S(1)}, bf16[2,2,2,8,8,1152]{5,4,3,2,1,0:T(8,128)(2,1)S(1)}, u32[]{:S(2)}, u32[]{:S(2)}) collective-permute-start(bf16[2,2,2,8,8,1152]{5,4,3,2,1,0:T(8,128)(2,1)S(1)} %get-tuple-element.82), channel_id=1, source_target_pairs={{0,1},{1,0},{2,3},{3,2},{4,5},{5,4},{6,7},{7,6},{8,9},{9,8},{10,11... | collective-permute-start | bytes 3538952 | tf_op jit(solution)/shard_map/ppermute | solution.py:470
  69.9 3.2 %query_side.1 = (bf16[512,128]{1,0:T(8,128)(2,1)S(1)}, bf16[512,128]{1,0:T(8,128)(2,1)S(1)}, bf16[96,256]{1,0:T(8,128)(2,1)S(1)}, bf16[96,256]{1,0:T(8,128)(2,1)S(1)}, bf16[2,96,256]{2,1,0:T(8,128)(2,1)S(1)}) custom-call(s32[32]{0:T(128)S(1)} %copy-done.6, s32[5]{0:T(128)S(1)} %stack.23.place_ref, bf16[32,32,576]{2,1,0:T(8,128)(2,1)S(1)} %get-tuple-element.67.own_keys, ...), custom_call_target="tpu_custom_call" | custom-call | flops 2147483648 | bytes 8388608 | tf_op jit(solution)/shard_map/query_side/pallas_call | solution.py:384
  73.5 2.7 %collective-permute-start.6 = (bf16[2,2,8,8,1152]{4,3,2,1,0:T(8,128)(2,1)S(1)}, bf16[2,2,8,8,1152]{4,3,2,1,0:T(8,128)(2,1)S(1)}, u32[]{:S(2)}, u32[]{:S(2)}) collective-permute-start(bf16[2,2,8,8,1152]{4,3,2,1,0:T(8,128)(2,1)S(1)} %get-tuple-element.87), channel_id=1, source_target_pairs={{0,2},{2,0},{4,6},{6,4},{1,3},{3,1},{5,7},{7,5},{8,10},{10,8},{12,... | collective-permute-start | bytes 1769480 | tf_op jit(solution)/shard_map/ppermute | solution.py:509
  76.1 2.6 %collective-permute-start.5 = (bf16[512,128]{1,0:T(8,128)(2,1)S(1)}, bf16[512,128]{1,0:T(8,128)(2,1)S(1)}, u32[]{:S(2)}, u32[]{:S(2)}) collective-permute-start(bf16[512,128]{1,0:T(8,128)(2,1)S(1)} %get-tuple-element.85), channel_id=1, source_target_pairs={{0,256},{256,0},{1,257},{257,1},{2,258},{258,2},{3,259},{259,3},{4... | collective-permute-start | bytes 393224 | tf_op jit(solution)/shard_map/ppermute | solution.py:470
  78.7 4.2 %collective-permute-start.10 = (bf16[2,96,256]{2,1,0:T(8,128)(2,1)S(1)}, bf16[2,96,256]{2,1,0:T(8,128)(2,1)S(1)}, u32[]{:S(2)}, u32[]{:S(2)}) collective-permute-start(bf16[2,96,256]{2,1,0:T(8,128)(2,1)S(1)} %get-tuple-element.93), channel_id=1, source_target_pairs={{0,16},{16,0},{1,17},{17,1},{2,18},{18,2},{3,19},{19,3},{4,20},{20... | collective-permute-start | bytes 294920 | tf_op jit(solution)/shard_map/ppermute | solution.py:470
  83.8 7.5 %all-to-all-start.2 = ((bf16[16,32,128]{2,1,0:T(8,128)(2,1)}), bf16[16,32,128]{2,1,0:T(8,128)(2,1)S(1)}, u32[]{:S(2)}, u32[]{:S(2)}) async-start(bf16[16,32,128]{2,1,0:T(8,128)(2,1)} %weight_sum.1), calls=%async_computation.2 | async-start | bytes 262144 | tf_op jit(solution)/shard_map/all_to_all | solution.py:466
  91.5 6.1 %collective-permute-start.7 = (bf16[8,8,1152]{2,1,0:T(8,128)(2,1)S(1)}, bf16[8,8,1152]{2,1,0:T(8,128)(2,1)S(1)}, u32[]{:S(2)}, u32[]{:S(2)}) collective-permute-start(bf16[8,8,1152]{2,1,0:T(8,128)(2,1)S(1)} %get-tuple-element.89), channel_id=1, source_target_pairs={{0,12},{2,14},{4,8},{6,10},{8,4},{10,6},{12,0},{14,2},{1,13},{3,15... | collective-permute-start | bytes 442376 | tf_op jit(solution)/shard_map/ppermute | solution.py:518
  97.6 2.8 %collective-permute-start.8 = (bf16[8,8,1152]{2,1,0:T(8,128)(2,1)S(1)}, bf16[8,8,1152]{2,1,0:T(8,128)(2,1)S(1)}, u32[]{:S(2)}, u32[]{:S(2)}) collective-permute-start(bf16[8,8,1152]{2,1,0:T(8,128)(2,1)S(1)} %get-tuple-element.90), channel_id=1, source_target_pairs={{0,4},{2,6},{4,0},{6,2},{8,12},{10,14},{12,8},{14,10},{1,5},{3,7},... | collective-permute-start | bytes 442376 | tf_op jit(solution)/shard_map/ppermute | solution.py:518
  100.4 3.4 %collective-permute-start.9 = (bf16[8,8,1152]{2,1,0:T(8,128)(2,1)S(1)}, bf16[8,8,1152]{2,1,0:T(8,128)(2,1)S(1)}, u32[]{:S(2)}, u32[]{:S(2)}) collective-permute-start(bf16[8,8,1152]{2,1,0:T(8,128)(2,1)S(1)} %get-tuple-element.91), channel_id=1, source_target_pairs={{0,8},{2,10},{4,12},{6,14},{8,0},{10,2},{12,4},{14,6},{1,9},{3,11}... | collective-permute-start | bytes 442376 | tf_op jit(solution)/shard_map/ppermute | solution.py:518
  103.8 2.0 %collective-permute-start.11 = (bf16[2,96,256]{2,1,0:T(8,128)(2,1)S(1)}, bf16[2,96,256]{2,1,0:T(8,128)(2,1)S(1)}, u32[]{:S(2)}, u32[]{:S(2)}) collective-permute-start(bf16[2,96,256]{2,1,0:T(8,128)(2,1)S(1)} %relay.1), channel_id=1, source_target_pairs={{0,32},{32,0},{1,33},{33,1},{2,34},{34,2},{3,35},{35,3},{4,36},{36... | collective-permute-start | bytes 294920 | tf_op jit(solution)/shard_map/ppermute | solution.py:470
  105.8 5.5 %collective-permute-done.11.far_ref = bf16[2,96,256]{2,1,0:T(8,128)(2,1)S(1)} collective-permute-done((bf16[2,96,256]{2,1,0:T(8,128)(2,1)S(1)}, bf16[2,96,256]{2,1,0:T(8,128)(2,1)S(1)}, u32[]{:S(2)}, u32[]{:S(2)}) %collective-permute-start.11) | collective-permute-done | bytes 98336 | tf_op jit(solution)/shard_map/ppermute | solution.py:470
  111.5 34.3 %all_to_all.26 = bf16[16,8,1600]{2,1,0:T(8,128)(2,1)S(1)} all-to-all(bf16[16,8,1600]{2,1,0:T(8,128)(2,1)S(1)} %pack.1), channel_id=1, replica_groups=mesh['dp'=2,'zq'=4,'z1'=2,'z0'=2,'yh'=2,'x'=4,'c'=2] {'zq','z1','z0'}, dimensions={0} | all-to-all | bytes 819200 | tf_op jit(solution)/shard_map/all_to_all | solution.py:466
  145.8 1.1 broadcast_in_dim.23
  146.9 3.5 %all-to-all-start.4 = ((bf16[4,16,8,1024]{3,2,1,0:T(8,128)(2,1)}), bf16[4,16,8,1024]{3,2,1,0:T(8,128)(2,1)S(1)}, u32[]{:S(2)}, u32[]{:S(2)}) async-start(bf16[4,16,8,1024]{3,2,1,0:T(8,128)(2,1)} %broadcast_in_dim.23), calls=%async_computation.4 | async-start | bytes 2097152 | tf_op jit(solution)/shard_map/all_to_all | solution.py:466
  150.4 1.4 put_heads.1
  152.4 7.4 %all-to-all-done.4.whole_ref = bf16[4,16,8,1024]{3,2,1,0:T(8,128)(2,1)S(1)} async-done(((bf16[4,16,8,1024]{3,2,1,0:T(8,128)(2,1)}), bf16[4,16,8,1024]{3,2,1,0:T(8,128)(2,1)S(1)}, u32[]{:S(2)}, u32[]{:S(2)}) %all-to-all-start.4) | async-done | bytes 1048608 | tf_op jit(solution)/shard_map/all_to_all | solution.py:466
  159.8 1.4 spread.1
  (41 shorter events, 3.5 us)
Async XLA Ops:
  0.6 0.9 copy-start
  32.6 7.2 %copy-start.3 = (bf16[1,128,512]{2,1,0:T(8,128)(2,1)S(1)}, bf16[1,128,512]{2,1,0:T(8,128)(2,1)}, u32[]{:S(2)}) copy-start(bf16[1,128,512]{2,1,0:T(8,128)(2,1)} %param.8) | copy-start | bytes 393220
  32.6 7.2 %copy-start.4 = (bf16[1,128,512]{2,1,0:T(8,128)(2,1)S(1)}, bf16[1,128,512]{2,1,0:T(8,128)(2,1)}, u32[]{:S(2)}) copy-start(bf16[1,128,512]{2,1,0:T(8,128)(2,1)} %param.10) | copy-start | bytes 393220
  32.6 7.2 %copy-start.5 = (bf16[1,128,256]{2,1,0:T(8,128)(2,1)S(1)}, bf16[1,128,256]{2,1,0:T(8,128)(2,1)}, u32[]{:S(2)}) copy-start(bf16[1,128,256]{2,1,0:T(8,128)(2,1)} %param.9) | copy-start | bytes 196612
  32.6 25.3 %copy-start.1 = (bf16[512,512]{1,0:T(8,128)(2,1)S(1)}, bf16[512,512]{1,0:T(8,128)(2,1)}, u32[]{:S(2)}) copy-start(bf16[512,512]{1,0:T(8,128)(2,1)} %refs_5_.1) | copy-start | bytes 1572868
  32.6 25.3 %copy-start.2 = (bf16[512,512]{1,0:T(8,128)(2,1)S(1)}, bf16[512,512]{1,0:T(8,128)(2,1)}, u32[]{:S(2)}) copy-start(bf16[512,512]{1,0:T(8,128)(2,1)} %wk_ref.1) | copy-start | bytes 1572868
  32.6 25.3 %copy-start.6 = (s32[32]{0:T(128)S(1)}, s32[32]{0:T(128)}, u32[]{:S(2)}) copy-start(s32[32]{0:T(128)} %order_ref.9) | copy-start | bytes 388
  32.6 23.3 %all-to-all-start.1 = ((bf16[8,8,8,1152]{3,2,1,0:T(8,128)(2,1)}), bf16[8,8,8,1152]{3,2,1,0:T(8,128)(2,1)S(1)}, u32[]{:S(2)}, u32[]{:S(2)}) async-start(bf16[8,8,8,1152]{3,2,1,0:T(8,128)(2,1)} %broadcast_in_dim.19), calls=%async_computation.1 | async-start | bytes 2359296 | tf_op jit(solution)/shard_map/all_to_all | solution.py:466
  40.6 9.2 %collective-permute-start = (bf16[160,256]{1,0:T(8,128)(2,1)S(1)}, bf16[160,256]{1,0:T(8,128)(2,1)S(1)}, u32[]{:S(2)}, u32[]{:S(2)}) collective-permute-start(bf16[160,256]{1,0:T(8,128)(2,1)S(1)} %get-tuple-element.57), channel_id=1, source_target_pairs={{0,16},{16,0},{32,48},{48,32},{1,17},{17,1},{33,49},{49,33},{2,18}... | collective-permute-start | bytes 245768 | tf_op jit(solution)/shard_map/ppermute | solution.py:476
  43.3 7.4 %collective-permute-start.1 = (bf16[160,256]{1,0:T(8,128)(2,1)S(1)}, bf16[160,256]{1,0:T(8,128)(2,1)S(1)}, u32[]{:S(2)}, u32[]{:S(2)}) collective-permute-start(bf16[160,256]{1,0:T(8,128)(2,1)S(1)} %get-tuple-element.58), channel_id=1, source_target_pairs={{0,32},{16,48},{32,0},{48,16},{1,33},{17,49},{33,1},{49,17},{2,34}... | collective-permute-start | bytes 245768 | tf_op jit(solution)/shard_map/ppermute | solution.py:476
  46.4 6.3 %collective-permute-start.2 = (bf16[160,256]{1,0:T(8,128)(2,1)S(1)}, bf16[160,256]{1,0:T(8,128)(2,1)S(1)}, u32[]{:S(2)}, u32[]{:S(2)}) collective-permute-start(bf16[160,256]{1,0:T(8,128)(2,1)S(1)} %get-tuple-element.59), channel_id=1, source_target_pairs={{0,48},{16,32},{32,16},{48,0},{1,49},{17,33},{33,17},{49,1},{2,50}... | collective-permute-start | bytes 245768 | tf_op jit(solution)/shard_map/ppermute | solution.py:476
  56.0 5.0 %collective-permute-start.3 = (bf16[2,4,8,8,1152]{4,3,2,1,0:T(8,128)(2,1)S(1)}, bf16[2,4,8,8,1152]{4,3,2,1,0:T(8,128)(2,1)S(1)}, u32[]{:S(2)}, u32[]{:S(2)}) collective-permute-start(bf16[2,4,8,8,1152]{4,3,2,1,0:T(8,128)(2,1)S(1)} %bitcast.22), channel_id=1, source_target_pairs={{0,1},{1,0},{2,3},{3,2},{4,5},{5,4},{6,7},{7,6},{8,9},{9,8},{10,11... | collective-permute-start | bytes 3538952 | tf_op jit(solution)/shard_map/ppermute | solution.py:470
  67.5 5.6 %collective-permute-start.4 = (bf16[2,2,2,8,8,1152]{5,4,3,2,1,0:T(8,128)(2,1)S(1)}, bf16[2,2,2,8,8,1152]{5,4,3,2,1,0:T(8,128)(2,1)S(1)}, u32[]{:S(2)}, u32[]{:S(2)}) collective-permute-start(bf16[2,2,2,8,8,1152]{5,4,3,2,1,0:T(8,128)(2,1)S(1)} %get-tuple-element.82), channel_id=1, source_target_pairs={{0,1},{1,0},{2,3},{3,2},{4,5},{5,4},{6,7},{7,6},{8,9},{9,8},{10,11... | collective-permute-start | bytes 3538952 | tf_op jit(solution)/shard_map/ppermute | solution.py:470
  73.5 17.9 %collective-permute-start.6 = (bf16[2,2,8,8,1152]{4,3,2,1,0:T(8,128)(2,1)S(1)}, bf16[2,2,8,8,1152]{4,3,2,1,0:T(8,128)(2,1)S(1)}, u32[]{:S(2)}, u32[]{:S(2)}) collective-permute-start(bf16[2,2,8,8,1152]{4,3,2,1,0:T(8,128)(2,1)S(1)} %get-tuple-element.87), channel_id=1, source_target_pairs={{0,2},{2,0},{4,6},{6,4},{1,3},{3,1},{5,7},{7,5},{8,10},{10,8},{12,... | collective-permute-start | bytes 1769480 | tf_op jit(solution)/shard_map/ppermute | solution.py:509
  76.1 7.0 %collective-permute-start.5 = (bf16[512,128]{1,0:T(8,128)(2,1)S(1)}, bf16[512,128]{1,0:T(8,128)(2,1)S(1)}, u32[]{:S(2)}, u32[]{:S(2)}) collective-permute-start(bf16[512,128]{1,0:T(8,128)(2,1)S(1)} %get-tuple-element.85), channel_id=1, source_target_pairs={{0,256},{256,0},{1,257},{257,1},{2,258},{258,2},{3,259},{259,3},{4... | collective-permute-start | bytes 393224 | tf_op jit(solution)/shard_map/ppermute | solution.py:470
  78.7 25.0 %collective-permute-start.10 = (bf16[2,96,256]{2,1,0:T(8,128)(2,1)S(1)}, bf16[2,96,256]{2,1,0:T(8,128)(2,1)S(1)}, u32[]{:S(2)}, u32[]{:S(2)}) collective-permute-start(bf16[2,96,256]{2,1,0:T(8,128)(2,1)S(1)} %get-tuple-element.93), channel_id=1, source_target_pairs={{0,16},{16,0},{1,17},{17,1},{2,18},{18,2},{3,19},{19,3},{4,20},{20... | collective-permute-start | bytes 294920 | tf_op jit(solution)/shard_map/ppermute | solution.py:470
  83.8 27.5 %all-to-all-start.2 = ((bf16[16,32,128]{2,1,0:T(8,128)(2,1)}), bf16[16,32,128]{2,1,0:T(8,128)(2,1)S(1)}, u32[]{:S(2)}, u32[]{:S(2)}) async-start(bf16[16,32,128]{2,1,0:T(8,128)(2,1)} %weight_sum.1), calls=%async_computation.2 | async-start | bytes 262144 | tf_op jit(solution)/shard_map/all_to_all | solution.py:466
  91.5 19.8 %collective-permute-start.7 = (bf16[8,8,1152]{2,1,0:T(8,128)(2,1)S(1)}, bf16[8,8,1152]{2,1,0:T(8,128)(2,1)S(1)}, u32[]{:S(2)}, u32[]{:S(2)}) collective-permute-start(bf16[8,8,1152]{2,1,0:T(8,128)(2,1)S(1)} %get-tuple-element.89), channel_id=1, source_target_pairs={{0,12},{2,14},{4,8},{6,10},{8,4},{10,6},{12,0},{14,2},{1,13},{3,15... | collective-permute-start | bytes 442376 | tf_op jit(solution)/shard_map/ppermute | solution.py:518
  97.6 13.7 %collective-permute-start.8 = (bf16[8,8,1152]{2,1,0:T(8,128)(2,1)S(1)}, bf16[8,8,1152]{2,1,0:T(8,128)(2,1)S(1)}, u32[]{:S(2)}, u32[]{:S(2)}) collective-permute-start(bf16[8,8,1152]{2,1,0:T(8,128)(2,1)S(1)} %get-tuple-element.90), channel_id=1, source_target_pairs={{0,4},{2,6},{4,0},{6,2},{8,12},{10,14},{12,8},{14,10},{1,5},{3,7},... | collective-permute-start | bytes 442376 | tf_op jit(solution)/shard_map/ppermute | solution.py:518
  100.4 10.9 %collective-permute-start.9 = (bf16[8,8,1152]{2,1,0:T(8,128)(2,1)S(1)}, bf16[8,8,1152]{2,1,0:T(8,128)(2,1)S(1)}, u32[]{:S(2)}, u32[]{:S(2)}) collective-permute-start(bf16[8,8,1152]{2,1,0:T(8,128)(2,1)S(1)} %get-tuple-element.91), channel_id=1, source_target_pairs={{0,8},{2,10},{4,12},{6,14},{8,0},{10,2},{12,4},{14,6},{1,9},{3,11}... | collective-permute-start | bytes 442376 | tf_op jit(solution)/shard_map/ppermute | solution.py:518
  103.8 7.5 %collective-permute-start.11 = (bf16[2,96,256]{2,1,0:T(8,128)(2,1)S(1)}, bf16[2,96,256]{2,1,0:T(8,128)(2,1)S(1)}, u32[]{:S(2)}, u32[]{:S(2)}) collective-permute-start(bf16[2,96,256]{2,1,0:T(8,128)(2,1)S(1)} %relay.1), channel_id=1, source_target_pairs={{0,32},{32,0},{1,33},{33,1},{2,34},{34,2},{3,35},{35,3},{4,36},{36... | collective-permute-start | bytes 294920 | tf_op jit(solution)/shard_map/ppermute | solution.py:470
  146.9 12.9 %all-to-all-start.4 = ((bf16[4,16,8,1024]{3,2,1,0:T(8,128)(2,1)}), bf16[4,16,8,1024]{3,2,1,0:T(8,128)(2,1)S(1)}, u32[]{:S(2)}, u32[]{:S(2)}) async-start(bf16[4,16,8,1024]{3,2,1,0:T(8,128)(2,1)} %broadcast_in_dim.23), calls=%async_computation.4 | async-start | bytes 2097152 | tf_op jit(solution)/shard_map/all_to_all | solution.py:466
